TPU v7x, 128 devices: a whole 4x4x4 slice. The times are simulated.
128 devices in a mesh: row: 8 (over x, z_hi), col: 16 (over z_lo, y, core).
Axes of the slice: x: 4, y: 4, z: 4 (z_hi: 2, z_lo: 2; z = z_hi * 2 + z_lo), core: 2. Of those that a mesh axis runs over, the one named last changes fastest.
Arguments:
- tokens: bfloat16 [128, 384, 256], P('row', 'col'), may hold values from -6 to 6
- grad_fine: bfloat16 [128, 384, 256], P('row', 'col'), may hold values from -6 to 6
- grad_coarse: bfloat16 [32, 96, 1024], P('row', 'col'), may hold values from -6 to 6
- fine_gain: float32 [256], replicated, may hold values from 0.25 to 1.75
- fine_qkv: bfloat16 [256, 768], replicated, may hold values from -2 to 2
- fine_out: bfloat16 [256, 256], replicated, may hold values from -0.375 to 0.375
- merge_weight: bfloat16 [4096, 1024], replicated, may hold values from -0.09375 to 0.09375
- coarse_gain: float32 [1024], replicated, may hold values from 0.4 to 2.5
- coarse_qkv: bfloat16 [1024, 3072], replicated, may hold values from -1 to 1
- coarse_out: bfloat16 [1024, 1024], replicated, may hold values from -0.1875 to 0.1875
Outputs:
- grad_tokens: bfloat16 [128, 384, 256], P('row', 'col')
- grad_fine_qkv: float32 [256, 768], P('row', 'col')
- grad_fine_out: float32 [256, 256], P('row', 'col')
All inputs are finite; a program needn't handle non-finite values.
Results may differ from a plain program's by a relative error of at most 0.04.
Values may be sent and summed in bfloat16 or wider, within the bound.
No kernel may reach another device: no remote copies, remote signals or barrier semaphores. Data moves between devices by JAX's collectives and lax.ppermute only.
A program may use at most 128 MiB of HBM per device.

v0:
```python
import jax
import jax.numpy as jnp
import numpy as np
from jax import lax
from jax.experimental import pallas as pl
from jax.experimental.pallas import tpu as pltpu
from jax.sharding import PartitionSpec as P

H0 = 4
H1 = 16
HEAD = 64
MERGE = 4
EPSILON = 1e-05
FAR = 1e30
D0 = 256
D1 = 1024

ROWS, COLS = 16, 24
CROWS, CCOLS = 4, 6
R8, C8 = ROWS + 16, COLS + 16
R4, C4 = ROWS + 8, COLS + 8
N4 = R4 * C4
BLOCK = 4 * C4
BLOCKS = R4 // 4
WROWS = R4 + 6
OWN = ROWS * C4
EXT = (CROWS + 2) * (CCOLS + 2)

F32 = jnp.float32
BF16 = jnp.bfloat16


def vmem_params(mib):
    return pltpu.CompilerParams(vmem_limit_bytes=mib * 1024 * 1024)


def whole():
    return pl.BlockSpec(memory_space=pltpu.VMEM)


def far():
    return pl.BlockSpec(memory_space=pltpu.HBM)


def fetch(source, target, sems, pieces):
    rows = source.shape[0] // pieces
    return [
        pltpu.make_async_copy(
            source.at[pl.ds(n * rows, rows)], target.at[pl.ds(n * rows, rows)], sems.at[n]
        )
        for n in range(pieces)
    ]


def dot(a, b, ca, cb):
    return lax.dot_general(a, b, (((ca,), (cb,)), ((), ())), preferred_element_type=F32)


def norm_forward(values):
    center = values - jnp.mean(values, axis=-1, keepdims=True)
    inverse = lax.rsqrt(jnp.mean(center * center, axis=-1, keepdims=True) + EPSILON)
    return center * inverse, inverse


def norm_backward(scaled, normed, inverse):
    return inverse * (
        scaled
        - jnp.mean(scaled, axis=-1, keepdims=True)
        - normed * jnp.mean(scaled * normed, axis=-1, keepdims=True)
    )


def head_lanes(rows):
    return lax.broadcasted_iota(jnp.int32, (rows, D0), 1) // HEAD


def stack_heads(values):
    lanes = head_lanes(values.shape[0])
    zero = jnp.zeros_like(values)
    return jnp.concatenate([jnp.where(lanes == h, values, zero) for h in range(H0)], axis=0)


def unstack_heads(stacked):
    rows = stacked.shape[0] // H0
    lanes = head_lanes(rows)
    result = stacked[:rows]
    for h in range(1, H0):
        result = jnp.where(lanes == h, stacked[h * rows : (h + 1) * rows], result)
    return result


AT_Q = 0
AT_ATT = N4
AT_K = 2 * N4
AT_V = AT_K + WROWS * C4
AT_X = AT_V + WROWS * C4
STASH = AT_X + OWN


def window_bias(key_cols, col_shift, key_row, key_col):
    shape = (10, key_cols, BLOCK)
    kr = lax.broadcasted_iota(jnp.int32, shape, 0)
    kc = lax.broadcasted_iota(jnp.int32, shape, 1)
    lane = lax.broadcasted_iota(jnp.int32, shape, 2)
    row_gap = kr - lane // C4
    col_gap = kc - lane % C4 - col_shift
    rows_ok = (row_gap >= 0) & (row_gap <= 6) & (col_gap >= 0) & (col_gap <= 6)
    grid_row = key_row + kr
    grid_col = key_col + kc
    inside = (grid_row >= 0) & (grid_row < 128) & (grid_col >= 0) & (grid_col < 384)
    return jnp.where(rows_ok & inside, 0.0, -FAR).reshape(10 * key_cols, BLOCK)


def forward_kernel(
    place,
    tokens,
    above,
    below,
    left,
    right,
    gain,
    w_qkv,
    w_out,
    w_merge_far,
    gain_coarse,
    w_coarse_far,
    grads,
    stash_far,
    lse,
    coarse_out,
    packed_far,
    x32,
    q32,
    k32,
    v32,
    hid32,
    stash,
    merged,
    w_merge,
    w_coarse,
    packed,
    merge_sems,
    coarse_sems,
    stash_sem,
    packed_sems,
):
    merge_copies = fetch(w_merge_far, w_merge, merge_sems, 4)
    coarse_copies = fetch(w_coarse_far, w_coarse, coarse_sems, 2)
    for copy in merge_copies + coarse_copies:
        copy.start()
    queries = stash.at[pl.ds(AT_Q, N4)]
    attended = stash.at[pl.ds(AT_ATT, N4)]
    keys_w = stash.at[pl.ds(AT_K, WROWS * C4)]
    values_w = stash.at[pl.ds(AT_V, WROWS * C4)]
    tokens_own = stash.at[pl.ds(AT_X, OWN)]
    row0 = place[0]
    col0 = place[1]
    middle = [above[...].astype(F32), tokens[...].astype(F32), below[...].astype(F32)]
    sides = [left[...].astype(F32), right[...].astype(F32)]
    for i in range(R8):
        part, at = (0, i) if i < 8 else (1, i - 8) if i < 8 + ROWS else (2, i - 8 - ROWS)
        x32[C8 * i : C8 * i + 8] = sides[0][8 * i : 8 * i + 8]
        x32[C8 * i + 8 : C8 * i + 8 + COLS] = middle[part][COLS * at : COLS * (at + 1)]
        x32[C8 * i + 8 + COLS : C8 * (i + 1)] = sides[1][8 * i : 8 * i + 8]
    normed, _ = norm_forward(x32[...])
    normed = (normed * gain[...]).astype(BF16)
    q32[...] = dot(normed, w_qkv[:, :D0], 1, 0).astype(BF16).astype(F32) * (HEAD**-0.5)
    k32[...] = dot(normed, w_qkv[:, D0 : 2 * D0], 1, 0).astype(BF16).astype(F32)
    v32[...] = dot(normed, w_qkv[:, 2 * D0 :], 1, 0).astype(BF16).astype(F32)
    for i in range(R4):
        queries[C4 * i : C4 * (i + 1)] = q32[pl.ds((i + 4) * C8 + 4, C4), :].astype(BF16)
    for i in range(WROWS):
        keys_w[C4 * i : C4 * (i + 1)] = k32[pl.ds((i + 1) * C8 + 4, C4), :].astype(BF16)
        values_w[C4 * i : C4 * (i + 1)] = v32[pl.ds((i + 1) * C8 + 4, C4), :].astype(BF16)
    for i in range(ROWS):
        tokens_own[C4 * i : C4 * (i + 1)] = x32[pl.ds((i + 8) * C8 + 4, C4), :].astype(BF16)
    lse[...] = jnp.full(lse.shape, FAR, F32)
    for b in range(BLOCKS):
        start = (4 * b + 1) * C8
        key_block = k32[start : start + 10 * C8].astype(BF16)
        value_block = v32[start : start + 10 * C8].astype(BF16)
        stacked = stack_heads(queries[BLOCK * b : BLOCK * (b + 1)].astype(F32)).astype(BF16)
        bias = window_bias(C8, 1, row0 - 7 + 4 * b, col0 - 8)
        scores = dot(key_block, stacked, 1, 1) + jnp.concatenate([bias] * H0, axis=1)
        maxima = jnp.max(scores, axis=0, keepdims=True)
        exponent = jnp.exp(scores - maxima)
        totals = jnp.sum(exponent, axis=0, keepdims=True)
        weights = (exponent * (1.0 / totals)).astype(BF16)
        result = unstack_heads(dot(weights, value_block, 0, 0)).astype(BF16)
        attended[BLOCK * b : BLOCK * (b + 1)] = result
        lane = lax.broadcasted_iota(jnp.int32, (1, H0 * BLOCK), 1) % BLOCK
        q_row = row0 - 4 + 4 * b + lane // C4
        q_col = col0 - 4 + lane % C4
        q_in = (q_row >= 0) & (q_row < 128) & (q_col >= 0) & (q_col < 384)
        lse[b : b + 1] = jnp.where(q_in, maxima + jnp.log(totals), FAR)
        projected = dot(result, w_out[...], 1, 0)
        for a in range(4):
            own = x32[pl.ds((4 * b + a + 4) * C8 + 4, C4), :]
            total = own + projected[C4 * a : C4 * (a + 1)]
            at = BLOCK * b + C4 * a
            total = total.astype(BF16).astype(F32)
            hid32[0, at : at + C4] = total[:, :128]
            hid32[1, at : at + C4] = total[:, 128:]
    for pair in range((CROWS + 2) // 2):
        for a in range(MERGE):
            for c in range(MERGE):
                for half in range(2):
                    parts = [
                        hid32[half, pl.ds((4 * i + a) * C4 + c, CCOLS + 2, stride=MERGE), :]
                        for i in (2 * pair, 2 * pair + 1)
                    ]
                    at = (a * MERGE + c) * D0 + half * 128
                    merged[16 * pair : 16 * (pair + 1), at : at + 128] = jnp.concatenate(
                        parts, axis=0
                    ).astype(BF16)
    stash_copy = pltpu.make_async_copy(stash, stash_far, stash_sem)
    stash_copy.start()
    total = None
    for n, copy in enumerate(merge_copies):
        copy.wait()
        part = dot(merged[:, D1 * n : D1 * (n + 1)], w_merge[D1 * n : D1 * (n + 1)], 1, 0)
        total = part if total is None else total + part
    coarse = total.astype(BF16)
    coarse_out[...] = coarse
    normed, _ = norm_forward(coarse.astype(F32))
    normed = normed * gain_coarse[...]
    wide = CCOLS + 2
    parts = [normed[wide * i + 1 : wide * i + 1 + CCOLS] for i in range(1, CROWS + 1)]
    normed = jnp.concatenate(parts, axis=0).astype(BF16)
    for copy in coarse_copies:
        copy.wait()
    packed_copies = []
    for n in range(8):
        result = dot(normed, w_coarse[:, 384 * n : 384 * (n + 1)], 1, 0)
        grad = grads[:, 128 * n : 128 * (n + 1)].astype(F32)
        parts = []
        for h in range(2):
            q = result[:, 192 * h : 192 * h + 64]
            k = result[:, 192 * h + 64 : 192 * h + 128]
            v = result[:, 192 * h + 128 : 192 * h + 192]
            g = grad[:, 64 * h : 64 * h + 64]
            parts.append(jnp.concatenate([k, v, q, g], axis=1))
        packed[n] = jnp.concatenate(parts, axis=0).astype(BF16)
        if n % 4 == 3:
            at = pl.ds(n - 3, 4)
            for r in range(8):
                packed_copies.append(
                    pltpu.make_async_copy(
                        packed.at[at], packed_far.at[r, at], packed_sems.at[n // 4, r]
                    )
                )
                packed_copies[-1].start()
    for copy in packed_copies + [stash_copy]:
        copy.wait()


def run_forward(place, pieces, gain, w_qkv, w_out, w_merge, gain_coarse, w_coarse, grads):
    flat = R8 * C8
    own = CROWS * CCOLS
    shapes = [
        ((STASH, D0), BF16),
        ((8, H0 * BLOCK), F32),
        ((EXT, D1), BF16),
        ((8, 8, 2 * own, 256), BF16),
    ]
    return pl.pallas_call(
        forward_kernel,
        out_shape=[
            pltpu.HBM(s, d) if n in (0, 3) else jax.ShapeDtypeStruct(s, d)
            for n, (s, d) in enumerate(shapes)
        ],
        in_specs=[pl.BlockSpec(memory_space=pltpu.SMEM)]
        + [whole()] * 8
        + [far(), whole(), far(), whole()],
        out_specs=[far(), whole(), whole(), far()],
        scratch_shapes=[pltpu.VMEM((flat, D0), F32)] * 4
        + [
            pltpu.VMEM((2, N4, 128), F32),
            pltpu.VMEM((STASH, D0), BF16),
            pltpu.VMEM((EXT, MERGE * MERGE * D0), BF16),
            pltpu.VMEM(w_merge.shape, BF16),
            pltpu.VMEM(w_coarse.shape, BF16),
            pltpu.VMEM((8, 2 * own, 256), BF16),
            pltpu.SemaphoreType.DMA((4,)),
            pltpu.SemaphoreType.DMA((2,)),
            pltpu.SemaphoreType.DMA(()),
            pltpu.SemaphoreType.DMA((2, 8)),
        ],
        compiler_params=vmem_params(48),
        cost_estimate=pl.CostEstimate(flops=3 * 10**9, bytes_accessed=2 * 10**7, transcendentals=10**6),
        name="forward_kernel",
    )(
        place,
        *[piece.reshape(-1, D0) for piece in pieces],
        gain.reshape(1, D0),
        w_qkv,
        w_out,
        w_merge,
        gain_coarse.reshape(1, D1),
        w_coarse,
        grads,
    )


def lane_half(values, low):
    lanes = lax.broadcasted_iota(jnp.int32, values.shape, 1)
    keep = lanes < HEAD if low else lanes >= HEAD
    return jnp.where(keep, values, jnp.zeros_like(values))


SLAB = 384
SLABS = 8
STRIP = 96
EDGE = SLAB + 2 * STRIP


def strip_pick():
    tile, j = np.divmod(np.arange(STRIP), CCOLS)
    pick = np.zeros((2, STRIP, SLAB), np.float32)
    last = (CROWS - 1) * CCOLS
    pick[0, np.arange(STRIP), tile * CROWS * CCOLS + last + j] = 1
    pick[1, np.arange(STRIP), tile * CROWS * CCOLS + j] = 1
    return pick


def tile_pick():
    c, i, j = np.meshgrid(np.arange(H1), np.arange(6), np.arange(8), indexing="ij")
    tile = (c + (j == 7) - (j == 0)) % H1
    jj = np.where(j == 0, 5, np.where(j == 7, 0, j - 1))
    middle = tile * 24 + (i - 1) * 6 + jj
    source = np.where(i == 0, SLAB + tile * 6 + jj, np.where(i == 5, SLAB + STRIP + tile * 6 + jj, middle))
    pick = np.zeros((H1 * EXT, EDGE), np.float32)
    pick[np.arange(H1 * EXT), source.reshape(-1)] = 1
    return pick


def coarse_forward(place, every, stats, scores_ref):
    keyval = every[:, :128]
    keys = lane_half(keyval.astype(F32) * (HEAD**-0.5), True).astype(BF16)
    own = every[pl.ds(pl.multiple_of(place[2] * SLAB, SLAB), SLAB), 128:]
    logs = []
    sums = []
    for b in range(3):
        part = own[128 * b : 128 * (b + 1)]
        scores_ref[...] = dot(keys, part, 1, 1)
        maxima = jnp.max(scores_ref[...], axis=0, keepdims=True)
        exponent = jnp.exp(scores_ref[...] - maxima)
        totals = jnp.sum(exponent, axis=0, keepdims=True)
        weights = (exponent * (1.0 / totals)).astype(BF16)
        attended = dot(keyval, weights, 0, 0).astype(BF16).astype(F32)
        grads = part.astype(F32).T
        sums.append(jnp.sum(grads[HEAD:] * attended[HEAD:], axis=0, keepdims=True))
        logs.append(maxima + jnp.log(totals))
    result = jnp.concatenate(logs + sums + [jnp.zeros((2, 128), F32)], axis=0)
    for r in range(SLABS):
        stats[r] = result


def run_coarse_forward(place, every):
    return pl.pallas_call(
        coarse_forward,
        out_shape=jax.ShapeDtypeStruct((SLABS, 8, 128), F32),
        in_specs=[pl.BlockSpec(memory_space=pltpu.SMEM), whole()],
        out_specs=whole(),
        scratch_shapes=[pltpu.VMEM((SLAB * SLABS, 128), F32)],
        compiler_params=vmem_params(16),
        cost_estimate=pl.CostEstimate(flops=10**9, bytes_accessed=2 * 10**6, transcendentals=10**6),
        name="coarse_forward",
    )(place, every)


def stat_rows(stats):
    lse = jnp.concatenate([stats[k : k + 1] for k in range(3)], axis=1)
    stat = jnp.concatenate([stats[k : k + 1] for k in range(3, 6)], axis=1)
    return lse, stat


def coarse_backward(place, every, stats, strips, tiles, out, edge, dq_ref, dk_ref, dv_ref):
    row = place[2]
    above = lax.rem(row + SLABS - 1, SLABS)
    below = lax.rem(row + 1, SLABS)

    def slab(index):
        return pl.ds(pl.multiple_of(index * SLAB, SLAB), SLAB)

    edge[:SLAB] = every[slab(row)]
    edge_lse, edge_stat = stat_rows(stats[row])
    for k, other in enumerate((above, below)):
        at = SLAB + STRIP * k
        edge[at : at + STRIP] = dot(strips[k], every[slab(other)], 1, 0).astype(BF16)
        both = jnp.concatenate(stat_rows(stats[other]) + (jnp.zeros((6, SLAB), F32),), axis=0)
        taken = lax.dot_general(
            both,
            strips[k].astype(F32),
            (((1,), (1,)), ((), ())),
            precision=lax.Precision.HIGHEST,
            preferred_element_type=F32,
        )
        edge_lse = jnp.concatenate([edge_lse, taken[0:1]], axis=1)
        edge_stat = jnp.concatenate([edge_stat, taken[1:2]], axis=1)
    edge_kv = edge[:, :128]
    edge_qg = edge[:, 128:]
    edge_k = lane_half(edge_kv.astype(F32) * (HEAD**-0.5), True).astype(BF16)
    edge_v = lane_half(edge_kv.astype(F32), False).astype(BF16)
    for n in range(SLABS):
        rows = slice(n * SLAB, (n + 1) * SLAB)
        keyval = every[rows, :128]
        wide = keyval.astype(F32)
        keys = lane_half(wide * (HEAD**-0.5), True).astype(BF16)
        values = lane_half(wide, False).astype(BF16)
        probs = jnp.exp(dot(keys, edge_qg, 1, 1) - edge_lse)
        slopes = (probs * (dot(values, edge_qg, 1, 1) - edge_stat)).astype(BF16)
        dq = dot(keyval, slopes, 0, 0)
        query = every[rows, 128:]
        lse, stat = stat_rows(stats[n])
        probs = jnp.exp(dot(edge_k, query, 1, 1) - lse)
        slopes = (probs * (dot(edge_v, query, 1, 1) - stat)).astype(BF16)
        dk = dot(slopes, query, 1, 0)
        dv = dot(probs.astype(BF16), query, 1, 0)
        if n == 0:
            dq_ref[...] = dq
            dk_ref[...] = dk
            dv_ref[...] = dv
        else:
            dq_ref[...] += dq
            dk_ref[...] += dk
            dv_ref[...] += dv
    lanes = lax.broadcasted_iota(jnp.int32, (EDGE, 128), 1)
    keyval = jnp.where(lanes < HEAD, dk_ref[...] * (HEAD**-0.5), dv_ref[...]).astype(BF16)
    query = (dq_ref[...].T * (HEAD**-0.5)).astype(BF16)
    out[:, :128] = dot(tiles[...], keyval, 1, 0).astype(BF16)
    out[:, 128:] = dot(tiles[...], query, 1, 0).astype(BF16)


def run_coarse_backward(place, every, stats):
    strips = jnp.asarray(strip_pick(), BF16)
    tiles = jnp.asarray(tile_pick(), BF16)
    return pl.pallas_call(
        coarse_backward,
        out_shape=jax.ShapeDtypeStruct((H1 * EXT, 256), BF16),
        in_specs=[pl.BlockSpec(memory_space=pltpu.SMEM)] + [whole()] * 4,
        out_specs=whole(),
        scratch_shapes=[
            pltpu.VMEM((EDGE, 256), BF16),
            pltpu.VMEM((128, EDGE), F32),
            pltpu.VMEM((EDGE, 128), F32),
            pltpu.VMEM((EDGE, 128), F32),
        ],
        compiler_params=vmem_params(20),
        cost_estimate=pl.CostEstimate(flops=3 * 10**9, bytes_accessed=2 * 10**6, transcendentals=4 * 10**6),
        name="coarse_backward",
    )(place, every, stats, strips, tiles)


def block_pick():
    c, b = np.meshgrid(np.arange(H1), np.arange(64), indexing="ij")
    source = np.where(b < 48, 48 * c + b, 3 * D0 + 16 * c + b - 48).reshape(-1)
    pick = np.zeros((4 * D0, 4 * D0), np.float32)
    pick[source, np.arange(4 * D0)] = 1
    return pick


def backward_kernel(
    place,
    terms_coarse,
    grads,
    grads_left,
    grads_right,
    coarse,
    lse,
    gain_coarse,
    gain,
    w_qkv,
    w_out,
    pick_block,
    w_merge_far,
    w_coarse_far,
    stash_far,
    grad_tokens,
    terms,
    grad_fine,
    sp32,
    gh_ref,
    ga_ref,
    dq_ref,
    dk_ref,
    dv_ref,
    gt_ref,
    stash,
    w_merge,
    w_coarse,
    merge_sems,
    coarse_sems,
    stash_sem,
):
    merge_copies = fetch(w_merge_far, w_merge, merge_sems, 4)
    coarse_copies = fetch(w_coarse_far, w_coarse, coarse_sems, 4)
    stash_copy = pltpu.make_async_copy(stash_far, stash, stash_sem)
    for copy in coarse_copies + merge_copies + [stash_copy]:
        copy.start()
    queries = stash.at[pl.ds(AT_Q, N4)]
    attended = stash.at[pl.ds(AT_ATT, N4)]
    keys_w = stash.at[pl.ds(AT_K, WROWS * C4)]
    values_w = stash.at[pl.ds(AT_V, WROWS * C4)]
    tokens_own = stash.at[pl.ds(AT_X, OWN)]
    row0 = place[0]
    col0 = place[1]
    wide = CCOLS + 2
    grad_coarse = []
    for i in range(CROWS + 2):
        parts = []
        for a in range(4):
            own = grads[4 * i + a].astype(F32)
            left = grads_left[4 * i + a].astype(F32)
            right = grads_right[4 * i + a].astype(F32)
            at = C4 * (4 * i + a)
            grad_fine[at : at + C4] = jnp.concatenate([left[:4], own[:COLS], right[:4]], axis=0)
            parts.append(jnp.concatenate([left[4:], own[COLS:], right[4:]], axis=0))
        grad_coarse.append(jnp.concatenate(parts, axis=1))
    grad_coarse = jnp.concatenate(grad_coarse, axis=0)
    parts = []
    for h in range(H1):
        block = terms_coarse[h].astype(F32)
        parts += [block[:, 128:192], block[:, :128]]
    heads = jnp.concatenate(parts, axis=1).astype(BF16)
    parts = []
    for n, copy in enumerate(coarse_copies):
        copy.wait()
        parts.append(dot(heads, w_coarse[256 * n : 256 * (n + 1)], 1, 1))
    upstream = jnp.concatenate(parts, axis=1) * gain_coarse[...]
    normed, inverse = norm_forward(coarse[...].astype(F32))
    back = norm_backward(upstream, normed, inverse)
    change = (grad_coarse + back).astype(BF16)
    for a, copy in enumerate(merge_copies):
        copy.wait()
        spread = dot(change, w_merge[D1 * a : D1 * (a + 1)], 1, 1)
        for i in range(CROWS + 2):
            for c in range(MERGE):
                for half in range(2):
                    at = c * D0 + half * 128
                    sp32[half, pl.ds((4 * i + a) * C4 + c, wide, stride=MERGE), :] = spread[
                        wide * i : wide * (i + 1), at : at + 128
                    ]
    for half in range(2):
        at = slice(half * 128, (half + 1) * 128)
        gh_ref[:, at] = (grad_fine[:, at] + sp32[half]).astype(BF16)
    ga_ref[...] = dot(gh_ref[...], w_out[...], 1, 1).astype(BF16)
    stash_copy.wait()
    dk_ref[...] = jnp.zeros_like(dk_ref)
    dv_ref[...] = jnp.zeros_like(dv_ref)
    pick = (
        lax.broadcasted_iota(jnp.int32, (8, D0), 1) // HEAD
        == lax.broadcasted_iota(jnp.int32, (8, D0), 0)
    ).astype(F32)
    for b in range(BLOCKS):
        at = slice(BLOCK * b, BLOCK * (b + 1))
        keep = slice(BLOCK * b, BLOCK * b + 10 * C4)
        grad = ga_ref[at].astype(F32)
        product = grad * attended[at].astype(F32)
        sums = lax.dot_general(
            pick,
            product,
            (((1,), (1,)), ((), ())),
            precision=lax.Precision.HIGHEST,
            preferred_element_type=F32,
        )
        stat = jnp.concatenate([sums[h : h + 1] for h in range(H0)], axis=1)
        stack_q = stack_heads(queries[at].astype(F32)).astype(BF16)
        stack_g = stack_heads(grad).astype(BF16)
        key_block = keys_w[keep]
        bias = window_bias(C4, -3, row0 - 7 + 4 * b, col0 - 4)
        scores = dot(key_block, stack_q, 1, 1) + jnp.concatenate([bias] * H0, axis=1)
        probs = jnp.exp(scores - lse[b : b + 1])
        slopes = (probs * (dot(values_w[keep], stack_g, 1, 1) - stat)).astype(BF16)
        dk_ref[keep] += dot(slopes, stack_q, 1, 0)
        dv_ref[keep] += dot(probs.astype(BF16), stack_g, 1, 0)
        if 1 <= b <= 4:
            dq = unstack_heads(dot(slopes, key_block, 0, 0)) * (HEAD**-0.5)
            dq_ref[BLOCK * (b - 1) : BLOCK * b] = dq.astype(BF16)
    own = slice(7 * C4, 7 * C4 + OWN)
    grads = jnp.concatenate(
        [dq_ref[...], dk_ref[own].astype(BF16), dv_ref[own].astype(BF16)], axis=1
    )
    column = lax.broadcasted_iota(jnp.int32, (ROWS, C4, D0), 1).reshape(OWN, D0)
    in_tile = (column >= 4) & (column < 4 + COLS)
    normed, inverse = norm_forward(tokens_own[...].astype(F32))
    rounded = jnp.where(in_tile, normed * gain[...], 0.0).astype(BF16)
    term_qkv = dot(rounded, grads, 0, 0).astype(BF16)
    inner = slice(BLOCK, BLOCK + OWN)
    att = jnp.where(in_tile, attended[inner].astype(F32), 0.0).astype(BF16)
    term_out = dot(att, gh_ref[inner], 0, 0).astype(BF16)
    both = dot(jnp.concatenate([term_qkv, term_out], axis=1), pick_block[...], 1, 0)
    low = lax.broadcasted_iota(jnp.int32, (16, 128), 1) < 64
    for r in range(8):
        for m in range(8):
            first = both[32 * r : 32 * r + 16, 128 * m : 128 * (m + 1)]
            last = both[32 * r + 16 : 32 * (r + 1), 128 * m : 128 * (m + 1)]
            terms[16 * r + 2 * m] = jnp.where(low, first, pltpu.roll(last, 64, 1)).astype(BF16)
            terms[16 * r + 2 * m + 1] = jnp.where(low, pltpu.roll(first, 64, 1), last).astype(BF16)
    upstream = dot(grads, w_qkv[...], 1, 1) * gain[...]
    gt_ref[...] = gh_ref[inner].astype(F32) + norm_backward(upstream, normed, inverse)
    for pair in range(ROWS // 2):
        parts = [gt_ref[pl.ds(i * C4 + 4, COLS), :] for i in (2 * pair, 2 * pair + 1)]
        grad_tokens[2 * COLS * pair : 2 * COLS * (pair + 1)] = jnp.concatenate(
            parts, axis=0
        ).astype(BF16)


def run_backward(place, *operands):
    shapes = [((ROWS * COLS, D0), BF16), ((128, 16, 128), BF16)]
    return pl.pallas_call(
        backward_kernel,
        out_shape=[jax.ShapeDtypeStruct(s, d) for s, d in shapes],
        in_specs=[pl.BlockSpec(memory_space=pltpu.SMEM)] + [whole()] * 11 + [far()] * 3,
        out_specs=[whole()] * 2,
        scratch_shapes=[
            pltpu.VMEM((N4, D0), F32),
            pltpu.VMEM((2, N4, 128), F32),
            pltpu.VMEM((N4, D0), BF16),
            pltpu.VMEM((N4, D0), BF16),
            pltpu.VMEM((OWN, D0), BF16),
            pltpu.VMEM((WROWS * C4, D0), F32),
            pltpu.VMEM((WROWS * C4, D0), F32),
            pltpu.VMEM((OWN, D0), F32),
            pltpu.VMEM((STASH, D0), BF16),
            pltpu.VMEM((MERGE * MERGE * D0, D1), BF16),
            pltpu.VMEM((D1, 3 * D1), BF16),
            pltpu.SemaphoreType.DMA((4,)),
            pltpu.SemaphoreType.DMA((4,)),
            pltpu.SemaphoreType.DMA(()),
        ],
        compiler_params=vmem_params(48),
        cost_estimate=pl.CostEstimate(flops=5 * 10**9, bytes_accessed=2 * 10**7, transcendentals=10**6),
        name="backward_kernel",
    )(place, *operands)


def sum_terms(terms, out_qkv, out_out):
    total = jnp.sum(terms[...].astype(F32), axis=0)
    total = jnp.concatenate([total[:, :64], total[:, 64:]], axis=0)
    out_qkv[...] = total[:, :48]
    out_out[...] = total[:, 48:].T


def run_sum_terms(terms):
    return pl.pallas_call(
        sum_terms,
        out_shape=[jax.ShapeDtypeStruct((32, 48), F32), jax.ShapeDtypeStruct((16, 32), F32)],
        in_specs=[whole()],
        out_specs=[whole()] * 2,
        compiler_params=vmem_params(8),
        name="sum_terms",
    )(terms)


def ring(axis, step):
    devices = lax.axis_size(axis)
    return [(i, (i + step) % devices) for i in range(devices)]


def swap_edges(first, last, axis):
    before = lax.ppermute(last, axis, ring(axis, 1))
    after = lax.ppermute(first, axis, ring(axis, -1))
    return before, after


def token_halo(tokens, width):
    above, below = swap_edges(tokens[:width], tokens[-width:], "row")
    first = jnp.concatenate([above[:, :width], tokens[:, :width], below[:, :width]], axis=0)
    last = jnp.concatenate([above[:, -width:], tokens[:, -width:], below[:, -width:]], axis=0)
    left, right = swap_edges(first, last, "col")
    return tokens, above, below, left, right


def grad_rows(grad_fine, grad_coarse):
    folded = grad_coarse.reshape(CROWS, CCOLS, 4, D0).transpose(0, 2, 1, 3)
    both = jnp.concatenate([grad_fine, folded.reshape(ROWS, CCOLS, D0)], axis=1)
    above, below = swap_edges(both[:4], both[-4:], "row")
    return jnp.concatenate([above, both, below], axis=0)


def grad_sides(both):
    first = jnp.concatenate([both[:, :4], both[:, COLS : COLS + 1]], axis=1)
    last = jnp.concatenate([both[:, COLS - 4 : COLS], both[:, -1:]], axis=1)
    return first, last


def on_device(
    tokens,
    grad_fine,
    grad_coarse,
    fine_gain,
    fine_qkv,
    fine_out,
    merge_weight,
    coarse_gain,
    coarse_qkv,
    coarse_out,
):
    row = lax.axis_index("row")
    col = lax.axis_index("col")
    place = jnp.stack([row * ROWS, col * COLS, row]).astype(jnp.int32)
    pieces = token_halo(tokens, 8)
    grad_heads = jnp.dot(
        grad_coarse.reshape(-1, D1), coarse_out.T, preferred_element_type=F32
    ).astype(BF16)
    stash, lse, coarse, packed = run_forward(
        place,
        pieces,
        fine_gain,
        fine_qkv,
        fine_out,
        merge_weight,
        coarse_gain,
        coarse_qkv,
        grad_heads,
    )
    every = lax.all_to_all(
        packed.reshape(8 * H1, CROWS * CCOLS, 256),
        ("row", "col"),
        split_axis=0,
        concat_axis=0,
        tiled=True,
    )
    coarse, grad_fine, grad_coarse = lax.optimization_barrier((coarse, grad_fine, grad_coarse))
    both = grad_rows(grad_fine, grad_coarse)
    every, both = lax.optimization_barrier((every, both))
    every = every.reshape(SLAB * SLABS, 256)
    stats = run_coarse_forward(place, every)
    stats, both = lax.optimization_barrier((stats, both))
    stats = lax.all_to_all(stats, "row", split_axis=0, concat_axis=0, tiled=True)
    left, right = swap_edges(*grad_sides(both), "col")
    stats, left, right = lax.optimization_barrier((stats, left, right))
    tiles = run_coarse_backward(place, every, stats).reshape(H1, EXT, 256)
    terms = lax.all_to_all(tiles, "col", split_axis=0, concat_axis=0, tiled=True)
    grad_tokens, blocks = run_backward(
        place,
        terms,
        both,
        left,
        right,
        coarse,
        lse,
        coarse_gain.reshape(1, D1),
        fine_gain.reshape(1, D0),
        fine_qkv,
        fine_out,
        jnp.asarray(block_pick(), BF16),
        merge_weight,
        coarse_qkv,
        stash,
    )
    blocks = lax.all_to_all(blocks, ("row", "col"), split_axis=0, concat_axis=0, tiled=True)
    grad_qkv, grad_out = run_sum_terms(blocks)
    return grad_tokens.reshape(ROWS, COLS, D0), grad_qkv, grad_out.T


def solution(mesh):
    return jax.shard_map(
        on_device,
        mesh=mesh,
        in_specs=(P("row", "col", None),) * 3 + (P(),) * 7,
        out_specs=(P("row", "col", None), P("row", "col"), P("row", "col")),
        check_vma=False,
    )
```

profile of v0, /device:TPU:1, one launch (start us, length us, event | category | flops | bytes accessed | tf_op | source)
XLA Modules:
  0.0 147.3 jit_solution(16743031853725909076)
XLA Ops:
  0.6 0.0 copy-start
  0.6 0.0 copy-start.3
  0.7 0.0 copy-start.4
  0.7 0.0 copy-start.2
  0.7 0.0 copy-start.5
  0.7 0.0 copy-start.6
  0.7 1.1 fusion.4
  1.8 6.7 %collective-permute-start.1 = (bf16[8,24,256]{2,1,0:T(8,128)(2,1)S(1)}, bf16[8,24,256]{2,1,0:T(8,128)(2,1)S(1)}, u32[]{:S(2)}, u32[]{:S(2)}) collective-permute-start(bf16[8,24,256]{2,1,0:T(8,128)(2,1)S(1)} %get-tuple-element.47), channel_id=1, source_target_pairs={{0,112},{16,0},{32,16},{48,32},{64,48},{80,64},{96,80},{112,96},{1... | collective-permute-start | bytes 294920 | tf_op jit(solution)/shard_map/ppermute | solution.py:663
  8.5 0.0 collective-permute-start
  8.5 0.9 fusion.3
  9.4 0.8 copy.17
  10.2 0.0 collective-permute-done.1
  10.3 5.3 %collective-permute-done = bf16[8,24,256]{2,1,0:T(8,128)(2,1)S(1)} collective-permute-done((bf16[8,24,256]{2,1,0:T(8,128)(2,1)S(1)}, bf16[8,24,256]{2,1,0:T(8,128)(2,1)S(1)}, u32[]{:S(2)}, u32[]{:S(2)}) %collective-permute-start) | collective-permute-done | bytes 98336 | tf_op jit(solution)/shard_map/ppermute | solution.py:662
  15.6 0.7 pad_maximum_fusion.1
  16.3 3.3 %collective-permute-start.2 = (bf16[32,8,256]{2,1,0:T(8,128)(2,1)}, bf16[32,8,256]{2,1,0:T(8,128)(2,1)S(1)}, u32[]{:S(2)}, u32[]{:S(2)}) collective-permute-start(bf16[32,8,256]{2,1,0:T(8,128)(2,1)} %pad_maximum_fusion.1), channel_id=1, source_target_pairs={{0,1},{1,2},{2,3},{3,4},{4,5},{5,6},{6,7},{7,8},{8,9},{9,10},{10,1... | collective-permute-start | bytes 393224 | tf_op jit(solution)/shard_map/ppermute | solution.py:662
  19.5 0.7 pad_maximum_fusion.2
  20.2 0.0 collective-permute-start.3
  20.2 0.0 copy-done
  20.2 0.7 convolution_convert_fusion.grads
  20.9 0.1 pad_add_fusion.place
  21.0 0.8 collective-permute-done.2
  21.8 3.0 %collective-permute-done.3 = bf16[32,8,256]{2,1,0:T(8,128)(2,1)S(1)} collective-permute-done((bf16[32,8,256]{2,1,0:T(8,128)(2,1)}, bf16[32,8,256]{2,1,0:T(8,128)(2,1)S(1)}, u32[]{:S(2)}, u32[]{:S(2)}) %collective-permute-start.3) | collective-permute-done | bytes 131104 | tf_op jit(solution)/shard_map/ppermute | solution.py:663
  24.8 0.0 copy-done.4
  24.8 14.0 %forward_kernel.1 = (bf16[3968,256]{1,0:T(8,128)(2,1)}, f32[8,512]{1,0:T(8,128)S(1)}, bf16[48,1024]{1,0:T(8,128)(2,1)S(1)}, bf16[8,8,48,256]{3,2,1,0:T(8,128)(2,1)}) custom-call(s32[3]{0:T(128)S(1)} %pad_add_fusion.place, bf16[384,256]{1,0:T(8,128)(2,1)S(1)} %bitcast.17, bf16[192,256]{1,0:T(8,128)(2,1)S(1)} %bitcast.20, bf16[192,256]{1,0:T(8,128)(2,1)S(1)} %bitcast.19, ...), custom_call_target="tpu_custom_call" | custom-call | flops 3000000000 | bytes 20000000 | tf_op jit(solution)/shard_map/forward_kernel/pallas_call | solution.py:266
  38.9 0.0 copy-start.9
  38.9 0.0 copy-start.10
  38.9 6.2 %all-to-all-start = ((bf16[128,24,256]{2,1,0:T(8,128)(2,1)}), bf16[128,24,256]{2,1,0:T(8,128)(2,1)}, u32[]{:S(2)}, u32[]{:S(2)}) async-start(bf16[128,24,256]{2,1,0:T(8,128)(2,1)} %bitcast.27), calls=%async_computation | async-start | bytes 3145728 | tf_op jit(solution)/shard_map/all_to_all | solution.py:718
  45.3 0.0 copy-done.10
  45.3 3.3 %collective-permute-start.4 = (bf16[4,30,256]{2,1,0:T(8,128)(2,1)S(1)}, bf16[4,30,256]{2,1,0:T(8,128)(2,1)S(1)}, u32[]{:S(2)}, u32[]{:S(2)}) collective-permute-start(bf16[4,30,256]{2,1,0:T(8,128)(2,1)S(1)} %get-tuple-element.43), channel_id=1, source_target_pairs={{0,16},{16,32},{32,48},{48,64},{64,80},{80,96},{96,112},{112,0},{1... | collective-permute-start | bytes 184328 | tf_op jit(solution)/shard_map/ppermute | solution.py:662
  48.7 2.4 %collective-permute-start.5 = (bf16[4,30,256]{2,1,0:T(8,128)(2,1)S(1)}, bf16[4,30,256]{2,1,0:T(8,128)(2,1)S(1)}, u32[]{:S(2)}, u32[]{:S(2)}) collective-permute-start(bf16[4,30,256]{2,1,0:T(8,128)(2,1)S(1)} %get-tuple-element.44), channel_id=1, source_target_pairs={{0,112},{16,0},{32,16},{48,32},{64,48},{80,64},{96,80},{112,96},{1... | collective-permute-start | bytes 184328 | tf_op jit(solution)/shard_map/ppermute | solution.py:663
  51.1 17.9 %collective-permute-done.4 = bf16[4,30,256]{2,1,0:T(8,128)(2,1)S(1)} collective-permute-done((bf16[4,30,256]{2,1,0:T(8,128)(2,1)S(1)}, bf16[4,30,256]{2,1,0:T(8,128)(2,1)S(1)}, u32[]{:S(2)}, u32[]{:S(2)}) %collective-permute-start.4) | collective-permute-done | bytes 61472 | tf_op jit(solution)/shard_map/ppermute | solution.py:662
  69.1 0.0 collective-permute-done.5
  69.1 0.1 pad_maximum_fusion.grads
  69.1 0.7 all-to-all-done
  69.8 5.0 %coarse_forward.1 = f32[8,8,128]{2,1,0:T(8,128)S(1)} custom-call(s32[3]{0:T(128)S(1)} %pad_add_fusion.place, bf16[3072,256]{1,0:T(8,128)(2,1)} %bitcast.11.every), custom_call_target="tpu_custom_call" | custom-call | flops 1000000000 | bytes 2000000 | tf_op jit(solution)/shard_map/coarse_forward/pallas_call | solution.py:360
  75.0 0.1 pad_maximum_fusion.3
  75.0 1.7 %collective-permute-start.6 = (bf16[24,5,256]{2,1,0:T(8,128)(2,1)S(1)}, bf16[24,5,256]{2,1,0:T(8,128)(2,1)S(1)}, u32[]{:S(2)}, u32[]{:S(2)}) collective-permute-start(bf16[24,5,256]{2,1,0:T(8,128)(2,1)S(1)} %pad_maximum_fusion.3), channel_id=1, source_target_pairs={{0,1},{1,2},{2,3},{3,4},{4,5},{5,6},{6,7},{7,8},{8,9},{9,10},{10,1... | collective-permute-start | bytes 184328 | tf_op jit(solution)/shard_map/ppermute | solution.py:662
  76.8 0.1 pad_maximum_fusion.4
  76.8 0.1 collective-permute-start.7
  76.9 9.1 %all_to_all.20.stats = f32[8,8,128]{2,1,0:T(8,128)S(1)} all-to-all(f32[8,8,128]{2,1,0:T(8,128)S(1)} %coarse_forward.1), channel_id=1, replica_groups=mesh['row'=8,'col'=16] {'row'}, dimensions={0} | all-to-all | bytes 65536 | tf_op jit(solution)/shard_map/all_to_all | solution.py:731
  86.0 0.0 collective-permute-done.6.grads_left
  86.0 0.0 collective-permute-done.7.grads_right
  86.0 0.0 copy-done.7
  86.0 10.2 %coarse_backward.1 = bf16[768,256]{1,0:T(8,128)(2,1)S(1)} custom-call(s32[3]{0:T(128)S(1)} %pad_add_fusion.place, bf16[3072,256]{1,0:T(8,128)(2,1)} %bitcast.11.every, f32[8,8,128]{2,1,0:T(8,128)S(1)} %all_to_all.20.stats, bf16[2,96,384]{2,1,0:T(8,128)(2,1)S(1)} %copy-done.8, bf16[768,576]{1,0:T(8,128)(2,1)S(1)} %copy-done.7), custom_call_target="tpu_custom_call" | custom-call | flops 3000000000 | bytes 2000000 | tf_op jit(solution)/shard_map/coarse_backward/pallas_call | solution.py:438
  96.3 16.0 %all_to_all.21.terms_coarse = bf16[16,48,256]{2,1,0:T(8,128)(2,1)S(1)} all-to-all(bf16[16,48,256]{2,1,0:T(8,128)(2,1)S(1)} %bitcast.18), channel_id=1, replica_groups=mesh['row'=8,'col'=16] {'col'}, dimensions={0} | all-to-all | bytes 786432 | tf_op jit(solution)/shard_map/all_to_all | solution.py:735
  112.3 16.6 %backward_kernel.1 = (bf16[384,256]{1,0:T(8,128)(2,1)}, bf16[128,16,128]{2,1,0:T(8,128)(2,1)S(1)}) custom-call(s32[3]{0:T(128)S(1)} %pad_add_fusion.place, bf16[16,48,256]{2,1,0:T(8,128)(2,1)S(1)} %all_to_all.21.terms_coarse, bf16[24,30,256]{2,1,0:T(8,128)(2,1)S(1)} %pad_maximum_fusion.grads, bf16[24,5,256]{2,1,0:T(8,128)(2,1)S(1)} %collective-permute-done.6.grads_left, ...), custom_call_target="tpu_custom_call" | custom-call | flops 5000000000 | bytes 20000000 | tf_op jit(solution)/shard_map/backward_kernel/pallas_call | solution.py:611
  128.9 17.5 %all_to_all.22.terms = bf16[128,16,128]{2,1,0:T(8,128)(2,1)S(1)} all-to-all(bf16[128,16,128]{2,1,0:T(8,128)(2,1)S(1)} %get-tuple-element.36), channel_id=1, replica_groups=mesh['row'=8,'col'=16] {'row','col'}, dimensions={0} | all-to-all | bytes 1048576 | tf_op jit(solution)/shard_map/all_to_all | solution.py:753
  146.3 1.0 sum_terms.1
  (22 shorter events, 0.3 us)
Async XLA Ops:
  0.6 19.6 %copy-start = (bf16[1024,1024]{1,0:T(8,128)(2,1)S(1)}, bf16[1024,1024]{1,0:T(8,128)(2,1)}, u32[]{:S(2)}) copy-start(bf16[1024,1024]{1,0:T(8,128)(2,1)} %param.22) | copy-start | bytes 6291460
  0.6 24.2 %copy-start.3 = (bf16[16,24,256]{2,1,0:T(8,128)(2,1)S(1)}, bf16[16,24,256]{2,1,0:T(8,128)(2,1)}, u32[]{:S(2)}) copy-start(bf16[16,24,256]{2,1,0:T(8,128)(2,1)} %param.13) | copy-start | bytes 589828
  0.7 24.2 %copy-start.4 = (bf16[256,256]{1,0:T(8,128)(2,1)S(1)}, bf16[256,256]{1,0:T(8,128)(2,1)}, u32[]{:S(2)}) copy-start(bf16[256,256]{1,0:T(8,128)(2,1)} %w_out.3) | copy-start | bytes 393220
  0.7 24.2 %copy-start.2 = (bf16[256,768]{1,0:T(8,128)(2,1)S(1)}, bf16[256,768]{1,0:T(8,128)(2,1)}, u32[]{:S(2)}) copy-start(bf16[256,768]{1,0:T(8,128)(2,1)} %w_qkv.3) | copy-start | bytes 1179652
  0.7 24.2 %copy-start.5 = (f32[1024]{0:T(1024)S(1)}, f32[1024]{0:T(1024)}, u32[]{:S(2)}) copy-start(f32[1024]{0:T(1024)} %param.20) | copy-start | bytes 12292
  0.7 24.2 %copy-start.6 = (f32[256]{0:T(256)S(1)}, f32[256]{0:T(256)}, u32[]{:S(2)}) copy-start(f32[256]{0:T(256)} %param.16) | copy-start | bytes 3076
  1.8 8.4 %collective-permute-start.1 = (bf16[8,24,256]{2,1,0:T(8,128)(2,1)S(1)}, bf16[8,24,256]{2,1,0:T(8,128)(2,1)S(1)}, u32[]{:S(2)}, u32[]{:S(2)}) collective-permute-start(bf16[8,24,256]{2,1,0:T(8,128)(2,1)S(1)} %get-tuple-element.47), channel_id=1, source_target_pairs={{0,112},{16,0},{32,16},{48,32},{64,48},{80,64},{96,80},{112,96},{1... | collective-permute-start | bytes 294920 | tf_op jit(solution)/shard_map/ppermute | solution.py:663
  8.5 7.1 %collective-permute-start = (bf16[8,24,256]{2,1,0:T(8,128)(2,1)S(1)}, bf16[8,24,256]{2,1,0:T(8,128)(2,1)S(1)}, u32[]{:S(2)}, u32[]{:S(2)}) collective-permute-start(bf16[8,24,256]{2,1,0:T(8,128)(2,1)S(1)} %get-tuple-element.48), channel_id=1, source_target_pairs={{0,16},{16,32},{32,48},{48,64},{64,80},{80,96},{96,112},{112,0},{1... | collective-permute-start | bytes 294920 | tf_op jit(solution)/shard_map/ppermute | solution.py:662
  16.3 5.6 %collective-permute-start.2 = (bf16[32,8,256]{2,1,0:T(8,128)(2,1)}, bf16[32,8,256]{2,1,0:T(8,128)(2,1)S(1)}, u32[]{:S(2)}, u32[]{:S(2)}) collective-permute-start(bf16[32,8,256]{2,1,0:T(8,128)(2,1)} %pad_maximum_fusion.1), channel_id=1, source_target_pairs={{0,1},{1,2},{2,3},{3,4},{4,5},{5,6},{6,7},{7,8},{8,9},{9,10},{10,1... | collective-permute-start | bytes 393224 | tf_op jit(solution)/shard_map/ppermute | solution.py:662
  20.2 4.6 %collective-permute-start.3 = (bf16[32,8,256]{2,1,0:T(8,128)(2,1)}, bf16[32,8,256]{2,1,0:T(8,128)(2,1)S(1)}, u32[]{:S(2)}, u32[]{:S(2)}) collective-permute-start(bf16[32,8,256]{2,1,0:T(8,128)(2,1)} %pad_maximum_fusion.2), channel_id=1, source_target_pairs={{0,15},{1,0},{2,1},{3,2},{4,3},{5,4},{6,5},{7,6},{8,7},{9,8},{10,9... | collective-permute-start | bytes 393224 | tf_op jit(solution)/shard_map/ppermute | solution.py:663
  38.9 6.2 %copy-start.9 = (bf16[4,6,1024]{2,0,1:T(4,128)(2,1)S(1)}, bf16[4,6,1024]{2,0,1:T(4,128)(2,1)}, u32[]{:S(2)}) copy-start(bf16[4,6,1024]{2,0,1:T(4,128)(2,1)} %param.15) | copy-start | bytes 147460
  38.9 6.4 %copy-start.10 = (bf16[16,24,256]{2,1,0:T(8,128)(2,1)S(1)}, bf16[16,24,256]{2,1,0:T(8,128)(2,1)}, u32[]{:S(2)}) copy-start(bf16[16,24,256]{2,1,0:T(8,128)(2,1)} %param.14) | copy-start | bytes 589828
  38.9 30.9 %all-to-all-start = ((bf16[128,24,256]{2,1,0:T(8,128)(2,1)}), bf16[128,24,256]{2,1,0:T(8,128)(2,1)}, u32[]{:S(2)}, u32[]{:S(2)}) async-start(bf16[128,24,256]{2,1,0:T(8,128)(2,1)} %bitcast.27), calls=%async_computation | async-start | bytes 3145728 | tf_op jit(solution)/shard_map/all_to_all | solution.py:718
  45.3 23.7 %collective-permute-start.4 = (bf16[4,30,256]{2,1,0:T(8,128)(2,1)S(1)}, bf16[4,30,256]{2,1,0:T(8,128)(2,1)S(1)}, u32[]{:S(2)}, u32[]{:S(2)}) collective-permute-start(bf16[4,30,256]{2,1,0:T(8,128)(2,1)S(1)} %get-tuple-element.43), channel_id=1, source_target_pairs={{0,16},{16,32},{32,48},{48,64},{64,80},{80,96},{96,112},{112,0},{1... | collective-permute-start | bytes 184328 | tf_op jit(solution)/shard_map/ppermute | solution.py:662
  48.7 20.4 %collective-permute-start.5 = (bf16[4,30,256]{2,1,0:T(8,128)(2,1)S(1)}, bf16[4,30,256]{2,1,0:T(8,128)(2,1)S(1)}, u32[]{:S(2)}, u32[]{:S(2)}) collective-permute-start(bf16[4,30,256]{2,1,0:T(8,128)(2,1)S(1)} %get-tuple-element.44), channel_id=1, source_target_pairs={{0,112},{16,0},{32,16},{48,32},{64,48},{80,64},{96,80},{112,96},{1... | collective-permute-start | bytes 184328 | tf_op jit(solution)/shard_map/ppermute | solution.py:663
  69.8 16.2 %copy-start.7 = (bf16[768,576]{1,0:T(8,128)(2,1)S(1)}, bf16[768,576]{1,0:T(8,128)(2,1)}, u32[]{:S(2)}) copy-start(bf16[768,576]{1,0:T(8,128)(2,1)} %constant.20.clone.tiles) | copy-start | bytes 2654212
  69.8 16.2 %copy-start.8 = (bf16[2,96,384]{2,1,0:T(8,128)(2,1)S(1)}, bf16[2,96,384]{2,1,0:T(8,128)(2,1)}, u32[]{:S(2)}) copy-start(bf16[2,96,384]{2,1,0:T(8,128)(2,1)} %constant.19.clone.strips) | copy-start | bytes 442372
  75.0 11.0 %collective-permute-start.6 = (bf16[24,5,256]{2,1,0:T(8,128)(2,1)S(1)}, bf16[24,5,256]{2,1,0:T(8,128)(2,1)S(1)}, u32[]{:S(2)}, u32[]{:S(2)}) collective-permute-start(bf16[24,5,256]{2,1,0:T(8,128)(2,1)S(1)} %pad_maximum_fusion.3), channel_id=1, source_target_pairs={{0,1},{1,2},{2,3},{3,4},{4,5},{5,6},{6,7},{7,8},{8,9},{9,10},{10,1... | collective-permute-start | bytes 184328 | tf_op jit(solution)/shard_map/ppermute | solution.py:662
  76.8 9.2 %collective-permute-start.7 = (bf16[24,5,256]{2,1,0:T(8,128)(2,1)S(1)}, bf16[24,5,256]{2,1,0:T(8,128)(2,1)S(1)}, u32[]{:S(2)}, u32[]{:S(2)}) collective-permute-start(bf16[24,5,256]{2,1,0:T(8,128)(2,1)S(1)} %pad_maximum_fusion.4), channel_id=1, source_target_pairs={{0,15},{1,0},{2,1},{3,2},{4,3},{5,4},{6,5},{7,6},{8,7},{9,8},{10,9... | collective-permute-start | bytes 184328 | tf_op jit(solution)/shard_map/ppermute | solution.py:663
  86.0 26.3 %copy-start.1 = (bf16[3968,256]{1,0:T(8,128)(2,1)S(1)}, bf16[3968,256]{1,0:T(8,128)(2,1)}, u32[]{:S(2)}) copy-start(bf16[3968,256]{1,0:T(8,128)(2,1)} %get-tuple-element.34.stash_far) | copy-start | bytes 6094852
where the time goes:
time: 148 us; the launch traced here: 147 us
  Pallas kernels  46.8 us (32%)
  blocking collectives  42.6 us (29%)
  waiting for transfers between devices  27.8 us (19%)
  starting transfers between devices  23.8 us (16%)
  local copies, waits for them, and re-layouts  3.06 us (2%)
  other arithmetic  1.63 us (1%)
    ppermute x4, waiting for transfers between devices, swap_edges(): before = lax.ppermute(last, axis, ring(axis, 1))  24.1 us
    all_to_all x1, blocking collectives, on_device(): lax.all_to_all(blocks, ('row', 'col'), split_axis=0, concat_axis=0, tiled...  17.5 us
    pallas_call x1, Pallas kernels, run_backward(): pl.pallas_call(backward_kernel, out_shape=[jax.ShapeDtypeStruct(s, d) for...  16.6 us
    all_to_all x1, blocking collectives, on_device(): lax.all_to_all(tiles, 'col', split_axis=0, concat_axis=0, tiled=True)  16 us
    pallas_call x1, Pallas kernels, run_forward(): pl.pallas_call(forward_kernel, out_shape=[pltpu.HBM(s, d) if n in (0, 3)...  14 us
    pallas_call x1, Pallas kernels, run_coarse_backward(): pl.pallas_call(coarse_backward, out_shape=jax.ShapeDtypeStruct((H1 * EXT,...  10.2 us
    ppermute x4, starting transfers between devices, swap_edges(): after = lax.ppermute(first, axis, ring(axis, -1))  9.19 us
    all_to_all x1, blocking collectives, on_device(): lax.all_to_all(stats, 'row', split_axis=0, concat_axis=0, tiled=True)  9.1 us
  transfers between devices with their start and end apart: 9, of which 5 were waited for; matrix products, arithmetic and copies ran while one was open for 2% of the time, Pallas kernels for 0%

commit v1 on v0

v1 whole, which is shorter than its diff:
```python
import jax
import jax.numpy as jnp
import numpy as np
from jax import lax
from jax.experimental import pallas as pl
from jax.experimental.pallas import tpu as pltpu
from jax.sharding import PartitionSpec as P

H0 = 4
H1 = 16
HEAD = 64
MERGE = 4
EPSILON = 1e-05
FAR = 1e30
D0 = 256
D1 = 1024

ROWS, COLS = 16, 24
CROWS, CCOLS = 4, 6
R8, C8 = ROWS + 16, COLS + 16
R4, C4 = ROWS + 8, COLS + 8
N4 = R4 * C4
BLOCK = 4 * C4
BLOCKS = R4 // 4
WROWS = R4 + 6
OWN = ROWS * C4
EXT = (CROWS + 2) * (CCOLS + 2)

F32 = jnp.float32
BF16 = jnp.bfloat16


def vmem_params(mib):
    return pltpu.CompilerParams(vmem_limit_bytes=mib * 1024 * 1024)


def whole():
    return pl.BlockSpec(memory_space=pltpu.VMEM)


def far():
    return pl.BlockSpec(memory_space=pltpu.HBM)


def fetch(source, target, sems, pieces):
    rows = source.shape[0] // pieces
    return [
        pltpu.make_async_copy(
            source.at[pl.ds(n * rows, rows)], target.at[pl.ds(n * rows, rows)], sems.at[n]
        )
        for n in range(pieces)
    ]


def dot(a, b, ca, cb):
    return lax.dot_general(a, b, (((ca,), (cb,)), ((), ())), preferred_element_type=F32)


def norm_forward(values):
    center = values - jnp.mean(values, axis=-1, keepdims=True)
    inverse = lax.rsqrt(jnp.mean(center * center, axis=-1, keepdims=True) + EPSILON)
    return center * inverse, inverse


def norm_backward(scaled, normed, inverse):
    return inverse * (
        scaled
        - jnp.mean(scaled, axis=-1, keepdims=True)
        - normed * jnp.mean(scaled * normed, axis=-1, keepdims=True)
    )


def head_lanes(rows):
    return lax.broadcasted_iota(jnp.int32, (rows, D0), 1) // HEAD


def stack_heads(values):
    lanes = head_lanes(values.shape[0])
    zero = jnp.zeros_like(values)
    return jnp.concatenate([jnp.where(lanes == h, values, zero) for h in range(H0)], axis=0)


def unstack_heads(stacked):
    rows = stacked.shape[0] // H0
    lanes = head_lanes(rows)
    result = stacked[:rows]
    for h in range(1, H0):
        result = jnp.where(lanes == h, stacked[h * rows : (h + 1) * rows], result)
    return result


AT_Q = 0
AT_ATT = N4
AT_K = 2 * N4
AT_V = AT_K + WROWS * C4
AT_X = AT_V + WROWS * C4
STASH = AT_X + OWN


def window_bias(key_cols, col_shift):
    shape = (10, key_cols, BLOCK)
    kr = lax.broadcasted_iota(jnp.int32, shape, 0)
    kc = lax.broadcasted_iota(jnp.int32, shape, 1)
    lane = lax.broadcasted_iota(jnp.int32, shape, 2)
    row_gap = kr - lane // C4
    col_gap = kc - lane % C4 - col_shift
    near = (row_gap >= 0) & (row_gap <= 6) & (col_gap >= 0) & (col_gap <= 6)
    return jnp.where(near, 0.0, -FAR).reshape(10 * key_cols, BLOCK)


def key_bias(key_cols, key_row, key_col):
    shape = (10, key_cols, 1)
    grid_row = key_row + lax.broadcasted_iota(jnp.int32, shape, 0)
    grid_col = key_col + lax.broadcasted_iota(jnp.int32, shape, 1)
    inside = (grid_row >= 0) & (grid_row < 128) & (grid_col >= 0) & (grid_col < 384)
    return jnp.where(inside, 0.0, -FAR).reshape(10 * key_cols, 1)


def all_heads(bias):
    return jnp.concatenate([bias] * H0, axis=1)


def near_kernel(
    place,
    tokens,
    above,
    below,
    left,
    right,
    gain,
    w_qkv,
    w_out,
    w_merge_far,
    gain_coarse,
    w_coarse_far,
    grads,
    packed_far,
    x32,
    keys,
    values,
    hid32,
    merged,
    w_merge,
    w_coarse,
    packed,
    merge_sems,
    coarse_sems,
    packed_sems,
):
    merge_copies = fetch(w_merge_far, w_merge, merge_sems, 4)
    coarse_copies = fetch(w_coarse_far, w_coarse, coarse_sems, 2)
    for copy in merge_copies + coarse_copies:
        copy.start()
    row0 = place[0]
    col0 = place[1]
    middle = [part[: 8 * COLS].astype(F32) for part in (above, below)]
    middle.insert(1, tokens[...].astype(F32))
    sides = [left[...].astype(F32), right[...].astype(F32)]
    for t in range(ROWS + 6):
        e = t + 5
        part, at = (0, e) if e < 8 else (1, e - 8) if e < 8 + ROWS else (2, e - 8 - ROWS)
        x32[C4 * t : C4 * (t + 1)] = jnp.concatenate(
            [
                sides[0][8 * e + 4 : 8 * e + 8],
                middle[part][COLS * at : COLS * (at + 1)],
                sides[1][8 * e : 8 * e + 4],
            ],
            axis=0,
        )
    normed, _ = norm_forward(x32[...])
    normed = (normed * gain[...]).astype(BF16)
    inner = slice(3 * C4, 3 * C4 + OWN)
    queries = dot(normed[inner], w_qkv[:, :D0], 1, 0).astype(BF16).astype(F32) * (HEAD**-0.5)
    keys[...] = dot(normed, w_qkv[:, D0 : 2 * D0], 1, 0).astype(BF16)
    values[...] = dot(normed, w_qkv[:, 2 * D0 :], 1, 0).astype(BF16)
    window = window_bias(C4, -3)
    for b in range(ROWS // 4):
        block = slice(BLOCK * b, BLOCK * b + 10 * C4)
        stacked = stack_heads(queries[BLOCK * b : BLOCK * (b + 1)]).astype(BF16)
        bias = all_heads(window + key_bias(C4, row0 - 3 + 4 * b, col0 - 4))
        scores = dot(keys[block], stacked, 1, 1) + bias
        maxima = jnp.max(scores, axis=0, keepdims=True)
        exponent = jnp.exp(scores - maxima)
        totals = jnp.sum(exponent, axis=0, keepdims=True)
        weights = (exponent * (1.0 / totals)).astype(BF16)
        attended = unstack_heads(dot(weights, values[block], 0, 0)).astype(BF16)
        at = BLOCK * b
        own = x32[3 * C4 + at : 3 * C4 + at + BLOCK]
        total = (own + dot(attended, w_out[...], 1, 0)).astype(BF16).astype(F32)
        hid32[0, at : at + BLOCK] = total[:, :128]
        hid32[1, at : at + BLOCK] = total[:, 128:]
    wide = CCOLS + 2
    merge_rows(hid32, merged, CROWS)
    total = None
    for n, copy in enumerate(merge_copies):
        copy.wait()
        part = dot(merged[:, D1 * n : D1 * (n + 1)], w_merge[D1 * n : D1 * (n + 1)], 1, 0)
        total = part if total is None else total + part
    normed, _ = norm_forward(total.astype(BF16).astype(F32))
    normed = normed * gain_coarse[...]
    parts = [normed[wide * i + 1 : wide * i + 1 + CCOLS] for i in range(CROWS)]
    normed = jnp.concatenate(parts, axis=0).astype(BF16)
    for copy in coarse_copies:
        copy.wait()
    packed_copies = []
    for n in range(4):
        result = dot(normed, w_coarse[:, 768 * n : 768 * (n + 1)], 1, 0)
        grad = grads[:, 256 * n : 256 * (n + 1)].astype(F32)
        parts = []
        for h in range(4):
            q = result[:, 192 * h : 192 * h + 64]
            k = result[:, 192 * h + 64 : 192 * h + 128]
            v = result[:, 192 * h + 128 : 192 * h + 192]
            g = grad[:, 64 * h : 64 * h + 64]
            parts.append(jnp.concatenate([k, v, q, g], axis=1))
        packed[2 * n] = jnp.concatenate(parts[:2], axis=0).astype(BF16)
        packed[2 * n + 1] = jnp.concatenate(parts[2:], axis=0).astype(BF16)
        at = pl.ds(2 * n, 2)
        for r in range(8):
            packed_copies.append(
                pltpu.make_async_copy(packed.at[at], packed_far.at[r, at], packed_sems.at[n, r])
            )
            packed_copies[-1].start()
    for copy in packed_copies:
        copy.wait()


def merge_rows(hid32, merged, count):
    for pair in range(count // 2):
        for a in range(MERGE):
            for c in range(MERGE):
                for half in range(2):
                    parts = [
                        hid32[half, pl.ds((4 * i + a) * C4 + c, CCOLS + 2, stride=MERGE), :]
                        for i in (2 * pair, 2 * pair + 1)
                    ]
                    at = (a * MERGE + c) * D0 + half * 128
                    merged[16 * pair : 16 * (pair + 1), at : at + 128] = jnp.concatenate(
                        parts, axis=0
                    ).astype(BF16)


def run_near(place, pieces, gain, w_qkv, w_out, w_merge, gain_coarse, w_coarse, grads):
    own = CROWS * CCOLS
    return pl.pallas_call(
        near_kernel,
        out_shape=pltpu.HBM((8, 8, 2 * own, 256), BF16),
        in_specs=[pl.BlockSpec(memory_space=pltpu.SMEM)]
        + [whole()] * 8
        + [far(), whole(), far(), whole()],
        out_specs=far(),
        scratch_shapes=[
            pltpu.VMEM(((ROWS + 6) * C4, D0), F32),
            pltpu.VMEM(((ROWS + 6) * C4, D0), BF16),
            pltpu.VMEM(((ROWS + 6) * C4, D0), BF16),
            pltpu.VMEM((2, OWN, 128), F32),
            pltpu.VMEM((CROWS * (CCOLS + 2), MERGE * MERGE * D0), BF16),
            pltpu.VMEM(w_merge.shape, BF16),
            pltpu.VMEM(w_coarse.shape, BF16),
            pltpu.VMEM((8, 2 * own, 256), BF16),
            pltpu.SemaphoreType.DMA((4,)),
            pltpu.SemaphoreType.DMA((2,)),
            pltpu.SemaphoreType.DMA((4, 8)),
        ],
        compiler_params=vmem_params(48),
        cost_estimate=pl.CostEstimate(flops=3 * 10**9, bytes_accessed=2 * 10**7, transcendentals=10**6),
        name="near_kernel",
    )(
        place,
        *[piece.reshape(-1, D0) for piece in pieces],
        gain.reshape(1, D0),
        w_qkv,
        w_out,
        in_hbm(w_merge),
        gain_coarse.reshape(1, D1),
        in_hbm(w_coarse),
        grads,
    )


def in_hbm(array):
    return pltpu.with_memory_space_constraint(array, pltpu.HBM)


def wide_kernel(
    place,
    tokens,
    above,
    below,
    left,
    right,
    gain,
    w_qkv,
    w_out,
    w_merge_far,
    stash_far,
    lse,
    coarse_out,
    x32,
    q32,
    k32,
    v32,
    hid32,
    stash,
    merged,
    w_merge,
    merge_sems,
    stash_sem,
):
    merge_copies = fetch(w_merge_far, w_merge, merge_sems, 4)
    for copy in merge_copies:
        copy.start()
    queries = stash.at[pl.ds(AT_Q, N4)]
    attended = stash.at[pl.ds(AT_ATT, N4)]
    keys_w = stash.at[pl.ds(AT_K, WROWS * C4)]
    values_w = stash.at[pl.ds(AT_V, WROWS * C4)]
    tokens_own = stash.at[pl.ds(AT_X, OWN)]
    row0 = place[0]
    col0 = place[1]
    middle = [part[: 8 * COLS].astype(F32) for part in (above, below)]
    middle.insert(1, tokens[...].astype(F32))
    sides = [left[...].astype(F32), right[...].astype(F32)]
    for i in range(R8):
        part, at = (0, i) if i < 8 else (1, i - 8) if i < 8 + ROWS else (2, i - 8 - ROWS)
        x32[C8 * i : C8 * i + 8] = sides[0][8 * i : 8 * i + 8]
        x32[C8 * i + 8 : C8 * i + 8 + COLS] = middle[part][COLS * at : COLS * (at + 1)]
        x32[C8 * i + 8 + COLS : C8 * (i + 1)] = sides[1][8 * i : 8 * i + 8]
    normed, _ = norm_forward(x32[...])
    normed = (normed * gain[...]).astype(BF16)
    q32[...] = dot(normed, w_qkv[:, :D0], 1, 0).astype(BF16).astype(F32) * (HEAD**-0.5)
    k32[...] = dot(normed, w_qkv[:, D0 : 2 * D0], 1, 0).astype(BF16).astype(F32)
    v32[...] = dot(normed, w_qkv[:, 2 * D0 :], 1, 0).astype(BF16).astype(F32)
    for i in range(R4):
        queries[C4 * i : C4 * (i + 1)] = q32[pl.ds((i + 4) * C8 + 4, C4), :].astype(BF16)
    for i in range(WROWS):
        keys_w[C4 * i : C4 * (i + 1)] = k32[pl.ds((i + 1) * C8 + 4, C4), :].astype(BF16)
        values_w[C4 * i : C4 * (i + 1)] = v32[pl.ds((i + 1) * C8 + 4, C4), :].astype(BF16)
    for i in range(ROWS):
        tokens_own[C4 * i : C4 * (i + 1)] = x32[pl.ds((i + 8) * C8 + 4, C4), :].astype(BF16)
    lse[...] = jnp.full(lse.shape, FAR, F32)
    window = window_bias(C8, 1)
    for b in range(BLOCKS):
        start = (4 * b + 1) * C8
        key_block = k32[start : start + 10 * C8].astype(BF16)
        value_block = v32[start : start + 10 * C8].astype(BF16)
        stacked = stack_heads(queries[BLOCK * b : BLOCK * (b + 1)].astype(F32)).astype(BF16)
        bias = all_heads(window + key_bias(C8, row0 - 7 + 4 * b, col0 - 8))
        scores = dot(key_block, stacked, 1, 1) + bias
        maxima = jnp.max(scores, axis=0, keepdims=True)
        exponent = jnp.exp(scores - maxima)
        totals = jnp.sum(exponent, axis=0, keepdims=True)
        weights = (exponent * (1.0 / totals)).astype(BF16)
        result = unstack_heads(dot(weights, value_block, 0, 0)).astype(BF16)
        attended[BLOCK * b : BLOCK * (b + 1)] = result
        lane = lax.broadcasted_iota(jnp.int32, (1, H0 * BLOCK), 1) % BLOCK
        q_row = row0 - 4 + 4 * b + lane // C4
        q_col = col0 - 4 + lane % C4
        q_in = (q_row >= 0) & (q_row < 128) & (q_col >= 0) & (q_col < 384)
        lse[b : b + 1] = jnp.where(q_in, maxima + jnp.log(totals), FAR)
        projected = dot(result, w_out[...], 1, 0)
        for a in range(4):
            own = x32[pl.ds((4 * b + a + 4) * C8 + 4, C4), :]
            total = own + projected[C4 * a : C4 * (a + 1)]
            at = BLOCK * b + C4 * a
            total = total.astype(BF16).astype(F32)
            hid32[0, at : at + C4] = total[:, :128]
            hid32[1, at : at + C4] = total[:, 128:]
    merge_rows(hid32, merged, CROWS + 2)
    stash_copy = pltpu.make_async_copy(stash, stash_far, stash_sem)
    stash_copy.start()
    total = None
    for n, copy in enumerate(merge_copies):
        copy.wait()
        part = dot(merged[:, D1 * n : D1 * (n + 1)], w_merge[D1 * n : D1 * (n + 1)], 1, 0)
        total = part if total is None else total + part
    coarse_out[...] = total.astype(BF16)
    stash_copy.wait()


def run_wide(place, pieces, gain, w_qkv, w_out, w_merge):
    flat = R8 * C8
    return pl.pallas_call(
        wide_kernel,
        out_shape=[
            pltpu.HBM((STASH, D0), BF16),
            pltpu.HBM((8, H0 * BLOCK), F32),
            pltpu.HBM((EXT, D1), BF16),
        ],
        in_specs=[pl.BlockSpec(memory_space=pltpu.SMEM)] + [whole()] * 8 + [far()],
        out_specs=[far(), whole(), whole()],
        scratch_shapes=[pltpu.VMEM((flat, D0), F32)] * 4
        + [
            pltpu.VMEM((2, N4, 128), F32),
            pltpu.VMEM((STASH, D0), BF16),
            pltpu.VMEM((EXT, MERGE * MERGE * D0), BF16),
            pltpu.VMEM(w_merge.shape, BF16),
            pltpu.SemaphoreType.DMA((4,)),
            pltpu.SemaphoreType.DMA(()),
        ],
        compiler_params=vmem_params(40),
        cost_estimate=pl.CostEstimate(flops=3 * 10**9, bytes_accessed=10**7, transcendentals=10**6),
        name="wide_kernel",
    )(
        place,
        *[piece.reshape(-1, D0) for piece in pieces],
        gain.reshape(1, D0),
        w_qkv,
        w_out,
        in_hbm(w_merge),
    )


def lane_half(values, low):
    lanes = lax.broadcasted_iota(jnp.int32, values.shape, 1)
    keep = lanes < HEAD if low else lanes >= HEAD
    return jnp.where(keep, values, jnp.zeros_like(values))


SLAB = 384
SLABS = 8
STRIP = 96
EDGE = SLAB + 2 * STRIP


def strip_pick():
    tile, j = np.divmod(np.arange(STRIP), CCOLS)
    pick = np.zeros((2, STRIP, SLAB), np.float32)
    last = (CROWS - 1) * CCOLS
    pick[0, np.arange(STRIP), tile * CROWS * CCOLS + last + j] = 1
    pick[1, np.arange(STRIP), tile * CROWS * CCOLS + j] = 1
    return pick


def tile_pick():
    c, i, j = np.meshgrid(np.arange(H1), np.arange(6), np.arange(8), indexing="ij")
    tile = (c + (j == 7) - (j == 0)) % H1
    jj = np.where(j == 0, 5, np.where(j == 7, 0, j - 1))
    middle = tile * 24 + (i - 1) * 6 + jj
    source = np.where(i == 0, SLAB + tile * 6 + jj, np.where(i == 5, SLAB + STRIP + tile * 6 + jj, middle))
    pick = np.zeros((H1 * EXT, EDGE), np.float32)
    pick[np.arange(H1 * EXT), source.reshape(-1)] = 1
    return pick


def coarse_forward(place, every, stats, scores_ref):
    keyval = every[:, :128]
    own = every[pl.ds(pl.multiple_of(place[2] * SLAB, SLAB), SLAB), 128:]
    queries = lane_half(own.astype(F32) * (HEAD**-0.5), True).astype(BF16)
    columns = []
    for b in range(3):
        rows = slice(128 * b, 128 * (b + 1))
        scores_ref[b] = dot(queries[rows], keyval, 1, 1)
        maxima = jnp.max(scores_ref[b], axis=1, keepdims=True)
        exponent = jnp.exp(scores_ref[b] - maxima)
        totals = jnp.sum(exponent, axis=1, keepdims=True)
        weights = (exponent * (1.0 / totals)).astype(BF16)
        attended = dot(weights, keyval, 1, 0).astype(BF16).astype(F32)
        product = lane_half(own[rows].astype(F32) * attended, False)
        columns.append((maxima + jnp.log(totals), jnp.sum(product, axis=1, keepdims=True)))
    lane = lax.broadcasted_iota(jnp.int32, (128, 128), 1)
    turned = [
        jnp.where(lane == 0, log, jnp.where(lane == 1, stat, 0.0)).T for log, stat in columns
    ]
    result = jnp.concatenate(
        [t[0:1] for t in turned] + [t[1:2] for t in turned] + [jnp.zeros((2, 128), F32)], axis=0
    )
    for r in range(SLABS):
        stats[r] = result


def run_coarse_forward(place, every):
    return pl.pallas_call(
        coarse_forward,
        out_shape=jax.ShapeDtypeStruct((SLABS, 8, 128), F32),
        in_specs=[pl.BlockSpec(memory_space=pltpu.SMEM), whole()],
        out_specs=whole(),
        scratch_shapes=[pltpu.VMEM((3, 128, SLAB * SLABS), F32)],
        compiler_params=vmem_params(16),
        cost_estimate=pl.CostEstimate(flops=10**9, bytes_accessed=2 * 10**6, transcendentals=10**6),
        name="coarse_forward",
    )(place, every)


def stat_rows(stats):
    lse = jnp.concatenate([stats[k : k + 1] for k in range(3)], axis=1)
    stat = jnp.concatenate([stats[k : k + 1] for k in range(3, 6)], axis=1)
    return lse, stat


def slab_rows(index):
    return pl.ds(pl.multiple_of(index * SLAB, SLAB), SLAB)


def turn(lse, stat):
    filler = jnp.zeros((128 - 2, lse.shape[1]), F32)
    turned = jnp.concatenate([lse, stat, filler], axis=0).T
    return turned[:, 0:1], turned[:, 1:2]


def query_side(every, rows, queries, grads, lse, stat):
    keyval = every[rows, :128]
    probs = jnp.exp(dot(queries, keyval, 1, 1) - lse)
    slopes = (probs * (dot(grads, keyval, 1, 1) - stat)).astype(BF16)
    return dot(slopes, keyval, 1, 0)


def halves(pair):
    wide = pair.astype(F32)
    return lane_half(wide * (HEAD**-0.5), True).astype(BF16), lane_half(wide, False).astype(BF16)


def coarse_own(place, every, stats, strips, edge, dq_out, dq_ref):
    row = place[2]
    edge[:SLAB] = every[slab_rows(row)]
    others = (lax.rem(row + SLABS - 1, SLABS), lax.rem(row + 1, SLABS))
    for k, other in enumerate(others):
        at = SLAB + STRIP * k
        edge[at : at + STRIP] = dot(strips[k], every[slab_rows(other)], 1, 0).astype(BF16)
    lse, stat = turn(*stat_rows(stats[0]))
    queries, grads = halves(edge[:SLAB, 128:])
    for n in range(SLABS // 2):
        rows = slice(2 * n * SLAB, 2 * (n + 1) * SLAB)
        term = query_side(every, rows, queries, grads, lse, stat)
        dq_ref[...] = term if n == 0 else dq_ref[...] + term
    dq_out[...] = (dq_ref[...] * (HEAD**-0.5)).astype(BF16)


def run_coarse_own(place, every, stats, strips):
    return pl.pallas_call(
        coarse_own,
        out_shape=[
            pltpu.HBM((EDGE, 256), BF16),
            pltpu.HBM((SLAB, 128), BF16),
        ],
        in_specs=[pl.BlockSpec(memory_space=pltpu.SMEM)] + [whole()] * 3,
        out_specs=[whole()] * 2,
        scratch_shapes=[pltpu.VMEM((SLAB, 128), F32)],
        compiler_params=vmem_params(24),
        cost_estimate=pl.CostEstimate(flops=10**9, bytes_accessed=2 * 10**6, transcendentals=10**6),
        name="coarse_own",
    )(place, every, stats, strips)


def coarse_backward(
    place,
    every,
    stats,
    strips,
    edge,
    dq_own,
    tiles_far,
    coarse_far,
    stash_far,
    out,
    w_coarse,
    stash,
    dq_ref,
    dk_ref,
    dv_ref,
    tiles,
    sems,
):
    pairs = (
        (tiles_far, tiles),
        (coarse_far, w_coarse),
        (stash_far, stash),
    )
    copies = [pltpu.make_async_copy(a, b, sems.at[n]) for n, (a, b) in enumerate(pairs)]
    for copy in copies:
        copy.start()
    row = place[2]
    others = (lax.rem(row + SLABS - 1, SLABS), lax.rem(row + 1, SLABS))
    taken = []
    for k, other in enumerate(others):
        both = jnp.concatenate(stat_rows(stats[other]) + (jnp.zeros((6, SLAB), F32),), axis=0)
        taken.append(
            lax.dot_general(
                both,
                strips[k].astype(F32),
                (((1,), (1,)), ((), ())),
                precision=lax.Precision.HIGHEST,
                preferred_element_type=F32,
            )
        )
    strip_lse, strip_stat = turn(
        jnp.concatenate([t[0:1] for t in taken], axis=1),
        jnp.concatenate([t[1:2] for t in taken], axis=1),
    )
    edge_k, edge_v = halves(edge[:, :128])
    edge_q, edge_g = halves(edge[SLAB:, 128:])
    for n in range(SLABS // 2):
        rows = slice(2 * n * SLAB, 2 * (n + 1) * SLAB)
        dq = query_side(every, rows, edge_q, edge_g, strip_lse, strip_stat)
        query = every[rows, 128:]
        both = [stat_rows(stats[2 * n + k]) for k in range(2)]
        lse = jnp.concatenate([pair[0] for pair in both], axis=1)
        stat = jnp.concatenate([pair[1] for pair in both], axis=1)
        probs = jnp.exp(dot(edge_k, query, 1, 1) - lse)
        slopes = (probs * (dot(edge_v, query, 1, 1) - stat)).astype(BF16)
        dk = dot(slopes, query, 1, 0)
        dv = dot(probs.astype(BF16), query, 1, 0)
        if n == 0:
            dq_ref[...] = dq
            dk_ref[...] = dk
            dv_ref[...] = dv
        else:
            dq_ref[...] += dq
            dk_ref[...] += dk
            dv_ref[...] += dv
    lanes = lax.broadcasted_iota(jnp.int32, (EDGE, 128), 1)
    keyval = jnp.where(lanes < HEAD, dk_ref[...] * (HEAD**-0.5), dv_ref[...]).astype(BF16)
    query = jnp.concatenate(
        [dq_own[...], (dq_ref[...] * (HEAD**-0.5)).astype(BF16)], axis=0
    )
    copies[0].wait()
    out[...] = dot(tiles[...], jnp.concatenate([keyval, query], axis=1), 1, 0).astype(BF16)
    for copy in copies[1:]:
        copy.wait()


def run_coarse_backward(place, every, stats, strips, edge, dq_own, *later):
    tiles = jnp.asarray(tile_pick(), BF16)
    return pl.pallas_call(
        coarse_backward,
        out_shape=[pltpu.HBM((H1 * EXT, 256), BF16)]
        + [pltpu.VMEM(array.shape, array.dtype) for array in later],
        in_specs=[pl.BlockSpec(memory_space=pltpu.SMEM)] + [whole()] * 5 + [far()] * 3,
        out_specs=[whole()] * 3,
        scratch_shapes=[
            pltpu.VMEM((2 * STRIP, 128), F32),
            pltpu.VMEM((EDGE, 128), F32),
            pltpu.VMEM((EDGE, 128), F32),
            pltpu.VMEM(tiles.shape, BF16),
            pltpu.SemaphoreType.DMA((3,)),
        ],
        compiler_params=vmem_params(24),
        cost_estimate=pl.CostEstimate(flops=3 * 10**9, bytes_accessed=2 * 10**6, transcendentals=4 * 10**6),
        name="coarse_backward",
    )(
        place,
        every,
        stats,
        strips,
        in_hbm(edge),
        in_hbm(dq_own),
        *[in_hbm(array) for array in (tiles,) + later],
    )


def block_pick():
    c, b = np.meshgrid(np.arange(H1), np.arange(64), indexing="ij")
    source = np.where(b < 48, 48 * c + b, 3 * D0 + 16 * c + b - 48).reshape(-1)
    pick = np.zeros((4 * D0, 4 * D0), np.float32)
    pick[source, np.arange(4 * D0)] = 1
    return pick


def merged_order(back):
    rows = lax.broadcasted_iota(jnp.int32, (BLOCK, BLOCK), 0)
    cols = lax.broadcasted_iota(jnp.int32, (BLOCK, BLOCK), 1)
    merged, grid = (cols, rows) if back else (rows, cols)
    a = merged // C4
    c = merged // 8 % MERGE
    j = merged % 8
    return (grid == a * C4 + j * MERGE + c).astype(F32).astype(BF16)


def backward_kernel(
    place,
    terms_coarse,
    own_fine,
    own_coarse,
    above,
    below,
    grads_left,
    grads_right,
    coarse,
    lse,
    gain_coarse,
    gain,
    w_qkv,
    w_out,
    w_coarse,
    stash,
    pick_far,
    w_merge_far,
    grad_tokens,
    terms,
    grad_fine,
    sp32,
    gh_ref,
    ga_ref,
    dq_ref,
    dk_ref,
    dv_ref,
    gt_ref,
    pick_block,
    w_merge,
    stack_ref,
    probs_ref,
    merge_sems,
    pick_sem,
):
    merge_copies = fetch(w_merge_far, w_merge, merge_sems, 4)
    pick_copy = pltpu.make_async_copy(pick_far, pick_block, pick_sem)
    for copy in merge_copies + [pick_copy]:
        copy.start()
    queries = stash.at[pl.ds(AT_Q, N4)]
    attended = stash.at[pl.ds(AT_ATT, N4)]
    keys_w = stash.at[pl.ds(AT_K, WROWS * C4)]
    values_w = stash.at[pl.ds(AT_V, WROWS * C4)]
    tokens_own = stash.at[pl.ds(AT_X, OWN)]
    row0 = place[0]
    col0 = place[1]
    wide = CCOLS + 2
    fine_rows, coarse_rows = grads_of(own_fine, own_coarse, above, below)
    side = [part[...].astype(F32) for part in (grads_left, grads_right)]
    for i, row in enumerate(fine_rows):
        outer = [part[4 * i : 4 * (i + 1)] for part in side]
        grad_fine[C4 * i : C4 * (i + 1)] = jnp.concatenate([outer[0], row, outer[1]], axis=0)
    grad_coarse = []
    for i, row in enumerate(coarse_rows):
        parts = []
        for g, piece in enumerate(row):
            at = 4 * R4 + 4 * i + g
            outer = [part[at : at + 1] for part in side]
            parts.append(jnp.concatenate([outer[0], piece, outer[1]], axis=0))
        grad_coarse.append(jnp.concatenate(parts, axis=1))
    grad_coarse = jnp.concatenate(grad_coarse, axis=0)
    parts = []
    for h in range(H1):
        block = terms_coarse[h].astype(F32)
        parts += [block[:, 128:192], block[:, :128]]
    heads = jnp.concatenate(parts, axis=1).astype(BF16)
    upstream = dot(heads, w_coarse[...], 1, 1) * gain_coarse[...]
    normed, inverse = norm_forward(coarse[...].astype(F32))
    back = norm_backward(upstream, normed, inverse)
    change = (grad_coarse + back).astype(BF16)
    for a, copy in enumerate(merge_copies):
        copy.wait()
        sp32[a] = dot(change, w_merge[D1 * a : D1 * (a + 1)], 1, 1)
    window = window_bias(C4, -3)
    for b in range(BLOCKS):
        stacked = stack_heads(queries[BLOCK * b : BLOCK * (b + 1)].astype(F32)).astype(BF16)
        stack_ref[b] = stacked
        bias = all_heads(window + key_bias(C4, row0 - 7 + 4 * b, col0 - 4))
        scores = dot(keys_w[BLOCK * b : BLOCK * b + 10 * C4], stacked, 1, 1) + bias
        probs_ref[b] = jnp.exp(scores - lse[b : b + 1])
    to_merged = merged_order(False)
    to_grid = merged_order(True)
    for i in range(CROWS + 2):
        block = slice(BLOCK * i, BLOCK * (i + 1))
        rows = slice(wide * i, wide * (i + 1))
        spread = [
            sp32[a, rows, D0 * c : D0 * (c + 1)] for a in range(MERGE) for c in range(MERGE)
        ]
        total = dot(to_merged, grad_fine[block].astype(BF16), 1, 0) + jnp.concatenate(spread, axis=0)
        gh_ref[block] = dot(to_grid, total.astype(BF16), 1, 0).astype(BF16)
    ga_ref[...] = dot(gh_ref[...], w_out[...], 1, 1).astype(BF16)
    dk_ref[...] = jnp.zeros_like(dk_ref)
    dv_ref[...] = jnp.zeros_like(dv_ref)
    pick = (
        lax.broadcasted_iota(jnp.int32, (8, D0), 1) // HEAD
        == lax.broadcasted_iota(jnp.int32, (8, D0), 0)
    ).astype(F32).astype(BF16)
    for b in range(BLOCKS):
        at = slice(BLOCK * b, BLOCK * (b + 1))
        keep = slice(BLOCK * b, BLOCK * b + 10 * C4)
        grad = ga_ref[at].astype(F32)
        product = grad * attended[at].astype(F32)
        upper = product.astype(BF16)
        lower = (product - upper.astype(F32)).astype(BF16)
        sums = dot(pick, upper, 1, 1) + dot(pick, lower, 1, 1)
        stat = jnp.concatenate([sums[h : h + 1] for h in range(H0)], axis=1)
        stack_q = stack_ref[b]
        stack_g = stack_heads(grad).astype(BF16)
        key_block = keys_w[keep]
        probs = probs_ref[b]
        slopes = (probs * (dot(values_w[keep], stack_g, 1, 1) - stat)).astype(BF16)
        dk_ref[keep] += dot(slopes, stack_q, 1, 0)
        dv_ref[keep] += dot(probs.astype(BF16), stack_g, 1, 0)
        if 1 <= b <= 4:
            dq = unstack_heads(dot(slopes, key_block, 0, 0)) * (HEAD**-0.5)
            dq_ref[BLOCK * (b - 1) : BLOCK * b] = dq.astype(BF16)
    own = slice(7 * C4, 7 * C4 + OWN)
    grads = jnp.concatenate(
        [dq_ref[...], dk_ref[own].astype(BF16), dv_ref[own].astype(BF16)], axis=1
    )
    column = lax.broadcasted_iota(jnp.int32, (ROWS, C4, D0), 1).reshape(OWN, D0)
    in_tile = (column >= 4) & (column < 4 + COLS)
    normed, inverse = norm_forward(tokens_own[...].astype(F32))
    rounded = jnp.where(in_tile, normed * gain[...], 0.0).astype(BF16)
    term_qkv = dot(rounded, grads, 0, 0).astype(BF16)
    inner = slice(BLOCK, BLOCK + OWN)
    att = jnp.where(in_tile, attended[inner].astype(F32), 0.0).astype(BF16)
    term_out = dot(att, gh_ref[inner], 0, 0).astype(BF16)
    pick_copy.wait()
    both = dot(jnp.concatenate([term_qkv, term_out], axis=1), pick_block[...], 1, 0)
    low = lax.broadcasted_iota(jnp.int32, (16, 128), 1) < 64
    for r in range(8):
        for m in range(8):
            first = both[32 * r : 32 * r + 16, 128 * m : 128 * (m + 1)]
            last = both[32 * r + 16 : 32 * (r + 1), 128 * m : 128 * (m + 1)]
            terms[16 * r + 2 * m] = jnp.where(low, first, pltpu.roll(last, 64, 1)).astype(BF16)
            terms[16 * r + 2 * m + 1] = jnp.where(low, pltpu.roll(first, 64, 1), last).astype(BF16)
    upstream = dot(grads, w_qkv[...], 1, 1) * gain[...]
    gt_ref[...] = gh_ref[inner].astype(F32) + norm_backward(upstream, normed, inverse)
    for pair in range(ROWS // 2):
        parts = [gt_ref[pl.ds(i * C4 + 4, COLS), :] for i in (2 * pair, 2 * pair + 1)]
        grad_tokens[2 * COLS * pair : 2 * COLS * (pair + 1)] = jnp.concatenate(
            parts, axis=0
        ).astype(BF16)


def run_backward(place, *operands):
    shapes = [((ROWS * COLS, D0), BF16), ((128, 16, 128), BF16)]
    return pl.pallas_call(
        backward_kernel,
        out_shape=[jax.ShapeDtypeStruct(s, d) for s, d in shapes],
        in_specs=[pl.BlockSpec(memory_space=pltpu.SMEM)] + [whole()] * 15 + [far()] * 2,
        out_specs=[whole()] * 2,
        scratch_shapes=[
            pltpu.VMEM((N4, D0), F32),
            pltpu.VMEM((MERGE, EXT, D1), F32),
            pltpu.VMEM((N4, D0), BF16),
            pltpu.VMEM((N4, D0), BF16),
            pltpu.VMEM((OWN, D0), BF16),
            pltpu.VMEM((WROWS * C4, D0), F32),
            pltpu.VMEM((WROWS * C4, D0), F32),
            pltpu.VMEM((OWN, D0), F32),
            pltpu.VMEM((4 * D0, 4 * D0), BF16),
            pltpu.VMEM((MERGE * MERGE * D0, D1), BF16),
            pltpu.VMEM((BLOCKS, H0 * BLOCK, D0), BF16),
            pltpu.VMEM((BLOCKS, 10 * C4, H0 * BLOCK), F32),
            pltpu.SemaphoreType.DMA((4,)),
            pltpu.SemaphoreType.DMA(()),
        ],
        compiler_params=vmem_params(40),
        cost_estimate=pl.CostEstimate(flops=5 * 10**9, bytes_accessed=2 * 10**7, transcendentals=10**6),
        name="backward_kernel",
    )(place, *operands[:-2], *[in_hbm(operand) for operand in operands[-2:]])


def sum_terms(terms, out_qkv, out_out):
    total = jnp.sum(terms[...].astype(F32), axis=0)
    total = jnp.concatenate([total[:, :64], total[:, 64:]], axis=0)
    out_qkv[...] = total[:, :48]
    out_out[...] = total[:, 48:].T


def run_sum_terms(terms):
    return pl.pallas_call(
        sum_terms,
        out_shape=[jax.ShapeDtypeStruct((32, 48), F32), jax.ShapeDtypeStruct((16, 32), F32)],
        in_specs=[whole()],
        out_specs=[whole()] * 2,
        compiler_params=vmem_params(8),
        name="sum_terms",
    )(terms)


def ring(axis, step):
    devices = lax.axis_size(axis)
    return [(i, (i + step) % devices) for i in range(devices)]


def swap_edges(first, last, axis):
    before = lax.ppermute(last, axis, ring(axis, 1))
    after = lax.ppermute(first, axis, ring(axis, -1))
    return before, after


HALO = 8
TOKEN_ROWS = HALO * COLS
FINE_ROWS = 4 * COLS
STRIP_ROWS = TOKEN_ROWS + FINE_ROWS + 4 * CCOLS


def row_strips(tokens, grad_fine, grad_coarse, first, last, flat, held, sems):
    fine_at = pl.ds(TOKEN_ROWS, FINE_ROWS)
    own = ROWS * COLS
    copies = [
        pltpu.make_async_copy(grad_coarse, held, sems.at[0]),
        pltpu.make_async_copy(
            tokens.at[pl.ds(0, TOKEN_ROWS)], first.at[pl.ds(0, TOKEN_ROWS)], sems.at[1]
        ),
        pltpu.make_async_copy(
            tokens.at[pl.ds(own - TOKEN_ROWS, TOKEN_ROWS)],
            last.at[pl.ds(0, TOKEN_ROWS)],
            sems.at[2],
        ),
        pltpu.make_async_copy(grad_fine.at[pl.ds(0, FINE_ROWS)], first.at[fine_at], sems.at[3]),
        pltpu.make_async_copy(
            grad_fine.at[pl.ds(own - FINE_ROWS, FINE_ROWS)], last.at[fine_at], sems.at[4]
        ),
    ]
    for copy in copies:
        copy.start()
    copies[0].wait()
    wide = held[...].astype(F32)
    rows = [wide[:, i, :] for i in range(CROWS)]
    flat[...] = jnp.concatenate(rows, axis=0).astype(BF16)
    for out, coarse in ((first, rows[0]), (last, rows[-1])):
        pieces = [coarse[:, D0 * g : D0 * (g + 1)] for g in range(4)]
        out[TOKEN_ROWS + FINE_ROWS :] = jnp.concatenate(pieces, axis=0).astype(BF16)
    for copy in copies[1:]:
        copy.wait()


def run_row_strips(tokens, grad_fine, grad_coarse):
    shapes = [(STRIP_ROWS, D0), (STRIP_ROWS, D0), (CROWS * CCOLS, D1)]
    operands = (tokens.reshape(-1, D0), grad_fine.reshape(-1, D0), grad_coarse.transpose(1, 0, 2))
    return pl.pallas_call(
        row_strips,
        out_shape=[jax.ShapeDtypeStruct(shape, BF16) for shape in shapes],
        in_specs=[far()] * 3,
        out_specs=[whole()] * 3,
        scratch_shapes=[
            pltpu.VMEM((CCOLS, CROWS, D1), BF16),
            pltpu.SemaphoreType.DMA((5,)),
        ],
        compiler_params=vmem_params(8),
        name="row_strips",
    )(*[in_hbm(operand) for operand in operands])


def column_strips(tokens, above, below, first, last):
    parts = [part[:TOKEN_ROWS].astype(F32) for part in (above, below)]
    parts.insert(1, tokens[...].astype(F32))
    left = []
    right = []
    for part in parts:
        for i in range(part.shape[0] // COLS):
            left.append(part[COLS * i : COLS * i + HALO])
            right.append(part[COLS * (i + 1) - HALO : COLS * (i + 1)])
    first[...] = jnp.concatenate(left, axis=0).astype(BF16)
    last[...] = jnp.concatenate(right, axis=0).astype(BF16)


def run_column_strips(tokens, above, below):
    return pl.pallas_call(
        column_strips,
        out_shape=[jax.ShapeDtypeStruct((R8 * HALO, D0), BF16)] * 2,
        in_specs=[whole()] * 3,
        out_specs=[whole()] * 2,
        compiler_params=vmem_params(8),
        name="column_strips",
    )(in_hbm(tokens.reshape(-1, D0)), above, below)


def grads_of(own_fine, own_coarse, above, below):
    at = TOKEN_ROWS + FINE_ROWS
    fine = []
    coarse = []
    for outer in (above, below):
        outer_fine = outer[TOKEN_ROWS:at].astype(F32)
        outer_coarse = outer[at:].astype(F32)
        fine.append([outer_fine[COLS * i : COLS * (i + 1)] for i in range(4)])
        coarse.append([outer_coarse[CCOLS * g : CCOLS * (g + 1)] for g in range(4)])
    wide = own_fine[...].astype(F32)
    flat = own_coarse[...].astype(F32)
    fine_rows = fine[0] + [wide[COLS * i : COLS * (i + 1)] for i in range(ROWS)] + fine[1]
    own = [
        [flat[CCOLS * i : CCOLS * (i + 1), D0 * g : D0 * (g + 1)] for g in range(4)]
        for i in range(CROWS)
    ]
    return fine_rows, [coarse[0]] + own + [coarse[1]]


def grad_strips(own_fine, own_coarse, above, below, first, last):
    fine, coarse = grads_of(own_fine, own_coarse, above, below)
    left = [row[:4] for row in fine] + [piece[:1] for row in coarse for piece in row]
    right = [row[-4:] for row in fine] + [piece[-1:] for row in coarse for piece in row]
    first[...] = jnp.concatenate(left, axis=0).astype(BF16)
    last[...] = jnp.concatenate(right, axis=0).astype(BF16)


def run_grad_strips(own_fine, own_coarse, above, below):
    return pl.pallas_call(
        grad_strips,
        out_shape=[jax.ShapeDtypeStruct((R4 * 4 + EXT // 2, D0), BF16)] * 2,
        in_specs=[whole()] * 4,
        out_specs=[whole()] * 2,
        compiler_params=vmem_params(8),
        name="grad_strips",
    )(own_fine, own_coarse, above, below)


def on_device(
    tokens,
    grad_fine,
    grad_coarse,
    fine_gain,
    fine_qkv,
    fine_out,
    merge_weight,
    coarse_gain,
    coarse_qkv,
    coarse_out,
):
    row = lax.axis_index("row")
    col = lax.axis_index("col")
    place = jnp.stack([row * ROWS, col * COLS, row]).astype(jnp.int32)
    first, last, grad_coarse = run_row_strips(tokens, grad_fine, grad_coarse)
    above, below = swap_edges(first, last, "row")
    left, right = swap_edges(*run_column_strips(tokens, above, below), "col")
    pieces = (tokens, above, below, left, right)
    grad_heads = jnp.dot(grad_coarse, coarse_out.T, preferred_element_type=F32).astype(BF16)
    packed = run_near(
        place,
        pieces,
        fine_gain,
        fine_qkv,
        fine_out,
        merge_weight,
        coarse_gain,
        coarse_qkv,
        grad_heads,
    )
    packed, grad_fine, grad_coarse, *pieces = lax.optimization_barrier(
        (packed, grad_fine, grad_coarse, *pieces)
    )
    every = lax.all_to_all(
        packed.reshape(8 * H1, CROWS * CCOLS, 256),
        ("row", "col"),
        split_axis=0,
        concat_axis=0,
        tiled=True,
    )
    grads = (grad_fine.reshape(-1, D0), grad_coarse, pieces[1], pieces[2])
    left, right = swap_edges(*run_grad_strips(*grads), "col")
    stash, lse, coarse = run_wide(place, pieces, fine_gain, fine_qkv, fine_out, merge_weight)
    every, left, right, stash, lse, coarse = lax.optimization_barrier(
        (every, left, right, stash, lse, coarse)
    )
    every = every.reshape(SLAB * SLABS, 256)
    strips = jnp.asarray(strip_pick(), BF16)
    own_stats = run_coarse_forward(place, every)
    stats = lax.all_to_all(own_stats, "row", split_axis=0, concat_axis=0, tiled=True)
    edge, dq_own = run_coarse_own(place, every, own_stats, strips)
    tiles, near_coarse, stash = run_coarse_backward(
        place, every, stats, strips, edge, dq_own, coarse_qkv, stash
    )
    tiles = tiles.reshape(H1, EXT, 256)
    terms = lax.all_to_all(tiles, "col", split_axis=0, concat_axis=0, tiled=True)
    grad_tokens, blocks = run_backward(
        place,
        terms,
        *grads,
        left,
        right,
        coarse,
        lse,
        coarse_gain.reshape(1, D1),
        fine_gain.reshape(1, D0),
        fine_qkv,
        fine_out,
        near_coarse,
        stash,
        jnp.asarray(block_pick(), BF16),
        merge_weight,
    )
    blocks = lax.all_to_all(blocks, ("row", "col"), split_axis=0, concat_axis=0, tiled=True)
    grad_qkv, grad_out = run_sum_terms(blocks)
    return grad_tokens.reshape(ROWS, COLS, D0), grad_qkv, grad_out.T


def solution(mesh):
    return jax.shard_map(
        on_device,
        mesh=mesh,
        in_specs=(P("row", "col", None),) * 3 + (P(),) * 7,
        out_specs=(P("row", "col", None), P("row", "col"), P("row", "col")),
        check_vma=False,
    )
```

time: 148 us -> 141 us (0.953)
  Pallas kernels: 46.8 us -> 55.9 us
  blocking collectives: 42.6 us -> 33.5 us
  waiting for transfers between devices: 27.8 us -> 24.5 us
  other arithmetic: 1.63 us -> 0.09 us
    ppermute x4 -> x3, waiting for transfers between devices: 24.1 us -> 5.45 us  [swap_edges(): before = lax.ppermute(last, axis, ring(axis, 1))]
    pallas_call x2 -> x7, Pallas kernels: 24.3 us -> 37.5 us  [the longest x1 11 us: run_coarse_backward(): pl.pallas_call(coarse_backward, out_shape=[pltpu.HBM((H1 * EXT, 256), BF1...]
    all_to_all x1 -> x0, blocking collectives: 9.1 us -> none  [on_device(): lax.all_to_all(stats, 'row', split_axis=0, concat_axis=0, tiled=True)]
    ppermute x4 -> x3, waiting for transfers between devices: 3.02 us -> 10.2 us  [swap_edges(): after = lax.ppermute(first, axis, ring(axis, -1))]
    ppermute x4 -> x3, starting transfers between devices: 9.19 us -> 2.28 us  [swap_edges(): after = lax.ppermute(first, axis, ring(axis, -1))]
    all_to_all x1, waiting for transfers between devices: 0.71 us -> 7.1 us  [on_device(): lax.all_to_all(packed.reshape(8 * H1, CROWS * CCOLS, 256), ('row', 'col')...]
    pallas_call x1, Pallas kernels: 16.6 us -> 12.5 us  [run_backward(): pl.pallas_call(backward_kernel, out_shape=[jax.ShapeDtypeStruct(s, d) for...]
    all_to_all x0 -> x1, starting transfers between devices: none -> 3.55 us  [on_device(): lax.all_to_all(own_stats, 'row', split_axis=0, concat_axis=0, tiled=True)]
  transfers between devices with their start and end apart: 9 -> 8, of which waited for: 5 -> 7; matrix products, arithmetic and copies ran while one was open for 2% -> 1% of each run, Pallas kernels for 0% -> 10%
where the time goes in v1:
time: 141 us
  Pallas kernels  55.9 us (40%)
  blocking collectives  33.5 us (24%)
  waiting for transfers between devices  24.5 us (17%)
  starting transfers between devices  22.6 us (16%)
  local copies, waits for them, and re-layouts  2.84 us (2%)
    all_to_all x1, blocking collectives, on_device(): lax.all_to_all(blocks, ('row', 'col'), split_axis=0, concat_axis=0, tiled...  18.2 us
    all_to_all x1, blocking collectives, on_device(): lax.all_to_all(tiles, 'col', split_axis=0, concat_axis=0, tiled=True)  15.3 us
    pallas_call x1, Pallas kernels, run_backward(): pl.pallas_call(backward_kernel, out_shape=[jax.ShapeDtypeStruct(s, d) for...  12.5 us
    pallas_call x1, Pallas kernels, run_coarse_backward(): pl.pallas_call(coarse_backward, out_shape=[pltpu.HBM((H1 * EXT, 256), BF1...  11 us
    ppermute x3, waiting for transfers between devices, swap_edges(): after = lax.ppermute(first, axis, ring(axis, -1))  10.2 us
    pallas_call x1, Pallas kernels, run_wide(): pl.pallas_call(wide_kernel, out_shape=[pltpu.HBM((STASH, D0), BF16), pltp...  9.75 us
    pallas_call x1, Pallas kernels, run_near(): pl.pallas_call(near_kernel, out_shape=pltpu.HBM((8, 8, 2 * own, 256), BF1...  9.43 us
    all_to_all x1, starting transfers between devices, on_device(): lax.all_to_all(packed.reshape(8 * H1, CROWS * CCOLS, 256), ('row', 'col')...  8.87 us
  transfers between devices with their start and end apart: 8, of which 7 were waited for; matrix products, arithmetic and copies ran while one was open for 1% of the time, Pallas kernels for 10%

profile of v1, /device:TPU:1, one launch (start us, length us, event | category | flops | bytes accessed | tf_op | source)
XLA Modules:
  0.0 140.9 jit_solution(8348084512898833436)
XLA Ops:
  0.6 0.0 copy-start
  0.6 0.0 copy-start.2
  0.7 0.0 copy-start.4
  0.7 0.0 copy-start.3
  0.7 0.0 copy-start.14
  0.7 0.0 copy-start.15
  0.7 1.2 row_strips.1
  1.9 4.5 %collective-permute-start = (bf16[312,256]{1,0:T(8,128)(2,1)S(1)}, bf16[312,256]{1,0:T(8,128)(2,1)S(1)}, u32[]{:S(2)}, u32[]{:S(2)}) collective-permute-start(bf16[312,256]{1,0:T(8,128)(2,1)S(1)} %get-tuple-element.36), channel_id=1, source_target_pairs={{0,16},{16,32},{32,48},{48,64},{64,80},{80,96},{96,112},{112,0},{1... | collective-permute-start | bytes 479240 | tf_op jit(solution)/shard_map/ppermute | solution.py:868
  6.4 2.3 %collective-permute-start.1 = (bf16[312,256]{1,0:T(8,128)(2,1)S(1)}, bf16[312,256]{1,0:T(8,128)(2,1)S(1)}, u32[]{:S(2)}, u32[]{:S(2)}) collective-permute-start(bf16[312,256]{1,0:T(8,128)(2,1)S(1)} %get-tuple-element.37), channel_id=1, source_target_pairs={{0,112},{16,0},{32,16},{48,32},{64,48},{80,64},{96,80},{112,96},{1... | collective-permute-start | bytes 479240 | tf_op jit(solution)/shard_map/ppermute | solution.py:869
  8.6 3.9 %collective-permute-done.above = bf16[312,256]{1,0:T(8,128)(2,1)S(1)} collective-permute-done((bf16[312,256]{1,0:T(8,128)(2,1)S(1)}, bf16[312,256]{1,0:T(8,128)(2,1)S(1)}, u32[]{:S(2)}, u32[]{:S(2)}) %collective-permute-start) | collective-permute-done | bytes 159776 | tf_op jit(solution)/shard_map/ppermute | solution.py:868
  12.6 4.0 %collective-permute-done.1.below = bf16[312,256]{1,0:T(8,128)(2,1)S(1)} collective-permute-done((bf16[312,256]{1,0:T(8,128)(2,1)S(1)}, bf16[312,256]{1,0:T(8,128)(2,1)S(1)}, u32[]{:S(2)}, u32[]{:S(2)}) %collective-permute-start.1) | collective-permute-done | bytes 159776 | tf_op jit(solution)/shard_map/ppermute | solution.py:869
  16.6 1.6 %column_strips.1 = (bf16[256,256]{1,0:T(8,128)(2,1)}, bf16[256,256]{1,0:T(8,128)(2,1)}) custom-call(bf16[384,256]{1,0:T(8,128)(2,1)} %bitcast.21, bf16[312,256]{1,0:T(8,128)(2,1)S(1)} %collective-permute-done.above, bf16[312,256]{1,0:T(8,128)(2,1)S(1)} %collective-permute-done.1.below), custom_call_target="tpu_custom_call" | custom-call | tf_op jit(solution)/shard_map/column_strips/pallas_call | solution.py:941
  18.2 1.7 %collective-permute-start.2 = (bf16[256,256]{1,0:T(8,128)(2,1)}, bf16[256,256]{1,0:T(8,128)(2,1)S(1)}, u32[]{:S(2)}, u32[]{:S(2)}) collective-permute-start(bf16[256,256]{1,0:T(8,128)(2,1)} %get-tuple-element.38), channel_id=1, source_target_pairs={{0,1},{1,2},{2,3},{3,4},{4,5},{5,6},{6,7},{7,8},{8,9},{9,10},{10,1... | collective-permute-start | bytes 393224 | tf_op jit(solution)/shard_map/ppermute | solution.py:868
  19.9 0.0 collective-permute-start.3
  19.9 0.0 copy-done
  19.9 0.7 convolution_convert_fusion.grads
  20.5 0.1 pad_add_fusion.place
  20.6 1.5 %collective-permute-done.2.left = bf16[256,256]{1,0:T(8,128)(2,1)S(1)} collective-permute-done((bf16[256,256]{1,0:T(8,128)(2,1)}, bf16[256,256]{1,0:T(8,128)(2,1)S(1)}, u32[]{:S(2)}, u32[]{:S(2)}) %collective-permute-start.2) | collective-permute-done | bytes 131104 | tf_op jit(solution)/shard_map/ppermute | solution.py:868
  22.1 2.6 %collective-permute-done.3.right = bf16[256,256]{1,0:T(8,128)(2,1)S(1)} collective-permute-done((bf16[256,256]{1,0:T(8,128)(2,1)}, bf16[256,256]{1,0:T(8,128)(2,1)S(1)}, u32[]{:S(2)}, u32[]{:S(2)}) %collective-permute-start.3) | collective-permute-done | bytes 131104 | tf_op jit(solution)/shard_map/ppermute | solution.py:869
  24.8 0.0 copy-done.4
  24.8 9.4 %near_kernel.1 = bf16[8,8,48,256]{3,2,1,0:T(8,128)(2,1)} custom-call(s32[3]{0:T(128)S(1)} %pad_add_fusion.place, bf16[384,256]{1,0:T(8,128)(2,1)S(1)} %bitcast.22, bf16[312,256]{1,0:T(8,128)(2,1)S(1)} %collective-permute-done.above, bf16[312,256]{1,0:T(8,128)(2,1)S(1)} %collective-permute-done.1.below, bf16[256,256]{1,0:T(8,128)(2,1)S(1)} %collective-permute-done.2.left, ...), custom_call_target="tpu_custom_call" | custom-call | flops 3000000000 | bytes 20000000 | tf_op jit(solution)/shard_map/near_kernel/pallas_call | solution.py:245
  34.2 0.0 copy-start.6
  34.2 0.6 copy-done.6
  34.9 8.9 %all-to-all-start = ((bf16[128,24,256]{2,1,0:T(8,128)(2,1)}), bf16[128,24,256]{2,1,0:T(8,128)(2,1)}, u32[]{:S(2)}, u32[]{:S(2)}) async-start(bf16[128,24,256]{2,1,0:T(8,128)(2,1)} %bitcast.29), calls=%async_computation | async-start | bytes 3145728 | tf_op jit(solution)/shard_map/all_to_all | solution.py:1023
  43.8 0.0 copy-done.1
  43.8 0.1 grad_strips.1
  43.8 1.7 %collective-permute-start.4 = (bf16[120,256]{1,0:T(8,128)(2,1)S(1)}, bf16[120,256]{1,0:T(8,128)(2,1)S(1)}, u32[]{:S(2)}, u32[]{:S(2)}) collective-permute-start(bf16[120,256]{1,0:T(8,128)(2,1)S(1)} %get-tuple-element.46), channel_id=1, source_target_pairs={{0,1},{1,2},{2,3},{3,4},{4,5},{5,6},{6,7},{7,8},{8,9},{9,10},{10,1... | collective-permute-start | bytes 184328 | tf_op jit(solution)/shard_map/ppermute | solution.py:868
  45.5 0.0 collective-permute-start.5
  45.6 0.9 copy-done.7
  46.5 9.7 %wide_kernel.1 = (bf16[3968,256]{1,0:T(8,128)(2,1)}, f32[8,512]{1,0:T(8,128)}, bf16[48,1024]{1,0:T(8,128)(2,1)}) custom-call(s32[3]{0:T(128)S(1)} %pad_add_fusion.place, bf16[384,256]{1,0:T(8,128)(2,1)S(1)} %bitcast.23, bf16[312,256]{1,0:T(8,128)(2,1)S(1)} %collective-permute-done.above, bf16[312,256]{1,0:T(8,128)(2,1)S(1)} %collective-permute-done.1.below, ...), custom_call_target="tpu_custom_call" | custom-call | flops 3000000000 | bytes 10000000 | tf_op jit(solution)/shard_map/wide_kernel/pallas_call | solution.py:382
  56.2 0.0 copy-start.5
  56.2 0.0 collective-permute-done.4.grads_left
  56.2 0.0 copy-start.9
  56.2 0.6 copy-done.9
  56.9 3.6 %collective-permute-done.5.grads_right = bf16[120,256]{1,0:T(8,128)(2,1)S(1)} collective-permute-done((bf16[120,256]{1,0:T(8,128)(2,1)S(1)}, bf16[120,256]{1,0:T(8,128)(2,1)S(1)}, u32[]{:S(2)}, u32[]{:S(2)}) %collective-permute-start.5) | collective-permute-done | bytes 61472 | tf_op jit(solution)/shard_map/ppermute | solution.py:869
  60.5 0.6 copy-done.11
  61.1 7.1 %all-to-all-done = bf16[128,24,256]{2,1,0:T(8,128)(2,1)} async-done(((bf16[128,24,256]{2,1,0:T(8,128)(2,1)}), bf16[128,24,256]{2,1,0:T(8,128)(2,1)}, u32[]{:S(2)}, u32[]{:S(2)}) %all-to-all-start) | async-done | bytes 1572896 | tf_op jit(solution)/shard_map/all_to_all | solution.py:1023
  68.2 4.9 %coarse_forward.1.stats = f32[8,8,128]{2,1,0:T(8,128)} custom-call(s32[3]{0:T(128)S(1)} %pad_add_fusion.place, bf16[3072,256]{1,0:T(8,128)(2,1)} %bitcast.11.every), custom_call_target="tpu_custom_call" | custom-call | flops 1000000000 | bytes 2000000 | tf_op jit(solution)/shard_map/coarse_forward/pallas_call | solution.py:472
  73.1 3.5 %all-to-all-start.1 = ((f32[8,8,128]{2,1,0:T(8,128)}), f32[8,8,128]{2,1,0:T(8,128)S(1)}, u32[]{:S(2)}, u32[]{:S(2)}) async-start(f32[8,8,128]{2,1,0:T(8,128)} %coarse_forward.1.stats), calls=%async_computation.1 | async-start | bytes 65536 | tf_op jit(solution)/shard_map/all_to_all | solution.py:1039
  76.7 0.0 copy-done.5
  76.7 4.5 %coarse_own.1 = (bf16[576,256]{1,0:T(8,128)(2,1)}, bf16[384,128]{1,0:T(8,128)(2,1)}) custom-call(s32[3]{0:T(128)S(1)} %pad_add_fusion.place, bf16[3072,256]{1,0:T(8,128)(2,1)} %bitcast.11.every, f32[8,8,128]{2,1,0:T(8,128)} %coarse_forward.1.stats, bf16[2,96,384]{2,1,0:T(8,128)(2,1)S(1)} %copy-done.5), custom_call_target="tpu_custom_call" | custom-call | flops 1000000000 | bytes 2000000 | tf_op jit(solution)/shard_map/coarse_own/pallas_call | solution.py:529
  81.2 1.8 %all-to-all-done.1.stats = f32[8,8,128]{2,1,0:T(8,128)S(1)} async-done(((f32[8,8,128]{2,1,0:T(8,128)}), f32[8,8,128]{2,1,0:T(8,128)S(1)}, u32[]{:S(2)}, u32[]{:S(2)}) %all-to-all-start.1) | async-done | bytes 32800 | tf_op jit(solution)/shard_map/all_to_all | solution.py:1039
  82.9 11.0 %coarse_backward.1 = (bf16[768,256]{1,0:T(8,128)(2,1)}, bf16[1024,3072]{1,0:T(8,128)(2,1)S(1)}, bf16[3968,256]{1,0:T(8,128)(2,1)S(1)}) custom-call(s32[3]{0:T(128)S(1)} %pad_add_fusion.place, bf16[3072,256]{1,0:T(8,128)(2,1)} %bitcast.11.every, f32[8,8,128]{2,1,0:T(8,128)S(1)} %all-to-all-done.1.stats, bf16[2,96,384]{2,1,0:T(8,128)(2,1)S(1)} %copy-done.5, ...), custom_call_target="tpu_custom_call" | custom-call | flops 3000000000 | bytes 2000000 | tf_op jit(solution)/shard_map/coarse_backward/pallas_call | solution.py:623
  94.0 15.3 %all_to_all.20.terms_coarse = bf16[16,48,256]{2,1,0:T(8,128)(2,1)S(1)} all-to-all(bf16[16,48,256]{2,1,0:T(8,128)(2,1)} %bitcast.30), channel_id=1, replica_groups=mesh['row'=8,'col'=16] {'col'}, dimensions={0} | all-to-all | bytes 786432 | tf_op jit(solution)/shard_map/all_to_all | solution.py:1045
  109.2 0.0 copy-done.13
  109.3 12.5 %backward_kernel.1 = (bf16[384,256]{1,0:T(8,128)(2,1)}, bf16[128,16,128]{2,1,0:T(8,128)(2,1)S(1)}) custom-call(s32[3]{0:T(128)S(1)} %pad_add_fusion.place, bf16[16,48,256]{2,1,0:T(8,128)(2,1)S(1)} %all_to_all.20.terms_coarse, bf16[384,256]{1,0:T(8,128)(2,1)S(1)} %bitcast.19, bf16[24,1024]{1,0:T(8,128)(2,1)S(1)} %get-tuple-element.43.own_coarse, ...), custom_call_target="tpu_custom_call" | custom-call | flops 5000000000 | bytes 20000000 | tf_op jit(solution)/shard_map/backward_kernel/pallas_call | solution.py:817
  121.7 18.2 %all_to_all.21.terms = bf16[128,16,128]{2,1,0:T(8,128)(2,1)S(1)} all-to-all(bf16[128,16,128]{2,1,0:T(8,128)(2,1)S(1)} %get-tuple-element.66), channel_id=1, replica_groups=mesh['row'=8,'col'=16] {'row','col'}, dimensions={0} | all-to-all | bytes 1048576 | tf_op jit(solution)/shard_map/all_to_all | solution.py:1063
  140.0 1.0 sum_terms.1
  (14 shorter events, 0.0 us)
Async XLA Ops:
  0.6 19.2 %copy-start = (bf16[1024,1024]{1,0:T(8,128)(2,1)S(1)}, bf16[1024,1024]{1,0:T(8,128)(2,1)}, u32[]{:S(2)}) copy-start(bf16[1024,1024]{1,0:T(8,128)(2,1)} %param.22) | copy-start | bytes 6291460
  0.6 24.1 %copy-start.2 = (bf16[16,24,256]{2,1,0:T(8,128)(2,1)S(1)}, bf16[16,24,256]{2,1,0:T(8,128)(2,1)}, u32[]{:S(2)}) copy-start(bf16[16,24,256]{2,1,0:T(8,128)(2,1)} %param.13) | copy-start | bytes 589828
  0.7 24.1 %copy-start.4 = (bf16[256,256]{1,0:T(8,128)(2,1)S(1)}, bf16[256,256]{1,0:T(8,128)(2,1)}, u32[]{:S(2)}) copy-start(bf16[256,256]{1,0:T(8,128)(2,1)} %w_out.5) | copy-start | bytes 393220
  0.7 24.1 %copy-start.3 = (bf16[256,768]{1,0:T(8,128)(2,1)S(1)}, bf16[256,768]{1,0:T(8,128)(2,1)}, u32[]{:S(2)}) copy-start(bf16[256,768]{1,0:T(8,128)(2,1)} %w_qkv.5) | copy-start | bytes 1179652
  0.7 24.1 %copy-start.14 = (f32[1024]{0:T(1024)S(1)}, f32[1024]{0:T(1024)}, u32[]{:S(2)}) copy-start(f32[1024]{0:T(1024)} %param.20) | copy-start | bytes 12292
  0.7 24.1 %copy-start.15 = (f32[256]{0:T(256)S(1)}, f32[256]{0:T(256)}, u32[]{:S(2)}) copy-start(f32[256]{0:T(256)} %param.16) | copy-start | bytes 3076
  1.9 10.7 %collective-permute-start = (bf16[312,256]{1,0:T(8,128)(2,1)S(1)}, bf16[312,256]{1,0:T(8,128)(2,1)S(1)}, u32[]{:S(2)}, u32[]{:S(2)}) collective-permute-start(bf16[312,256]{1,0:T(8,128)(2,1)S(1)} %get-tuple-element.36), channel_id=1, source_target_pairs={{0,16},{16,32},{32,48},{48,64},{64,80},{80,96},{96,112},{112,0},{1... | collective-permute-start | bytes 479240 | tf_op jit(solution)/shard_map/ppermute | solution.py:868
  6.4 10.2 %collective-permute-start.1 = (bf16[312,256]{1,0:T(8,128)(2,1)S(1)}, bf16[312,256]{1,0:T(8,128)(2,1)S(1)}, u32[]{:S(2)}, u32[]{:S(2)}) collective-permute-start(bf16[312,256]{1,0:T(8,128)(2,1)S(1)} %get-tuple-element.37), channel_id=1, source_target_pairs={{0,112},{16,0},{32,16},{48,32},{64,48},{80,64},{96,80},{112,96},{1... | collective-permute-start | bytes 479240 | tf_op jit(solution)/shard_map/ppermute | solution.py:869
  18.2 3.9 %collective-permute-start.2 = (bf16[256,256]{1,0:T(8,128)(2,1)}, bf16[256,256]{1,0:T(8,128)(2,1)S(1)}, u32[]{:S(2)}, u32[]{:S(2)}) collective-permute-start(bf16[256,256]{1,0:T(8,128)(2,1)} %get-tuple-element.38), channel_id=1, source_target_pairs={{0,1},{1,2},{2,3},{3,4},{4,5},{5,6},{6,7},{7,8},{8,9},{9,10},{10,1... | collective-permute-start | bytes 393224 | tf_op jit(solution)/shard_map/ppermute | solution.py:868
  19.9 4.9 %collective-permute-start.3 = (bf16[256,256]{1,0:T(8,128)(2,1)}, bf16[256,256]{1,0:T(8,128)(2,1)S(1)}, u32[]{:S(2)}, u32[]{:S(2)}) collective-permute-start(bf16[256,256]{1,0:T(8,128)(2,1)} %get-tuple-element.39), channel_id=1, source_target_pairs={{0,15},{1,0},{2,1},{3,2},{4,3},{5,4},{6,5},{7,6},{8,7},{9,8},{10,9... | collective-permute-start | bytes 393224 | tf_op jit(solution)/shard_map/ppermute | solution.py:869
  34.2 0.7 copy-start.6
  34.9 8.9 %copy-start.1 = (bf16[16,24,256]{2,1,0:T(8,128)(2,1)S(1)}, bf16[16,24,256]{2,1,0:T(8,128)(2,1)}, u32[]{:S(2)}) copy-start(bf16[16,24,256]{2,1,0:T(8,128)(2,1)} %param.14) | copy-start | bytes 589828
  34.9 33.3 %all-to-all-start = ((bf16[128,24,256]{2,1,0:T(8,128)(2,1)}), bf16[128,24,256]{2,1,0:T(8,128)(2,1)}, u32[]{:S(2)}, u32[]{:S(2)}) async-start(bf16[128,24,256]{2,1,0:T(8,128)(2,1)} %bitcast.29), calls=%async_computation | async-start | bytes 3145728 | tf_op jit(solution)/shard_map/all_to_all | solution.py:1023
  43.8 12.4 %collective-permute-start.4 = (bf16[120,256]{1,0:T(8,128)(2,1)S(1)}, bf16[120,256]{1,0:T(8,128)(2,1)S(1)}, u32[]{:S(2)}, u32[]{:S(2)}) collective-permute-start(bf16[120,256]{1,0:T(8,128)(2,1)S(1)} %get-tuple-element.46), channel_id=1, source_target_pairs={{0,1},{1,2},{2,3},{3,4},{4,5},{5,6},{6,7},{7,8},{8,9},{9,10},{10,1... | collective-permute-start | bytes 184328 | tf_op jit(solution)/shard_map/ppermute | solution.py:868
  45.5 14.9 %collective-permute-start.5 = (bf16[120,256]{1,0:T(8,128)(2,1)S(1)}, bf16[120,256]{1,0:T(8,128)(2,1)S(1)}, u32[]{:S(2)}, u32[]{:S(2)}) collective-permute-start(bf16[120,256]{1,0:T(8,128)(2,1)S(1)} %get-tuple-element.47), channel_id=1, source_target_pairs={{0,15},{1,0},{2,1},{3,2},{4,3},{5,4},{6,5},{7,6},{8,7},{9,8},{10,9... | collective-permute-start | bytes 184328 | tf_op jit(solution)/shard_map/ppermute | solution.py:869
  45.6 0.9 copy-start.7
  56.2 20.4 %copy-start.5 = (bf16[2,96,384]{2,1,0:T(8,128)(2,1)S(1)}, bf16[2,96,384]{2,1,0:T(8,128)(2,1)}, u32[]{:S(2)}) copy-start(bf16[2,96,384]{2,1,0:T(8,128)(2,1)} %constant.19.clone.strips) | copy-start | bytes 442372
  56.2 0.6 copy-start.9
  60.5 0.6 copy-start.11
  73.1 9.8 %all-to-all-start.1 = ((f32[8,8,128]{2,1,0:T(8,128)}), f32[8,8,128]{2,1,0:T(8,128)S(1)}, u32[]{:S(2)}, u32[]{:S(2)}) async-start(f32[8,8,128]{2,1,0:T(8,128)} %coarse_forward.1.stats), calls=%async_computation.1 | async-start | bytes 65536 | tf_op jit(solution)/shard_map/all_to_all | solution.py:1039
  82.9 26.3 %copy-start.8 = (bf16[48,1024]{1,0:T(8,128)(2,1)S(1)}, bf16[48,1024]{1,0:T(8,128)(2,1)}, u32[]{:S(2)}) copy-start(bf16[48,1024]{1,0:T(8,128)(2,1)} %get-tuple-element.61.coarse) | copy-start | bytes 294916
  82.9 26.3 %copy-start.10 = (bf16[120,256]{1,0:T(8,128)(2,1)S(1)}, bf16[120,256]{1,0:T(8,128)(2,1)}, u32[]{:S(2)}) copy-start(bf16[120,256]{1,0:T(8,128)(2,1)} %copy-done.9) | copy-start | bytes 184324
  82.9 26.3 %copy-start.12 = (bf16[120,256]{1,0:T(8,128)(2,1)S(1)}, bf16[120,256]{1,0:T(8,128)(2,1)}, u32[]{:S(2)}) copy-start(bf16[120,256]{1,0:T(8,128)(2,1)} %copy-done.11) | copy-start | bytes 184324
  82.9 26.3 %copy-start.13 = (f32[8,512]{1,0:T(8,128)S(1)}, f32[8,512]{1,0:T(8,128)}, u32[]{:S(2)}) copy-start(f32[8,512]{1,0:T(8,128)} %get-tuple-element.62.lse) | copy-start | bytes 49156

commit v2 on v1

--- a/solution.py
+++ b/solution.py
@@ -147,8 +147,8 @@
     coarse_sems,
     packed_sems,
 ):
-    merge_copies = fetch(w_merge_far, w_merge, merge_sems, 4)
-    coarse_copies = fetch(w_coarse_far, w_coarse, coarse_sems, 2)
+    merge_copies = fetch(w_merge_far, w_merge, merge_sems, 2)
+    coarse_copies = fetch(w_coarse_far, w_coarse, coarse_sems, 4)
     for copy in merge_copies + coarse_copies:
         copy.start()
     row0 = place[0]
@@ -192,8 +192,9 @@
     wide = CCOLS + 2
     merge_rows(hid32, merged, CROWS)
     total = None
-    for n, copy in enumerate(merge_copies):
-        copy.wait()
+    for n in range(4):
+        if n % 2 == 0:
+            merge_copies[n // 2].wait()
         part = dot(merged[:, D1 * n : D1 * (n + 1)], w_merge[D1 * n : D1 * (n + 1)], 1, 0)
         total = part if total is None else total + part
     normed, _ = norm_forward(total.astype(BF16).astype(F32))
@@ -258,8 +259,8 @@
             pltpu.VMEM(w_merge.shape, BF16),
             pltpu.VMEM(w_coarse.shape, BF16),
             pltpu.VMEM((8, 2 * own, 256), BF16),
+            pltpu.SemaphoreType.DMA((2,)),
             pltpu.SemaphoreType.DMA((4,)),
-            pltpu.SemaphoreType.DMA((2,)),
             pltpu.SemaphoreType.DMA((4, 8)),
         ],
         compiler_params=vmem_params(48),
@@ -551,9 +552,13 @@
     tiles_far,
     coarse_far,
     stash_far,
+    merge_far,
+    pick_far,
     out,
     w_coarse,
     stash,
+    w_merge,
+    pick,
     dq_ref,
     dk_ref,
     dv_ref,
@@ -561,11 +566,15 @@
     sems,
 ):
     pairs = (
-        (tiles_far, tiles),
-        (coarse_far, w_coarse),
-        (stash_far, stash),
-    )
-    copies = [pltpu.make_async_copy(a, b, sems.at[n]) for n, (a, b) in enumerate(pairs)]
+        (tiles_far, tiles, 1),
+        (coarse_far, w_coarse, 2),
+        (stash_far, stash, 1),
+        (merge_far, w_merge, 2),
+        (pick_far, pick, 1),
+    )
+    copies = []
+    for n, (source, target, pieces) in enumerate(pairs):
+        copies += fetch(source, target, sems.at[n], pieces)
     for copy in copies:
         copy.start()
     row = place[2]
@@ -624,16 +633,16 @@
         coarse_backward,
         out_shape=[pltpu.HBM((H1 * EXT, 256), BF16)]
         + [pltpu.VMEM(array.shape, array.dtype) for array in later],
-        in_specs=[pl.BlockSpec(memory_space=pltpu.SMEM)] + [whole()] * 5 + [far()] * 3,
-        out_specs=[whole()] * 3,
+        in_specs=[pl.BlockSpec(memory_space=pltpu.SMEM)] + [whole()] * 5 + [far()] * 5,
+        out_specs=[whole()] * 5,
         scratch_shapes=[
             pltpu.VMEM((2 * STRIP, 128), F32),
             pltpu.VMEM((EDGE, 128), F32),
             pltpu.VMEM((EDGE, 128), F32),
             pltpu.VMEM(tiles.shape, BF16),
-            pltpu.SemaphoreType.DMA((3,)),
+            pltpu.SemaphoreType.DMA((5, 4)),
         ],
-        compiler_params=vmem_params(24),
+        compiler_params=vmem_params(16),
         cost_estimate=pl.CostEstimate(flops=3 * 10**9, bytes_accessed=2 * 10**6, transcendentals=4 * 10**6),
         name="coarse_backward",
     )(
@@ -682,8 +691,8 @@
     w_out,
     w_coarse,
     stash,
-    pick_far,
-    w_merge_far,
+    pick_block,
+    w_merge,
     grad_tokens,
     terms,
     grad_fine,
@@ -694,17 +703,9 @@
     dk_ref,
     dv_ref,
     gt_ref,
-    pick_block,
-    w_merge,
     stack_ref,
     probs_ref,
-    merge_sems,
-    pick_sem,
 ):
-    merge_copies = fetch(w_merge_far, w_merge, merge_sems, 4)
-    pick_copy = pltpu.make_async_copy(pick_far, pick_block, pick_sem)
-    for copy in merge_copies + [pick_copy]:
-        copy.start()
     queries = stash.at[pl.ds(AT_Q, N4)]
     attended = stash.at[pl.ds(AT_ATT, N4)]
     keys_w = stash.at[pl.ds(AT_K, WROWS * C4)]
@@ -736,8 +737,7 @@
     normed, inverse = norm_forward(coarse[...].astype(F32))
     back = norm_backward(upstream, normed, inverse)
     change = (grad_coarse + back).astype(BF16)
-    for a, copy in enumerate(merge_copies):
-        copy.wait()
+    for a in range(MERGE):
         sp32[a] = dot(change, w_merge[D1 * a : D1 * (a + 1)], 1, 1)
     window = window_bias(C4, -3)
     for b in range(BLOCKS):
@@ -794,7 +794,6 @@
     inner = slice(BLOCK, BLOCK + OWN)
     att = jnp.where(in_tile, attended[inner].astype(F32), 0.0).astype(BF16)
     term_out = dot(att, gh_ref[inner], 0, 0).astype(BF16)
-    pick_copy.wait()
     both = dot(jnp.concatenate([term_qkv, term_out], axis=1), pick_block[...], 1, 0)
     low = lax.broadcasted_iota(jnp.int32, (16, 128), 1) < 64
     for r in range(8):
@@ -817,7 +816,7 @@
     return pl.pallas_call(
         backward_kernel,
         out_shape=[jax.ShapeDtypeStruct(s, d) for s, d in shapes],
-        in_specs=[pl.BlockSpec(memory_space=pltpu.SMEM)] + [whole()] * 15 + [far()] * 2,
+        in_specs=[pl.BlockSpec(memory_space=pltpu.SMEM)] + [whole()] * 17,
         out_specs=[whole()] * 2,
         scratch_shapes=[
             pltpu.VMEM((N4, D0), F32),
@@ -828,17 +827,13 @@
             pltpu.VMEM((WROWS * C4, D0), F32),
             pltpu.VMEM((WROWS * C4, D0), F32),
             pltpu.VMEM((OWN, D0), F32),
-            pltpu.VMEM((4 * D0, 4 * D0), BF16),
-            pltpu.VMEM((MERGE * MERGE * D0, D1), BF16),
             pltpu.VMEM((BLOCKS, H0 * BLOCK, D0), BF16),
             pltpu.VMEM((BLOCKS, 10 * C4, H0 * BLOCK), F32),
-            pltpu.SemaphoreType.DMA((4,)),
-            pltpu.SemaphoreType.DMA(()),
         ],
-        compiler_params=vmem_params(40),
+        compiler_params=vmem_params(20),
         cost_estimate=pl.CostEstimate(flops=5 * 10**9, bytes_accessed=2 * 10**7, transcendentals=10**6),
         name="backward_kernel",
-    )(place, *operands[:-2], *[in_hbm(operand) for operand in operands[-2:]])
+    )(place, *operands)
 
 
 def sum_terms(terms, out_qkv, out_out):
@@ -1038,8 +1033,9 @@
     own_stats = run_coarse_forward(place, every)
     stats = lax.all_to_all(own_stats, "row", split_axis=0, concat_axis=0, tiled=True)
     edge, dq_own = run_coarse_own(place, every, own_stats, strips)
-    tiles, near_coarse, stash = run_coarse_backward(
-        place, every, stats, strips, edge, dq_own, coarse_qkv, stash
+    pick = jnp.asarray(block_pick(), BF16)
+    tiles, near_coarse, stash, near_merge, pick = run_coarse_backward(
+        place, every, stats, strips, edge, dq_own, coarse_qkv, stash, merge_weight, pick
     )
     tiles = tiles.reshape(H1, EXT, 256)
     terms = lax.all_to_all(tiles, "col", split_axis=0, concat_axis=0, tiled=True)
@@ -1057,8 +1053,8 @@
         fine_out,
         near_coarse,
         stash,
-        jnp.asarray(block_pick(), BF16),
-        merge_weight,
+        pick,
+        near_merge,
     )
     blocks = lax.all_to_all(blocks, ("row", "col"), split_axis=0, concat_axis=0, tiled=True)
     grad_qkv, grad_out = run_sum_terms(blocks)

time: 141 us -> 138 us (0.979)
  Pallas kernels: 55.9 us -> 52.5 us
    pallas_call x1, Pallas kernels: 11 us -> 9.29 us  [run_coarse_backward(): pl.pallas_call(coarse_backward, out_shape=[pltpu.HBM((H1 * EXT, 256), BF1...]
where the time goes in v2:
time: 138 us; the launch traced here: 137 us
  Pallas kernels  52.5 us (38%)
  blocking collectives  33.5 us (24%)
  waiting for transfers between devices  24.5 us (18%)
  starting transfers between devices  22.6 us (16%)
  local copies, waits for them, and re-layouts  2.84 us (2%)
    all_to_all x1, blocking collectives, on_device(): lax.all_to_all(blocks, ('row', 'col'), split_axis=0, concat_axis=0, tiled...  18.2 us
    all_to_all x1, blocking collectives, on_device(): lax.all_to_all(tiles, 'col', split_axis=0, concat_axis=0, tiled=True)  15.3 us
    pallas_call x1, Pallas kernels, run_backward(): pl.pallas_call(backward_kernel, out_shape=[jax.ShapeDtypeStruct(s, d) for...  11.2 us
    ppermute x3, waiting for transfers between devices, swap_edges(): after = lax.ppermute(first, axis, ring(axis, -1))  10.2 us
    pallas_call x1, Pallas kernels, run_wide(): pl.pallas_call(wide_kernel, out_shape=[pltpu.HBM((STASH, D0), BF16), pltp...  9.76 us
    pallas_call x1, Pallas kernels, run_coarse_backward(): pl.pallas_call(coarse_backward, out_shape=[pltpu.HBM((H1 * EXT, 256), BF1...  9.29 us
    pallas_call x1, Pallas kernels, run_near(): pl.pallas_call(near_kernel, out_shape=pltpu.HBM((8, 8, 2 * own, 256), BF1...  9 us
    all_to_all x1, starting transfers between devices, on_device(): lax.all_to_all(packed.reshape(8 * H1, CROWS * CCOLS, 256), ('row', 'col')...  8.87 us
  transfers between devices with their start and end apart: 8, of which 7 were waited for; matrix products, arithmetic and copies ran while one was open for 1% of the time, Pallas kernels for 10%

profile of v2, /device:TPU:1, one launch (start us, length us, event | category | flops | bytes accessed | tf_op | source)
XLA Modules:
  0.0 137.5 jit_solution(9178380300554760827)
XLA Ops:
  0.6 0.0 copy-start
  0.6 0.0 copy-start.2
  0.7 0.0 copy-start.4
  0.7 0.0 copy-start.3
  0.7 0.0 copy-start.14
  0.7 0.0 copy-start.15
  0.7 1.2 row_strips.1
  1.9 4.5 %collective-permute-start = (bf16[312,256]{1,0:T(8,128)(2,1)S(1)}, bf16[312,256]{1,0:T(8,128)(2,1)S(1)}, u32[]{:S(2)}, u32[]{:S(2)}) collective-permute-start(bf16[312,256]{1,0:T(8,128)(2,1)S(1)} %get-tuple-element.38), channel_id=1, source_target_pairs={{0,16},{16,32},{32,48},{48,64},{64,80},{80,96},{96,112},{112,0},{1... | collective-permute-start | bytes 479240 | tf_op jit(solution)/shard_map/ppermute | solution.py:863
  6.4 2.3 %collective-permute-start.1 = (bf16[312,256]{1,0:T(8,128)(2,1)S(1)}, bf16[312,256]{1,0:T(8,128)(2,1)S(1)}, u32[]{:S(2)}, u32[]{:S(2)}) collective-permute-start(bf16[312,256]{1,0:T(8,128)(2,1)S(1)} %get-tuple-element.39), channel_id=1, source_target_pairs={{0,112},{16,0},{32,16},{48,32},{64,48},{80,64},{96,80},{112,96},{1... | collective-permute-start | bytes 479240 | tf_op jit(solution)/shard_map/ppermute | solution.py:864
  8.6 3.9 %collective-permute-done.above = bf16[312,256]{1,0:T(8,128)(2,1)S(1)} collective-permute-done((bf16[312,256]{1,0:T(8,128)(2,1)S(1)}, bf16[312,256]{1,0:T(8,128)(2,1)S(1)}, u32[]{:S(2)}, u32[]{:S(2)}) %collective-permute-start) | collective-permute-done | bytes 159776 | tf_op jit(solution)/shard_map/ppermute | solution.py:863
  12.6 4.0 %collective-permute-done.1.below = bf16[312,256]{1,0:T(8,128)(2,1)S(1)} collective-permute-done((bf16[312,256]{1,0:T(8,128)(2,1)S(1)}, bf16[312,256]{1,0:T(8,128)(2,1)S(1)}, u32[]{:S(2)}, u32[]{:S(2)}) %collective-permute-start.1) | collective-permute-done | bytes 159776 | tf_op jit(solution)/shard_map/ppermute | solution.py:864
  16.6 1.6 %column_strips.1 = (bf16[256,256]{1,0:T(8,128)(2,1)}, bf16[256,256]{1,0:T(8,128)(2,1)}) custom-call(bf16[384,256]{1,0:T(8,128)(2,1)} %bitcast.21, bf16[312,256]{1,0:T(8,128)(2,1)S(1)} %collective-permute-done.above, bf16[312,256]{1,0:T(8,128)(2,1)S(1)} %collective-permute-done.1.below), custom_call_target="tpu_custom_call" | custom-call | tf_op jit(solution)/shard_map/column_strips/pallas_call | solution.py:936
  18.2 1.7 %collective-permute-start.2 = (bf16[256,256]{1,0:T(8,128)(2,1)}, bf16[256,256]{1,0:T(8,128)(2,1)S(1)}, u32[]{:S(2)}, u32[]{:S(2)}) collective-permute-start(bf16[256,256]{1,0:T(8,128)(2,1)} %get-tuple-element.40), channel_id=1, source_target_pairs={{0,1},{1,2},{2,3},{3,4},{4,5},{5,6},{6,7},{7,8},{8,9},{9,10},{10,1... | collective-permute-start | bytes 393224 | tf_op jit(solution)/shard_map/ppermute | solution.py:863
  19.9 0.0 collective-permute-start.3
  19.9 0.0 copy-done
  19.9 0.7 convolution_convert_fusion.grads
  20.5 0.1 pad_add_fusion.place
  20.6 1.5 %collective-permute-done.2.left = bf16[256,256]{1,0:T(8,128)(2,1)S(1)} collective-permute-done((bf16[256,256]{1,0:T(8,128)(2,1)}, bf16[256,256]{1,0:T(8,128)(2,1)S(1)}, u32[]{:S(2)}, u32[]{:S(2)}) %collective-permute-start.2) | collective-permute-done | bytes 131104 | tf_op jit(solution)/shard_map/ppermute | solution.py:863
  22.1 2.6 %collective-permute-done.3.right = bf16[256,256]{1,0:T(8,128)(2,1)S(1)} collective-permute-done((bf16[256,256]{1,0:T(8,128)(2,1)}, bf16[256,256]{1,0:T(8,128)(2,1)S(1)}, u32[]{:S(2)}, u32[]{:S(2)}) %collective-permute-start.3) | collective-permute-done | bytes 131104 | tf_op jit(solution)/shard_map/ppermute | solution.py:864
  24.8 0.0 copy-done.2
  24.8 0.0 copy-done.4
  24.8 0.0 copy-done.3
  24.8 0.0 copy-done.14
  24.8 0.0 copy-done.15
  24.8 9.0 %near_kernel.1 = bf16[8,8,48,256]{3,2,1,0:T(8,128)(2,1)} custom-call(s32[3]{0:T(128)S(1)} %pad_add_fusion.place, bf16[384,256]{1,0:T(8,128)(2,1)S(1)} %bitcast.22, bf16[312,256]{1,0:T(8,128)(2,1)S(1)} %collective-permute-done.above, bf16[312,256]{1,0:T(8,128)(2,1)S(1)} %collective-permute-done.1.below, bf16[256,256]{1,0:T(8,128)(2,1)S(1)} %collective-permute-done.2.left, ...), custom_call_target="tpu_custom_call" | custom-call | flops 3000000000 | bytes 20000000 | tf_op jit(solution)/shard_map/near_kernel/pallas_call | solution.py:246
  33.8 0.0 copy-start.6
  33.8 0.6 copy-done.6
  34.5 8.9 %all-to-all-start = ((bf16[128,24,256]{2,1,0:T(8,128)(2,1)}), bf16[128,24,256]{2,1,0:T(8,128)(2,1)}, u32[]{:S(2)}, u32[]{:S(2)}) async-start(bf16[128,24,256]{2,1,0:T(8,128)(2,1)} %bitcast.29), calls=%async_computation | async-start | bytes 3145728 | tf_op jit(solution)/shard_map/all_to_all | solution.py:1018
  43.3 0.1 grad_strips.1
  43.4 1.7 %collective-permute-start.4 = (bf16[120,256]{1,0:T(8,128)(2,1)S(1)}, bf16[120,256]{1,0:T(8,128)(2,1)S(1)}, u32[]{:S(2)}, u32[]{:S(2)}) collective-permute-start(bf16[120,256]{1,0:T(8,128)(2,1)S(1)} %get-tuple-element.48), channel_id=1, source_target_pairs={{0,1},{1,2},{2,3},{3,4},{4,5},{5,6},{6,7},{7,8},{8,9},{9,10},{10,1... | collective-permute-start | bytes 184328 | tf_op jit(solution)/shard_map/ppermute | solution.py:863
  45.1 0.0 collective-permute-start.5
  45.1 0.9 copy-done.7
  46.0 9.8 %wide_kernel.1 = (bf16[3968,256]{1,0:T(8,128)(2,1)}, f32[8,512]{1,0:T(8,128)}, bf16[48,1024]{1,0:T(8,128)(2,1)}) custom-call(s32[3]{0:T(128)S(1)} %pad_add_fusion.place, bf16[384,256]{1,0:T(8,128)(2,1)S(1)} %bitcast.23, bf16[312,256]{1,0:T(8,128)(2,1)S(1)} %collective-permute-done.above, bf16[312,256]{1,0:T(8,128)(2,1)S(1)} %collective-permute-done.1.below, ...), custom_call_target="tpu_custom_call" | custom-call | flops 3000000000 | bytes 10000000 | tf_op jit(solution)/shard_map/wide_kernel/pallas_call | solution.py:383
  55.8 0.0 copy-start.5
  55.8 0.0 collective-permute-done.4.grads_left
  55.8 0.6 copy-done.9
  56.4 3.6 %collective-permute-done.5.grads_right = bf16[120,256]{1,0:T(8,128)(2,1)S(1)} collective-permute-done((bf16[120,256]{1,0:T(8,128)(2,1)S(1)}, bf16[120,256]{1,0:T(8,128)(2,1)S(1)}, u32[]{:S(2)}, u32[]{:S(2)}) %collective-permute-start.5) | collective-permute-done | bytes 61472 | tf_op jit(solution)/shard_map/ppermute | solution.py:864
  60.0 0.6 copy-done.11
  60.6 7.1 %all-to-all-done = bf16[128,24,256]{2,1,0:T(8,128)(2,1)} async-done(((bf16[128,24,256]{2,1,0:T(8,128)(2,1)}), bf16[128,24,256]{2,1,0:T(8,128)(2,1)}, u32[]{:S(2)}, u32[]{:S(2)}) %all-to-all-start) | async-done | bytes 1572896 | tf_op jit(solution)/shard_map/all_to_all | solution.py:1018
  67.7 4.9 %coarse_forward.1.stats = f32[8,8,128]{2,1,0:T(8,128)} custom-call(s32[3]{0:T(128)S(1)} %pad_add_fusion.place, bf16[3072,256]{1,0:T(8,128)(2,1)} %bitcast.11.every), custom_call_target="tpu_custom_call" | custom-call | flops 1000000000 | bytes 2000000 | tf_op jit(solution)/shard_map/coarse_forward/pallas_call | solution.py:473
  72.7 3.5 %all-to-all-start.1 = ((f32[8,8,128]{2,1,0:T(8,128)}), f32[8,8,128]{2,1,0:T(8,128)S(1)}, u32[]{:S(2)}, u32[]{:S(2)}) async-start(f32[8,8,128]{2,1,0:T(8,128)} %coarse_forward.1.stats), calls=%async_computation.1 | async-start | bytes 65536 | tf_op jit(solution)/shard_map/all_to_all | solution.py:1034
  76.2 4.5 %coarse_own.1 = (bf16[576,256]{1,0:T(8,128)(2,1)}, bf16[384,128]{1,0:T(8,128)(2,1)}) custom-call(s32[3]{0:T(128)S(1)} %pad_add_fusion.place, bf16[3072,256]{1,0:T(8,128)(2,1)} %bitcast.11.every, f32[8,8,128]{2,1,0:T(8,128)} %coarse_forward.1.stats, bf16[2,96,384]{2,1,0:T(8,128)(2,1)S(1)} %copy-done.5), custom_call_target="tpu_custom_call" | custom-call | flops 1000000000 | bytes 2000000 | tf_op jit(solution)/shard_map/coarse_own/pallas_call | solution.py:530
  80.8 1.8 %all-to-all-done.1.stats = f32[8,8,128]{2,1,0:T(8,128)S(1)} async-done(((f32[8,8,128]{2,1,0:T(8,128)}), f32[8,8,128]{2,1,0:T(8,128)S(1)}, u32[]{:S(2)}, u32[]{:S(2)}) %all-to-all-start.1) | async-done | bytes 32800 | tf_op jit(solution)/shard_map/all_to_all | solution.py:1034
  82.5 9.3 %coarse_backward.1 = (bf16[768,256]{1,0:T(8,128)(2,1)}, bf16[1024,3072]{1,0:T(8,128)(2,1)S(1)}, bf16[3968,256]{1,0:T(8,128)(2,1)S(1)}, bf16[4096,1024]{1,0:T(8,128)(2,1)S(1)}, bf16[1024,1024]{1,0:T(8,128)(2,1)S(1)}) custom-call(s32[3]{0:T(128)S(1)} %pad_add_fusion.place, bf16[3072,256]{1,0:T(8,128)(2,1)} %bitcast.11.every, ...), custom_call_target="tpu_custom_call" | custom-call | flops 3000000000 | bytes 2000000 | tf_op jit(solution)/shard_map/coarse_backward/pallas_call | solution.py:632
  91.8 15.3 %all_to_all.20.terms_coarse = bf16[16,48,256]{2,1,0:T(8,128)(2,1)S(1)} all-to-all(bf16[16,48,256]{2,1,0:T(8,128)(2,1)} %bitcast.30), channel_id=1, replica_groups=mesh['row'=8,'col'=16] {'col'}, dimensions={0} | all-to-all | bytes 786432 | tf_op jit(solution)/shard_map/all_to_all | solution.py:1041
  107.1 11.2 %backward_kernel.1 = (bf16[384,256]{1,0:T(8,128)(2,1)}, bf16[128,16,128]{2,1,0:T(8,128)(2,1)S(1)}) custom-call(s32[3]{0:T(128)S(1)} %pad_add_fusion.place, bf16[16,48,256]{2,1,0:T(8,128)(2,1)S(1)} %all_to_all.20.terms_coarse, bf16[384,256]{1,0:T(8,128)(2,1)S(1)} %bitcast.19, bf16[24,1024]{1,0:T(8,128)(2,1)S(1)} %get-tuple-element.45.own_coarse, ...), custom_call_target="tpu_custom_call" | custom-call | flops 5000000000 | bytes 20000000 | tf_op jit(solution)/shard_map/backward_kernel/pallas_call | solution.py:816
  118.3 18.2 %all_to_all.21.terms = bf16[128,16,128]{2,1,0:T(8,128)(2,1)S(1)} all-to-all(bf16[128,16,128]{2,1,0:T(8,128)(2,1)S(1)} %get-tuple-element.70), channel_id=1, replica_groups=mesh['row'=8,'col'=16] {'row','col'}, dimensions={0} | all-to-all | bytes 1048576 | tf_op jit(solution)/shard_map/all_to_all | solution.py:1059
  136.5 1.0 sum_terms.1
  (14 shorter events, 0.0 us)
Async XLA Ops:
  0.6 19.2 %copy-start = (bf16[1024,1024]{1,0:T(8,128)(2,1)S(1)}, bf16[1024,1024]{1,0:T(8,128)(2,1)}, u32[]{:S(2)}) copy-start(bf16[1024,1024]{1,0:T(8,128)(2,1)} %param.22) | copy-start | bytes 6291460
  0.6 24.1 %copy-start.2 = (bf16[16,24,256]{2,1,0:T(8,128)(2,1)S(1)}, bf16[16,24,256]{2,1,0:T(8,128)(2,1)}, u32[]{:S(2)}) copy-start(bf16[16,24,256]{2,1,0:T(8,128)(2,1)} %param.13) | copy-start | bytes 589828
  0.7 24.1 %copy-start.4 = (bf16[256,256]{1,0:T(8,128)(2,1)S(1)}, bf16[256,256]{1,0:T(8,128)(2,1)}, u32[]{:S(2)}) copy-start(bf16[256,256]{1,0:T(8,128)(2,1)} %w_out.5) | copy-start | bytes 393220
  0.7 24.1 %copy-start.3 = (bf16[256,768]{1,0:T(8,128)(2,1)S(1)}, bf16[256,768]{1,0:T(8,128)(2,1)}, u32[]{:S(2)}) copy-start(bf16[256,768]{1,0:T(8,128)(2,1)} %w_qkv.5) | copy-start | bytes 1179652
  0.7 24.1 %copy-start.14 = (f32[1024]{0:T(1024)S(1)}, f32[1024]{0:T(1024)}, u32[]{:S(2)}) copy-start(f32[1024]{0:T(1024)} %param.20) | copy-start | bytes 12292
  0.7 24.1 %copy-start.15 = (f32[256]{0:T(256)S(1)}, f32[256]{0:T(256)}, u32[]{:S(2)}) copy-start(f32[256]{0:T(256)} %param.16) | copy-start | bytes 3076
  1.9 10.7 %collective-permute-start = (bf16[312,256]{1,0:T(8,128)(2,1)S(1)}, bf16[312,256]{1,0:T(8,128)(2,1)S(1)}, u32[]{:S(2)}, u32[]{:S(2)}) collective-permute-start(bf16[312,256]{1,0:T(8,128)(2,1)S(1)} %get-tuple-element.38), channel_id=1, source_target_pairs={{0,16},{16,32},{32,48},{48,64},{64,80},{80,96},{96,112},{112,0},{1... | collective-permute-start | bytes 479240 | tf_op jit(solution)/shard_map/ppermute | solution.py:863
  6.4 10.2 %collective-permute-start.1 = (bf16[312,256]{1,0:T(8,128)(2,1)S(1)}, bf16[312,256]{1,0:T(8,128)(2,1)S(1)}, u32[]{:S(2)}, u32[]{:S(2)}) collective-permute-start(bf16[312,256]{1,0:T(8,128)(2,1)S(1)} %get-tuple-element.39), channel_id=1, source_target_pairs={{0,112},{16,0},{32,16},{48,32},{64,48},{80,64},{96,80},{112,96},{1... | collective-permute-start | bytes 479240 | tf_op jit(solution)/shard_map/ppermute | solution.py:864
  18.2 3.9 %collective-permute-start.2 = (bf16[256,256]{1,0:T(8,128)(2,1)}, bf16[256,256]{1,0:T(8,128)(2,1)S(1)}, u32[]{:S(2)}, u32[]{:S(2)}) collective-permute-start(bf16[256,256]{1,0:T(8,128)(2,1)} %get-tuple-element.40), channel_id=1, source_target_pairs={{0,1},{1,2},{2,3},{3,4},{4,5},{5,6},{6,7},{7,8},{8,9},{9,10},{10,1... | collective-permute-start | bytes 393224 | tf_op jit(solution)/shard_map/ppermute | solution.py:863
  19.9 4.9 %collective-permute-start.3 = (bf16[256,256]{1,0:T(8,128)(2,1)}, bf16[256,256]{1,0:T(8,128)(2,1)S(1)}, u32[]{:S(2)}, u32[]{:S(2)}) collective-permute-start(bf16[256,256]{1,0:T(8,128)(2,1)} %get-tuple-element.41), channel_id=1, source_target_pairs={{0,15},{1,0},{2,1},{3,2},{4,3},{5,4},{6,5},{7,6},{8,7},{9,8},{10,9... | collective-permute-start | bytes 393224 | tf_op jit(solution)/shard_map/ppermute | solution.py:864
  33.8 0.7 copy-start.6
  34.5 8.9 %copy-start.1 = (bf16[16,24,256]{2,1,0:T(8,128)(2,1)S(1)}, bf16[16,24,256]{2,1,0:T(8,128)(2,1)}, u32[]{:S(2)}) copy-start(bf16[16,24,256]{2,1,0:T(8,128)(2,1)} %param.14) | copy-start | bytes 589828
  34.5 33.3 %all-to-all-start = ((bf16[128,24,256]{2,1,0:T(8,128)(2,1)}), bf16[128,24,256]{2,1,0:T(8,128)(2,1)}, u32[]{:S(2)}, u32[]{:S(2)}) async-start(bf16[128,24,256]{2,1,0:T(8,128)(2,1)} %bitcast.29), calls=%async_computation | async-start | bytes 3145728 | tf_op jit(solution)/shard_map/all_to_all | solution.py:1018
  43.4 12.4 %collective-permute-start.4 = (bf16[120,256]{1,0:T(8,128)(2,1)S(1)}, bf16[120,256]{1,0:T(8,128)(2,1)S(1)}, u32[]{:S(2)}, u32[]{:S(2)}) collective-permute-start(bf16[120,256]{1,0:T(8,128)(2,1)S(1)} %get-tuple-element.48), channel_id=1, source_target_pairs={{0,1},{1,2},{2,3},{3,4},{4,5},{5,6},{6,7},{7,8},{8,9},{9,10},{10,1... | collective-permute-start | bytes 184328 | tf_op jit(solution)/shard_map/ppermute | solution.py:863
  45.1 14.9 %collective-permute-start.5 = (bf16[120,256]{1,0:T(8,128)(2,1)S(1)}, bf16[120,256]{1,0:T(8,128)(2,1)S(1)}, u32[]{:S(2)}, u32[]{:S(2)}) collective-permute-start(bf16[120,256]{1,0:T(8,128)(2,1)S(1)} %get-tuple-element.49), channel_id=1, source_target_pairs={{0,15},{1,0},{2,1},{3,2},{4,3},{5,4},{6,5},{7,6},{8,7},{9,8},{10,9... | collective-permute-start | bytes 184328 | tf_op jit(solution)/shard_map/ppermute | solution.py:864
  45.1 0.9 copy-start.7
  55.8 20.4 %copy-start.5 = (bf16[2,96,384]{2,1,0:T(8,128)(2,1)S(1)}, bf16[2,96,384]{2,1,0:T(8,128)(2,1)}, u32[]{:S(2)}) copy-start(bf16[2,96,384]{2,1,0:T(8,128)(2,1)} %constant.19.clone.strips) | copy-start | bytes 442372
  55.8 0.6 copy-start.9
  60.0 0.6 copy-start.11
  72.7 9.8 %all-to-all-start.1 = ((f32[8,8,128]{2,1,0:T(8,128)}), f32[8,8,128]{2,1,0:T(8,128)S(1)}, u32[]{:S(2)}, u32[]{:S(2)}) async-start(f32[8,8,128]{2,1,0:T(8,128)} %coarse_forward.1.stats), calls=%async_computation.1 | async-start | bytes 65536 | tf_op jit(solution)/shard_map/all_to_all | solution.py:1034
  82.5 24.6 %copy-start.8 = (bf16[48,1024]{1,0:T(8,128)(2,1)S(1)}, bf16[48,1024]{1,0:T(8,128)(2,1)}, u32[]{:S(2)}) copy-start(bf16[48,1024]{1,0:T(8,128)(2,1)} %get-tuple-element.63.coarse) | copy-start | bytes 294916
  82.5 24.6 %copy-start.10 = (bf16[120,256]{1,0:T(8,128)(2,1)S(1)}, bf16[120,256]{1,0:T(8,128)(2,1)}, u32[]{:S(2)}) copy-start(bf16[120,256]{1,0:T(8,128)(2,1)} %copy-done.9) | copy-start | bytes 184324
  82.5 24.6 %copy-start.12 = (bf16[120,256]{1,0:T(8,128)(2,1)S(1)}, bf16[120,256]{1,0:T(8,128)(2,1)}, u32[]{:S(2)}) copy-start(bf16[120,256]{1,0:T(8,128)(2,1)} %copy-done.11) | copy-start | bytes 184324
  82.5 24.6 %copy-start.13 = (f32[8,512]{1,0:T(8,128)S(1)}, f32[8,512]{1,0:T(8,128)}, u32[]{:S(2)}) copy-start(f32[8,512]{1,0:T(8,128)} %get-tuple-element.64.lse) | copy-start | bytes 49156

commit v3 on v2

--- a/solution.py
+++ b/solution.py
@@ -919,28 +919,48 @@
     )(*[in_hbm(operand) for operand in operands])
 
 
-def column_strips(tokens, above, below, first, last):
-    parts = [part[:TOKEN_ROWS].astype(F32) for part in (above, below)]
-    parts.insert(1, tokens[...].astype(F32))
-    left = []
-    right = []
-    for part in parts:
-        for i in range(part.shape[0] // COLS):
-            left.append(part[COLS * i : COLS * i + HALO])
-            right.append(part[COLS * (i + 1) - HALO : COLS * (i + 1)])
-    first[...] = jnp.concatenate(left, axis=0).astype(BF16)
-    last[...] = jnp.concatenate(right, axis=0).astype(BF16)
-
-
-def run_column_strips(tokens, above, below):
+def own_columns(tokens, first, last):
+    wide = tokens[...].astype(F32)
+    rows = [wide[COLS * i : COLS * (i + 1)] for i in range(ROWS)]
+    first[...] = jnp.concatenate([row[:HALO] for row in rows], axis=0).astype(BF16)
+    last[...] = jnp.concatenate([row[-HALO:] for row in rows], axis=0).astype(BF16)
+
+
+def run_own_columns(tokens):
+    return pl.pallas_call(
+        own_columns,
+        out_shape=[jax.ShapeDtypeStruct((ROWS * HALO, D0), BF16)] * 2,
+        in_specs=[whole()],
+        out_specs=[whole()] * 2,
+        compiler_params=vmem_params(8),
+        name="own_columns",
+    )(in_hbm(tokens.reshape(-1, D0)))
+
+
+def column_strips(own_first, own_last, above, below, first, last):
+    upper, lower = [part[:TOKEN_ROWS].astype(F32) for part in (above, below)]
+    upper, lower = [
+        [part[COLS * i : COLS * (i + 1)] for i in range(HALO)] for part in (upper, lower)
+    ]
+    for out, own, at in (
+        (first, own_first, slice(0, HALO)),
+        (last, own_last, slice(COLS - HALO, COLS)),
+    ):
+        rows = HALO * HALO
+        out[:rows] = jnp.concatenate([row[at] for row in upper], axis=0).astype(BF16)
+        out[rows:-rows] = own[...]
+        out[-rows:] = jnp.concatenate([row[at] for row in lower], axis=0).astype(BF16)
+
+
+def run_column_strips(own_first, own_last, above, below):
     return pl.pallas_call(
         column_strips,
         out_shape=[jax.ShapeDtypeStruct((R8 * HALO, D0), BF16)] * 2,
-        in_specs=[whole()] * 3,
+        in_specs=[whole()] * 4,
         out_specs=[whole()] * 2,
         compiler_params=vmem_params(8),
         name="column_strips",
-    )(in_hbm(tokens.reshape(-1, D0)), above, below)
+    )(own_first, own_last, above, below)
 
 
 def grads_of(own_fine, own_coarse, above, below):
@@ -998,7 +1018,8 @@
     place = jnp.stack([row * ROWS, col * COLS, row]).astype(jnp.int32)
     first, last, grad_coarse = run_row_strips(tokens, grad_fine, grad_coarse)
     above, below = swap_edges(first, last, "row")
-    left, right = swap_edges(*run_column_strips(tokens, above, below), "col")
+    columns = run_own_columns(tokens)
+    left, right = swap_edges(*run_column_strips(*columns, above, below), "col")
     pieces = (tokens, above, below, left, right)
     grad_heads = jnp.dot(grad_coarse, coarse_out.T, preferred_element_type=F32).astype(BF16)
     packed = run_near(
@@ -1029,13 +1050,13 @@
         (every, left, right, stash, lse, coarse)
     )
     every = every.reshape(SLAB * SLABS, 256)
-    strips = jnp.asarray(strip_pick(), BF16)
+    edges = jnp.asarray(strip_pick(), BF16)
     own_stats = run_coarse_forward(place, every)
     stats = lax.all_to_all(own_stats, "row", split_axis=0, concat_axis=0, tiled=True)
-    edge, dq_own = run_coarse_own(place, every, own_stats, strips)
+    edge, dq_own = run_coarse_own(place, every, own_stats, edges)
     pick = jnp.asarray(block_pick(), BF16)
     tiles, near_coarse, stash, near_merge, pick = run_coarse_backward(
-        place, every, stats, strips, edge, dq_own, coarse_qkv, stash, merge_weight, pick
+        place, every, stats, edges, edge, dq_own, coarse_qkv, stash, merge_weight, pick
     )
     tiles = tiles.reshape(H1, EXT, 256)
     terms = lax.all_to_all(tiles, "col", split_axis=0, concat_axis=0, tiled=True)

time: 138 us -> 137 us (level)
  transfers between devices with their start and end apart: 8 -> 8, of which waited for: 7 -> 7; matrix products, arithmetic and copies ran while one was open for 1% -> 1% of each run, Pallas kernels for 10% -> 11%
where the time goes in v3:
time: 137 us
  Pallas kernels  52.5 us (38%)
  blocking collectives  33.5 us (24%)
  waiting for transfers between devices  23.5 us (17%)
  starting transfers between devices  22.6 us (16%)
  local copies, waits for them, and re-layouts  2.86 us (2%)
    all_to_all x1, blocking collectives, on_device(): lax.all_to_all(blocks, ('row', 'col'), split_axis=0, concat_axis=0, tiled...  18.2 us
    all_to_all x1, blocking collectives, on_device(): lax.all_to_all(tiles, 'col', split_axis=0, concat_axis=0, tiled=True)  15.3 us
    pallas_call x1, Pallas kernels, run_backward(): pl.pallas_call(backward_kernel, out_shape=[jax.ShapeDtypeStruct(s, d) for...  11.2 us
    ppermute x3, waiting for transfers between devices, swap_edges(): after = lax.ppermute(first, axis, ring(axis, -1))  10.2 us
    pallas_call x1, Pallas kernels, run_wide(): pl.pallas_call(wide_kernel, out_shape=[pltpu.HBM((STASH, D0), BF16), pltp...  9.76 us
    pallas_call x1, Pallas kernels, run_coarse_backward(): pl.pallas_call(coarse_backward, out_shape=[pltpu.HBM((H1 * EXT, 256), BF1...  9.3 us
    pallas_call x1, Pallas kernels, run_near(): pl.pallas_call(near_kernel, out_shape=pltpu.HBM((8, 8, 2 * own, 256), BF1...  9 us
    all_to_all x1, starting transfers between devices, on_device(): lax.all_to_all(packed.reshape(8 * H1, CROWS * CCOLS, 256), ('row', 'col')...  8.87 us
  transfers between devices with their start and end apart: 8, of which 7 were waited for; matrix products, arithmetic and copies ran while one was open for 1% of the time, Pallas kernels for 11%

profile of v3, /device:TPU:1, one launch (start us, length us, event | category | flops | bytes accessed | tf_op | source)
XLA Modules:
  0.0 136.6 jit_solution(7303726635215142417)
XLA Ops:
  0.6 0.0 copy-start
  0.6 0.0 copy-start.1
  0.7 0.0 copy-start.4
  0.7 0.0 copy-start.3
  0.7 0.0 copy-start.14
  0.7 0.0 copy-start.15
  0.7 1.2 row_strips.1
  1.9 4.5 %collective-permute-start = (bf16[312,256]{1,0:T(8,128)(2,1)S(1)}, bf16[312,256]{1,0:T(8,128)(2,1)S(1)}, u32[]{:S(2)}, u32[]{:S(2)}) collective-permute-start(bf16[312,256]{1,0:T(8,128)(2,1)S(1)} %get-tuple-element.40), channel_id=1, source_target_pairs={{0,16},{16,32},{32,48},{48,64},{64,80},{80,96},{96,112},{112,0},{1... | collective-permute-start | bytes 479240 | tf_op jit(solution)/shard_map/ppermute | solution.py:863
  6.4 2.3 %collective-permute-start.1 = (bf16[312,256]{1,0:T(8,128)(2,1)S(1)}, bf16[312,256]{1,0:T(8,128)(2,1)S(1)}, u32[]{:S(2)}, u32[]{:S(2)}) collective-permute-start(bf16[312,256]{1,0:T(8,128)(2,1)S(1)} %get-tuple-element.41), channel_id=1, source_target_pairs={{0,112},{16,0},{32,16},{48,32},{64,48},{80,64},{96,80},{112,96},{1... | collective-permute-start | bytes 479240 | tf_op jit(solution)/shard_map/ppermute | solution.py:864
  8.6 0.9 own_columns.1
  9.6 3.0 %collective-permute-done.above = bf16[312,256]{1,0:T(8,128)(2,1)S(1)} collective-permute-done((bf16[312,256]{1,0:T(8,128)(2,1)S(1)}, bf16[312,256]{1,0:T(8,128)(2,1)S(1)}, u32[]{:S(2)}, u32[]{:S(2)}) %collective-permute-start) | collective-permute-done | bytes 159776 | tf_op jit(solution)/shard_map/ppermute | solution.py:863
  12.6 4.0 %collective-permute-done.1.below = bf16[312,256]{1,0:T(8,128)(2,1)S(1)} collective-permute-done((bf16[312,256]{1,0:T(8,128)(2,1)S(1)}, bf16[312,256]{1,0:T(8,128)(2,1)S(1)}, u32[]{:S(2)}, u32[]{:S(2)}) %collective-permute-start.1) | collective-permute-done | bytes 159776 | tf_op jit(solution)/shard_map/ppermute | solution.py:864
  16.6 0.7 column_strips.1
  17.3 1.7 %collective-permute-start.2 = (bf16[256,256]{1,0:T(8,128)(2,1)}, bf16[256,256]{1,0:T(8,128)(2,1)S(1)}, u32[]{:S(2)}, u32[]{:S(2)}) collective-permute-start(bf16[256,256]{1,0:T(8,128)(2,1)} %get-tuple-element.44), channel_id=1, source_target_pairs={{0,1},{1,2},{2,3},{3,4},{4,5},{5,6},{6,7},{7,8},{8,9},{9,10},{10,1... | collective-permute-start | bytes 393224 | tf_op jit(solution)/shard_map/ppermute | solution.py:863
  18.9 0.0 collective-permute-start.3
  18.9 0.0 copy-done
  18.9 0.7 convolution_convert_fusion.grads
  19.6 0.1 pad_add_fusion.place
  19.7 1.5 %collective-permute-done.2.left = bf16[256,256]{1,0:T(8,128)(2,1)S(1)} collective-permute-done((bf16[256,256]{1,0:T(8,128)(2,1)}, bf16[256,256]{1,0:T(8,128)(2,1)S(1)}, u32[]{:S(2)}, u32[]{:S(2)}) %collective-permute-start.2) | collective-permute-done | bytes 131104 | tf_op jit(solution)/shard_map/ppermute | solution.py:863
  21.2 2.6 %collective-permute-done.3.right = bf16[256,256]{1,0:T(8,128)(2,1)S(1)} collective-permute-done((bf16[256,256]{1,0:T(8,128)(2,1)}, bf16[256,256]{1,0:T(8,128)(2,1)S(1)}, u32[]{:S(2)}, u32[]{:S(2)}) %collective-permute-start.3) | collective-permute-done | bytes 131104 | tf_op jit(solution)/shard_map/ppermute | solution.py:864
  23.8 0.0 copy-done.1
  23.8 0.0 copy-done.4
  23.8 0.0 copy-done.3
  23.9 9.0 %near_kernel.1 = bf16[8,8,48,256]{3,2,1,0:T(8,128)(2,1)} custom-call(s32[3]{0:T(128)S(1)} %pad_add_fusion.place, bf16[384,256]{1,0:T(8,128)(2,1)S(1)} %bitcast.19, bf16[312,256]{1,0:T(8,128)(2,1)S(1)} %collective-permute-done.above, bf16[312,256]{1,0:T(8,128)(2,1)S(1)} %collective-permute-done.1.below, bf16[256,256]{1,0:T(8,128)(2,1)S(1)} %collective-permute-done.2.left, ...), custom_call_target="tpu_custom_call" | custom-call | flops 3000000000 | bytes 20000000 | tf_op jit(solution)/shard_map/near_kernel/pallas_call | solution.py:246
  32.9 0.0 copy-start.6
  32.9 0.6 copy-done.6
  33.5 8.9 %all-to-all-start = ((bf16[128,24,256]{2,1,0:T(8,128)(2,1)}), bf16[128,24,256]{2,1,0:T(8,128)(2,1)}, u32[]{:S(2)}, u32[]{:S(2)}) async-start(bf16[128,24,256]{2,1,0:T(8,128)(2,1)} %bitcast.29), calls=%async_computation | async-start | bytes 3145728 | tf_op jit(solution)/shard_map/all_to_all | solution.py:1039
  42.4 0.1 grad_strips.1
  42.5 1.7 %collective-permute-start.4 = (bf16[120,256]{1,0:T(8,128)(2,1)S(1)}, bf16[120,256]{1,0:T(8,128)(2,1)S(1)}, u32[]{:S(2)}, u32[]{:S(2)}) collective-permute-start(bf16[120,256]{1,0:T(8,128)(2,1)S(1)} %get-tuple-element.52), channel_id=1, source_target_pairs={{0,1},{1,2},{2,3},{3,4},{4,5},{5,6},{6,7},{7,8},{8,9},{9,10},{10,1... | collective-permute-start | bytes 184328 | tf_op jit(solution)/shard_map/ppermute | solution.py:863
  44.2 0.0 collective-permute-start.5
  44.2 0.9 copy-done.7
  45.1 9.8 %wide_kernel.1 = (bf16[3968,256]{1,0:T(8,128)(2,1)}, f32[8,512]{1,0:T(8,128)}, bf16[48,1024]{1,0:T(8,128)(2,1)}) custom-call(s32[3]{0:T(128)S(1)} %pad_add_fusion.place, bf16[384,256]{1,0:T(8,128)(2,1)S(1)} %bitcast.20, bf16[312,256]{1,0:T(8,128)(2,1)S(1)} %collective-permute-done.above, bf16[312,256]{1,0:T(8,128)(2,1)S(1)} %collective-permute-done.1.below, ...), custom_call_target="tpu_custom_call" | custom-call | flops 3000000000 | bytes 10000000 | tf_op jit(solution)/shard_map/wide_kernel/pallas_call | solution.py:383
  54.9 0.0 copy-start.5
  54.9 0.0 collective-permute-done.4.grads_left
  54.9 0.6 copy-done.9
  55.5 3.6 %collective-permute-done.5.grads_right = bf16[120,256]{1,0:T(8,128)(2,1)S(1)} collective-permute-done((bf16[120,256]{1,0:T(8,128)(2,1)S(1)}, bf16[120,256]{1,0:T(8,128)(2,1)S(1)}, u32[]{:S(2)}, u32[]{:S(2)}) %collective-permute-start.5) | collective-permute-done | bytes 61472 | tf_op jit(solution)/shard_map/ppermute | solution.py:864
  59.1 0.6 copy-done.11
  59.7 7.1 %all-to-all-done = bf16[128,24,256]{2,1,0:T(8,128)(2,1)} async-done(((bf16[128,24,256]{2,1,0:T(8,128)(2,1)}), bf16[128,24,256]{2,1,0:T(8,128)(2,1)}, u32[]{:S(2)}, u32[]{:S(2)}) %all-to-all-start) | async-done | bytes 1572896 | tf_op jit(solution)/shard_map/all_to_all | solution.py:1039
  66.8 4.9 %coarse_forward.1.stats = f32[8,8,128]{2,1,0:T(8,128)} custom-call(s32[3]{0:T(128)S(1)} %pad_add_fusion.place, bf16[3072,256]{1,0:T(8,128)(2,1)} %bitcast.11.every), custom_call_target="tpu_custom_call" | custom-call | flops 1000000000 | bytes 2000000 | tf_op jit(solution)/shard_map/coarse_forward/pallas_call | solution.py:473
  71.8 3.5 %all-to-all-start.1 = ((f32[8,8,128]{2,1,0:T(8,128)}), f32[8,8,128]{2,1,0:T(8,128)S(1)}, u32[]{:S(2)}, u32[]{:S(2)}) async-start(f32[8,8,128]{2,1,0:T(8,128)} %coarse_forward.1.stats), calls=%async_computation.1 | async-start | bytes 65536 | tf_op jit(solution)/shard_map/all_to_all | solution.py:1055
  75.3 4.5 %coarse_own.1 = (bf16[576,256]{1,0:T(8,128)(2,1)}, bf16[384,128]{1,0:T(8,128)(2,1)}) custom-call(s32[3]{0:T(128)S(1)} %pad_add_fusion.place, bf16[3072,256]{1,0:T(8,128)(2,1)} %bitcast.11.every, f32[8,8,128]{2,1,0:T(8,128)} %coarse_forward.1.stats, bf16[2,96,384]{2,1,0:T(8,128)(2,1)S(1)} %copy-done.5), custom_call_target="tpu_custom_call" | custom-call | flops 1000000000 | bytes 2000000 | tf_op jit(solution)/shard_map/coarse_own/pallas_call | solution.py:530
  79.8 1.8 %all-to-all-done.1.stats = f32[8,8,128]{2,1,0:T(8,128)S(1)} async-done(((f32[8,8,128]{2,1,0:T(8,128)}), f32[8,8,128]{2,1,0:T(8,128)S(1)}, u32[]{:S(2)}, u32[]{:S(2)}) %all-to-all-start.1) | async-done | bytes 32800 | tf_op jit(solution)/shard_map/all_to_all | solution.py:1055
  81.6 9.3 %coarse_backward.1 = (bf16[768,256]{1,0:T(8,128)(2,1)}, bf16[1024,3072]{1,0:T(8,128)(2,1)S(1)}, bf16[3968,256]{1,0:T(8,128)(2,1)S(1)}, bf16[4096,1024]{1,0:T(8,128)(2,1)S(1)}, bf16[1024,1024]{1,0:T(8,128)(2,1)S(1)}) custom-call(s32[3]{0:T(128)S(1)} %pad_add_fusion.place, bf16[3072,256]{1,0:T(8,128)(2,1)} %bitcast.11.every, ...), custom_call_target="tpu_custom_call" | custom-call | flops 3000000000 | bytes 2000000 | tf_op jit(solution)/shard_map/coarse_backward/pallas_call | solution.py:632
  90.9 15.3 %all_to_all.20.terms_coarse = bf16[16,48,256]{2,1,0:T(8,128)(2,1)S(1)} all-to-all(bf16[16,48,256]{2,1,0:T(8,128)(2,1)} %bitcast.30), channel_id=1, replica_groups=mesh['row'=8,'col'=16] {'col'}, dimensions={0} | all-to-all | bytes 786432 | tf_op jit(solution)/shard_map/all_to_all | solution.py:1062
  106.2 0.0 copy-done.13
  106.2 11.2 %backward_kernel.1 = (bf16[384,256]{1,0:T(8,128)(2,1)}, bf16[128,16,128]{2,1,0:T(8,128)(2,1)S(1)}) custom-call(s32[3]{0:T(128)S(1)} %pad_add_fusion.place, bf16[16,48,256]{2,1,0:T(8,128)(2,1)S(1)} %all_to_all.20.terms_coarse, bf16[384,256]{1,0:T(8,128)(2,1)S(1)} %bitcast.23, bf16[24,1024]{1,0:T(8,128)(2,1)S(1)} %get-tuple-element.49.own_coarse, ...), custom_call_target="tpu_custom_call" | custom-call | flops 5000000000 | bytes 20000000 | tf_op jit(solution)/shard_map/backward_kernel/pallas_call | solution.py:816
  117.4 18.2 %all_to_all.21.terms = bf16[128,16,128]{2,1,0:T(8,128)(2,1)S(1)} all-to-all(bf16[128,16,128]{2,1,0:T(8,128)(2,1)S(1)} %get-tuple-element.74), channel_id=1, replica_groups=mesh['row'=8,'col'=16] {'row','col'}, dimensions={0} | all-to-all | bytes 1048576 | tf_op jit(solution)/shard_map/all_to_all | solution.py:1080
  135.6 1.0 sum_terms.1
  (15 shorter events, 0.0 us)
Async XLA Ops:
  0.6 18.3 %copy-start = (bf16[1024,1024]{1,0:T(8,128)(2,1)S(1)}, bf16[1024,1024]{1,0:T(8,128)(2,1)}, u32[]{:S(2)}) copy-start(bf16[1024,1024]{1,0:T(8,128)(2,1)} %param.22) | copy-start | bytes 6291460
  0.6 23.2 %copy-start.1 = (bf16[16,24,256]{2,1,0:T(8,128)(2,1)S(1)}, bf16[16,24,256]{2,1,0:T(8,128)(2,1)}, u32[]{:S(2)}) copy-start(bf16[16,24,256]{2,1,0:T(8,128)(2,1)} %param.13) | copy-start | bytes 589828
  0.7 23.2 %copy-start.4 = (bf16[256,256]{1,0:T(8,128)(2,1)S(1)}, bf16[256,256]{1,0:T(8,128)(2,1)}, u32[]{:S(2)}) copy-start(bf16[256,256]{1,0:T(8,128)(2,1)} %w_out.5) | copy-start | bytes 393220
  0.7 23.2 %copy-start.3 = (bf16[256,768]{1,0:T(8,128)(2,1)S(1)}, bf16[256,768]{1,0:T(8,128)(2,1)}, u32[]{:S(2)}) copy-start(bf16[256,768]{1,0:T(8,128)(2,1)} %w_qkv.5) | copy-start | bytes 1179652
  0.7 23.2 %copy-start.14 = (f32[1024]{0:T(1024)S(1)}, f32[1024]{0:T(1024)}, u32[]{:S(2)}) copy-start(f32[1024]{0:T(1024)} %param.20) | copy-start | bytes 12292
  0.7 23.2 %copy-start.15 = (f32[256]{0:T(256)S(1)}, f32[256]{0:T(256)}, u32[]{:S(2)}) copy-start(f32[256]{0:T(256)} %param.16) | copy-start | bytes 3076
  1.9 10.7 %collective-permute-start = (bf16[312,256]{1,0:T(8,128)(2,1)S(1)}, bf16[312,256]{1,0:T(8,128)(2,1)S(1)}, u32[]{:S(2)}, u32[]{:S(2)}) collective-permute-start(bf16[312,256]{1,0:T(8,128)(2,1)S(1)} %get-tuple-element.40), channel_id=1, source_target_pairs={{0,16},{16,32},{32,48},{48,64},{64,80},{80,96},{96,112},{112,0},{1... | collective-permute-start | bytes 479240 | tf_op jit(solution)/shard_map/ppermute | solution.py:863
  6.4 10.2 %collective-permute-start.1 = (bf16[312,256]{1,0:T(8,128)(2,1)S(1)}, bf16[312,256]{1,0:T(8,128)(2,1)S(1)}, u32[]{:S(2)}, u32[]{:S(2)}) collective-permute-start(bf16[312,256]{1,0:T(8,128)(2,1)S(1)} %get-tuple-element.41), channel_id=1, source_target_pairs={{0,112},{16,0},{32,16},{48,32},{64,48},{80,64},{96,80},{112,96},{1... | collective-permute-start | bytes 479240 | tf_op jit(solution)/shard_map/ppermute | solution.py:864
  17.3 3.9 %collective-permute-start.2 = (bf16[256,256]{1,0:T(8,128)(2,1)}, bf16[256,256]{1,0:T(8,128)(2,1)S(1)}, u32[]{:S(2)}, u32[]{:S(2)}) collective-permute-start(bf16[256,256]{1,0:T(8,128)(2,1)} %get-tuple-element.44), channel_id=1, source_target_pairs={{0,1},{1,2},{2,3},{3,4},{4,5},{5,6},{6,7},{7,8},{8,9},{9,10},{10,1... | collective-permute-start | bytes 393224 | tf_op jit(solution)/shard_map/ppermute | solution.py:863
  18.9 4.9 %collective-permute-start.3 = (bf16[256,256]{1,0:T(8,128)(2,1)}, bf16[256,256]{1,0:T(8,128)(2,1)S(1)}, u32[]{:S(2)}, u32[]{:S(2)}) collective-permute-start(bf16[256,256]{1,0:T(8,128)(2,1)} %get-tuple-element.45), channel_id=1, source_target_pairs={{0,15},{1,0},{2,1},{3,2},{4,3},{5,4},{6,5},{7,6},{8,7},{9,8},{10,9... | collective-permute-start | bytes 393224 | tf_op jit(solution)/shard_map/ppermute | solution.py:864
  32.9 0.7 copy-start.6
  33.5 8.9 %copy-start.2 = (bf16[16,24,256]{2,1,0:T(8,128)(2,1)S(1)}, bf16[16,24,256]{2,1,0:T(8,128)(2,1)}, u32[]{:S(2)}) copy-start(bf16[16,24,256]{2,1,0:T(8,128)(2,1)} %param.14) | copy-start | bytes 589828
  33.5 33.3 %all-to-all-start = ((bf16[128,24,256]{2,1,0:T(8,128)(2,1)}), bf16[128,24,256]{2,1,0:T(8,128)(2,1)}, u32[]{:S(2)}, u32[]{:S(2)}) async-start(bf16[128,24,256]{2,1,0:T(8,128)(2,1)} %bitcast.29), calls=%async_computation | async-start | bytes 3145728 | tf_op jit(solution)/shard_map/all_to_all | solution.py:1039
  42.5 12.4 %collective-permute-start.4 = (bf16[120,256]{1,0:T(8,128)(2,1)S(1)}, bf16[120,256]{1,0:T(8,128)(2,1)S(1)}, u32[]{:S(2)}, u32[]{:S(2)}) collective-permute-start(bf16[120,256]{1,0:T(8,128)(2,1)S(1)} %get-tuple-element.52), channel_id=1, source_target_pairs={{0,1},{1,2},{2,3},{3,4},{4,5},{5,6},{6,7},{7,8},{8,9},{9,10},{10,1... | collective-permute-start | bytes 184328 | tf_op jit(solution)/shard_map/ppermute | solution.py:863
  44.2 14.9 %collective-permute-start.5 = (bf16[120,256]{1,0:T(8,128)(2,1)S(1)}, bf16[120,256]{1,0:T(8,128)(2,1)S(1)}, u32[]{:S(2)}, u32[]{:S(2)}) collective-permute-start(bf16[120,256]{1,0:T(8,128)(2,1)S(1)} %get-tuple-element.53), channel_id=1, source_target_pairs={{0,15},{1,0},{2,1},{3,2},{4,3},{5,4},{6,5},{7,6},{8,7},{9,8},{10,9... | collective-permute-start | bytes 184328 | tf_op jit(solution)/shard_map/ppermute | solution.py:864
  44.2 0.9 copy-start.7
  54.9 20.4 %copy-start.5 = (bf16[2,96,384]{2,1,0:T(8,128)(2,1)S(1)}, bf16[2,96,384]{2,1,0:T(8,128)(2,1)}, u32[]{:S(2)}) copy-start(bf16[2,96,384]{2,1,0:T(8,128)(2,1)} %constant.19.clone.strips) | copy-start | bytes 442372
  54.9 0.6 copy-start.9
  59.1 0.6 copy-start.11
  71.8 9.8 %all-to-all-start.1 = ((f32[8,8,128]{2,1,0:T(8,128)}), f32[8,8,128]{2,1,0:T(8,128)S(1)}, u32[]{:S(2)}, u32[]{:S(2)}) async-start(f32[8,8,128]{2,1,0:T(8,128)} %coarse_forward.1.stats), calls=%async_computation.1 | async-start | bytes 65536 | tf_op jit(solution)/shard_map/all_to_all | solution.py:1055
  81.6 24.6 %copy-start.8 = (bf16[48,1024]{1,0:T(8,128)(2,1)S(1)}, bf16[48,1024]{1,0:T(8,128)(2,1)}, u32[]{:S(2)}) copy-start(bf16[48,1024]{1,0:T(8,128)(2,1)} %get-tuple-element.67.coarse) | copy-start | bytes 294916
  81.6 24.6 %copy-start.10 = (bf16[120,256]{1,0:T(8,128)(2,1)S(1)}, bf16[120,256]{1,0:T(8,128)(2,1)}, u32[]{:S(2)}) copy-start(bf16[120,256]{1,0:T(8,128)(2,1)} %copy-done.9) | copy-start | bytes 184324
  81.6 24.6 %copy-start.12 = (bf16[120,256]{1,0:T(8,128)(2,1)S(1)}, bf16[120,256]{1,0:T(8,128)(2,1)}, u32[]{:S(2)}) copy-start(bf16[120,256]{1,0:T(8,128)(2,1)} %copy-done.11) | copy-start | bytes 184324
  81.6 24.6 %copy-start.13 = (f32[8,512]{1,0:T(8,128)S(1)}, f32[8,512]{1,0:T(8,128)}, u32[]{:S(2)}) copy-start(f32[8,512]{1,0:T(8,128)} %get-tuple-element.68.lse) | copy-start | bytes 49156

commit v4 on v3

--- a/solution.py
+++ b/solution.py
@@ -868,7 +868,8 @@
 HALO = 8
 TOKEN_ROWS = HALO * COLS
 FINE_ROWS = 4 * COLS
-STRIP_ROWS = TOKEN_ROWS + FINE_ROWS + 4 * CCOLS
+FILL = 8
+STRIP_ROWS = TOKEN_ROWS + FINE_ROWS + 4 * CCOLS + FILL
 
 
 def row_strips(tokens, grad_fine, grad_coarse, first, last, flat, held, sems):
@@ -897,6 +898,7 @@
     flat[...] = jnp.concatenate(rows, axis=0).astype(BF16)
     for out, coarse in ((first, rows[0]), (last, rows[-1])):
         pieces = [coarse[:, D0 * g : D0 * (g + 1)] for g in range(4)]
+        pieces.append(jnp.zeros((FILL, D0), F32))
         out[TOKEN_ROWS + FINE_ROWS :] = jnp.concatenate(pieces, axis=0).astype(BF16)
     for copy in copies[1:]:
         copy.wait()
@@ -986,6 +988,8 @@
     fine, coarse = grads_of(own_fine, own_coarse, above, below)
     left = [row[:4] for row in fine] + [piece[:1] for row in coarse for piece in row]
     right = [row[-4:] for row in fine] + [piece[-1:] for row in coarse for piece in row]
+    left.append(jnp.zeros((FILL, D0), F32))
+    right.append(jnp.zeros((FILL, D0), F32))
     first[...] = jnp.concatenate(left, axis=0).astype(BF16)
     last[...] = jnp.concatenate(right, axis=0).astype(BF16)
 
@@ -993,7 +997,7 @@
 def run_grad_strips(own_fine, own_coarse, above, below):
     return pl.pallas_call(
         grad_strips,
-        out_shape=[jax.ShapeDtypeStruct((R4 * 4 + EXT // 2, D0), BF16)] * 2,
+        out_shape=[jax.ShapeDtypeStruct((R4 * 4 + EXT // 2 + FILL, D0), BF16)] * 2,
         in_specs=[whole()] * 4,
         out_specs=[whole()] * 2,
         compiler_params=vmem_params(8),

time: 137 us -> 138 us (level)
  no operation moved by 1% of the time
where the time goes in v4:
time: 138 us; the launch traced here: 137 us
  Pallas kernels  52.7 us (38%)
  blocking collectives  33.6 us (24%)
  waiting for transfers between devices  23.7 us (17%)
  starting transfers between devices  22.6 us (16%)
  local copies, waits for them, and re-layouts  2.86 us (2%)
    all_to_all x1, blocking collectives, on_device(): lax.all_to_all(blocks, ('row', 'col'), split_axis=0, concat_axis=0, tiled...  18.2 us
    all_to_all x1, blocking collectives, on_device(): lax.all_to_all(tiles, 'col', split_axis=0, concat_axis=0, tiled=True)  15.4 us
    pallas_call x1, Pallas kernels, run_backward(): pl.pallas_call(backward_kernel, out_shape=[jax.ShapeDtypeStruct(s, d) for...  11.3 us
    ppermute x3, waiting for transfers between devices, swap_edges(): after = lax.ppermute(first, axis, ring(axis, -1))  10.2 us
    pallas_call x1, Pallas kernels, run_wide(): pl.pallas_call(wide_kernel, out_shape=[pltpu.HBM((STASH, D0), BF16), pltp...  9.77 us
    pallas_call x1, Pallas kernels, run_coarse_backward(): pl.pallas_call(coarse_backward, out_shape=[pltpu.HBM((H1 * EXT, 256), BF1...  9.31 us
    pallas_call x1, Pallas kernels, run_near(): pl.pallas_call(near_kernel, out_shape=pltpu.HBM((8, 8, 2 * own, 256), BF1...  9 us
    all_to_all x1, starting transfers between devices, on_device(): lax.all_to_all(packed.reshape(8 * H1, CROWS * CCOLS, 256), ('row', 'col')...  8.87 us
  transfers between devices with their start and end apart: 8, of which 7 were waited for; matrix products, arithmetic and copies ran while one was open for 1% of the time, Pallas kernels for 11%

profile of v4, /device:TPU:1, one launch (start us, length us, event | category | flops | bytes accessed | tf_op | source)
XLA Modules:
  0.0 137.0 jit_solution(12723459801094561134)
XLA Ops:
  0.6 0.0 copy-start
  0.6 0.0 copy-start.1
  0.7 0.0 copy-start.4
  0.7 0.0 copy-start.3
  0.7 0.0 copy-start.14
  0.7 0.0 copy-start.15
  0.7 1.2 row_strips.1
  1.9 4.5 %collective-permute-start = (bf16[320,256]{1,0:T(8,128)(2,1)S(1)}, bf16[320,256]{1,0:T(8,128)(2,1)S(1)}, u32[]{:S(2)}, u32[]{:S(2)}) collective-permute-start(bf16[320,256]{1,0:T(8,128)(2,1)S(1)} %get-tuple-element.40), channel_id=1, source_target_pairs={{0,16},{16,32},{32,48},{48,64},{64,80},{80,96},{96,112},{112,0},{1... | collective-permute-start | bytes 491528 | tf_op jit(solution)/shard_map/ppermute | solution.py:863
  6.4 2.3 %collective-permute-start.1 = (bf16[320,256]{1,0:T(8,128)(2,1)S(1)}, bf16[320,256]{1,0:T(8,128)(2,1)S(1)}, u32[]{:S(2)}, u32[]{:S(2)}) collective-permute-start(bf16[320,256]{1,0:T(8,128)(2,1)S(1)} %get-tuple-element.41), channel_id=1, source_target_pairs={{0,112},{16,0},{32,16},{48,32},{64,48},{80,64},{96,80},{112,96},{1... | collective-permute-start | bytes 491528 | tf_op jit(solution)/shard_map/ppermute | solution.py:864
  8.6 0.9 own_columns.1
  9.6 3.2 %collective-permute-done.above = bf16[320,256]{1,0:T(8,128)(2,1)S(1)} collective-permute-done((bf16[320,256]{1,0:T(8,128)(2,1)S(1)}, bf16[320,256]{1,0:T(8,128)(2,1)S(1)}, u32[]{:S(2)}, u32[]{:S(2)}) %collective-permute-start) | collective-permute-done | bytes 163872 | tf_op jit(solution)/shard_map/ppermute | solution.py:863
  12.7 4.0 %collective-permute-done.1.below = bf16[320,256]{1,0:T(8,128)(2,1)S(1)} collective-permute-done((bf16[320,256]{1,0:T(8,128)(2,1)S(1)}, bf16[320,256]{1,0:T(8,128)(2,1)S(1)}, u32[]{:S(2)}, u32[]{:S(2)}) %collective-permute-start.1) | collective-permute-done | bytes 163872 | tf_op jit(solution)/shard_map/ppermute | solution.py:864
  16.7 0.7 column_strips.1
  17.4 1.7 %collective-permute-start.2 = (bf16[256,256]{1,0:T(8,128)(2,1)}, bf16[256,256]{1,0:T(8,128)(2,1)S(1)}, u32[]{:S(2)}, u32[]{:S(2)}) collective-permute-start(bf16[256,256]{1,0:T(8,128)(2,1)} %get-tuple-element.44), channel_id=1, source_target_pairs={{0,1},{1,2},{2,3},{3,4},{4,5},{5,6},{6,7},{7,8},{8,9},{9,10},{10,1... | collective-permute-start | bytes 393224 | tf_op jit(solution)/shard_map/ppermute | solution.py:863
  19.1 0.0 collective-permute-start.3
  19.1 0.0 copy-done
  19.1 0.7 convolution_convert_fusion.grads
  19.8 0.1 pad_add_fusion.place
  19.9 1.5 %collective-permute-done.2.left = bf16[256,256]{1,0:T(8,128)(2,1)S(1)} collective-permute-done((bf16[256,256]{1,0:T(8,128)(2,1)}, bf16[256,256]{1,0:T(8,128)(2,1)S(1)}, u32[]{:S(2)}, u32[]{:S(2)}) %collective-permute-start.2) | collective-permute-done | bytes 131104 | tf_op jit(solution)/shard_map/ppermute | solution.py:863
  21.4 2.6 %collective-permute-done.3.right = bf16[256,256]{1,0:T(8,128)(2,1)S(1)} collective-permute-done((bf16[256,256]{1,0:T(8,128)(2,1)}, bf16[256,256]{1,0:T(8,128)(2,1)S(1)}, u32[]{:S(2)}, u32[]{:S(2)}) %collective-permute-start.3) | collective-permute-done | bytes 131104 | tf_op jit(solution)/shard_map/ppermute | solution.py:864
  24.0 0.0 copy-done.1
  24.0 0.0 copy-done.4
  24.0 0.0 copy-done.3
  24.0 9.0 %near_kernel.1 = bf16[8,8,48,256]{3,2,1,0:T(8,128)(2,1)} custom-call(s32[3]{0:T(128)S(1)} %pad_add_fusion.place, bf16[384,256]{1,0:T(8,128)(2,1)S(1)} %bitcast.19, bf16[320,256]{1,0:T(8,128)(2,1)S(1)} %collective-permute-done.above, bf16[320,256]{1,0:T(8,128)(2,1)S(1)} %collective-permute-done.1.below, bf16[256,256]{1,0:T(8,128)(2,1)S(1)} %collective-permute-done.2.left, ...), custom_call_target="tpu_custom_call" | custom-call | flops 3000000000 | bytes 20000000 | tf_op jit(solution)/shard_map/near_kernel/pallas_call | solution.py:246
  33.0 0.0 copy-start.6
  33.1 0.6 copy-done.6
  33.7 8.9 %all-to-all-start = ((bf16[128,24,256]{2,1,0:T(8,128)(2,1)}), bf16[128,24,256]{2,1,0:T(8,128)(2,1)}, u32[]{:S(2)}, u32[]{:S(2)}) async-start(bf16[128,24,256]{2,1,0:T(8,128)(2,1)} %bitcast.29), calls=%async_computation | async-start | bytes 3145728 | tf_op jit(solution)/shard_map/all_to_all | solution.py:1043
  42.6 0.1 grad_strips.1
  42.7 1.7 %collective-permute-start.4 = (bf16[128,256]{1,0:T(8,128)(2,1)S(1)}, bf16[128,256]{1,0:T(8,128)(2,1)S(1)}, u32[]{:S(2)}, u32[]{:S(2)}) collective-permute-start(bf16[128,256]{1,0:T(8,128)(2,1)S(1)} %get-tuple-element.52), channel_id=1, source_target_pairs={{0,1},{1,2},{2,3},{3,4},{4,5},{5,6},{6,7},{7,8},{8,9},{9,10},{10,1... | collective-permute-start | bytes 196616 | tf_op jit(solution)/shard_map/ppermute | solution.py:863
  44.4 0.0 collective-permute-start.5
  44.4 0.9 copy-done.7
  45.3 9.8 %wide_kernel.1 = (bf16[3968,256]{1,0:T(8,128)(2,1)}, f32[8,512]{1,0:T(8,128)}, bf16[48,1024]{1,0:T(8,128)(2,1)}) custom-call(s32[3]{0:T(128)S(1)} %pad_add_fusion.place, bf16[384,256]{1,0:T(8,128)(2,1)S(1)} %bitcast.20, bf16[320,256]{1,0:T(8,128)(2,1)S(1)} %collective-permute-done.above, bf16[320,256]{1,0:T(8,128)(2,1)S(1)} %collective-permute-done.1.below, ...), custom_call_target="tpu_custom_call" | custom-call | flops 3000000000 | bytes 10000000 | tf_op jit(solution)/shard_map/wide_kernel/pallas_call | solution.py:383
  55.1 0.0 copy-start.5
  55.1 0.0 collective-permute-done.4.grads_left
  55.1 0.6 copy-done.9
  55.7 3.6 %collective-permute-done.5.grads_right = bf16[128,256]{1,0:T(8,128)(2,1)S(1)} collective-permute-done((bf16[128,256]{1,0:T(8,128)(2,1)S(1)}, bf16[128,256]{1,0:T(8,128)(2,1)S(1)}, u32[]{:S(2)}, u32[]{:S(2)}) %collective-permute-start.5) | collective-permute-done | bytes 65568 | tf_op jit(solution)/shard_map/ppermute | solution.py:864
  59.3 0.6 copy-done.11
  59.9 7.0 %all-to-all-done = bf16[128,24,256]{2,1,0:T(8,128)(2,1)} async-done(((bf16[128,24,256]{2,1,0:T(8,128)(2,1)}), bf16[128,24,256]{2,1,0:T(8,128)(2,1)}, u32[]{:S(2)}, u32[]{:S(2)}) %all-to-all-start) | async-done | bytes 1572896 | tf_op jit(solution)/shard_map/all_to_all | solution.py:1043
  67.0 4.9 %coarse_forward.1.stats = f32[8,8,128]{2,1,0:T(8,128)} custom-call(s32[3]{0:T(128)S(1)} %pad_add_fusion.place, bf16[3072,256]{1,0:T(8,128)(2,1)} %bitcast.11.every), custom_call_target="tpu_custom_call" | custom-call | flops 1000000000 | bytes 2000000 | tf_op jit(solution)/shard_map/coarse_forward/pallas_call | solution.py:473
  71.9 3.5 %all-to-all-start.1 = ((f32[8,8,128]{2,1,0:T(8,128)}), f32[8,8,128]{2,1,0:T(8,128)S(1)}, u32[]{:S(2)}, u32[]{:S(2)}) async-start(f32[8,8,128]{2,1,0:T(8,128)} %coarse_forward.1.stats), calls=%async_computation.1 | async-start | bytes 65536 | tf_op jit(solution)/shard_map/all_to_all | solution.py:1059
  75.5 4.5 %coarse_own.1 = (bf16[576,256]{1,0:T(8,128)(2,1)}, bf16[384,128]{1,0:T(8,128)(2,1)}) custom-call(s32[3]{0:T(128)S(1)} %pad_add_fusion.place, bf16[3072,256]{1,0:T(8,128)(2,1)} %bitcast.11.every, f32[8,8,128]{2,1,0:T(8,128)} %coarse_forward.1.stats, bf16[2,96,384]{2,1,0:T(8,128)(2,1)S(1)} %copy-done.5), custom_call_target="tpu_custom_call" | custom-call | flops 1000000000 | bytes 2000000 | tf_op jit(solution)/shard_map/coarse_own/pallas_call | solution.py:530
  80.0 1.8 %all-to-all-done.1.stats = f32[8,8,128]{2,1,0:T(8,128)S(1)} async-done(((f32[8,8,128]{2,1,0:T(8,128)}), f32[8,8,128]{2,1,0:T(8,128)S(1)}, u32[]{:S(2)}, u32[]{:S(2)}) %all-to-all-start.1) | async-done | bytes 32800 | tf_op jit(solution)/shard_map/all_to_all | solution.py:1059
  81.8 9.3 %coarse_backward.1 = (bf16[768,256]{1,0:T(8,128)(2,1)}, bf16[1024,3072]{1,0:T(8,128)(2,1)S(1)}, bf16[3968,256]{1,0:T(8,128)(2,1)S(1)}, bf16[4096,1024]{1,0:T(8,128)(2,1)S(1)}, bf16[1024,1024]{1,0:T(8,128)(2,1)S(1)}) custom-call(s32[3]{0:T(128)S(1)} %pad_add_fusion.place, bf16[3072,256]{1,0:T(8,128)(2,1)} %bitcast.11.every, ...), custom_call_target="tpu_custom_call" | custom-call | flops 3000000000 | bytes 2000000 | tf_op jit(solution)/shard_map/coarse_backward/pallas_call | solution.py:632
  91.1 15.4 %all_to_all.20.terms_coarse = bf16[16,48,256]{2,1,0:T(8,128)(2,1)S(1)} all-to-all(bf16[16,48,256]{2,1,0:T(8,128)(2,1)} %bitcast.30), channel_id=1, replica_groups=mesh['row'=8,'col'=16] {'col'}, dimensions={0} | all-to-all | bytes 786432 | tf_op jit(solution)/shard_map/all_to_all | solution.py:1066
  106.4 0.0 copy-done.8
  106.5 11.3 %backward_kernel.1 = (bf16[384,256]{1,0:T(8,128)(2,1)}, bf16[128,16,128]{2,1,0:T(8,128)(2,1)S(1)}) custom-call(s32[3]{0:T(128)S(1)} %pad_add_fusion.place, bf16[16,48,256]{2,1,0:T(8,128)(2,1)S(1)} %all_to_all.20.terms_coarse, bf16[384,256]{1,0:T(8,128)(2,1)S(1)} %bitcast.23, bf16[24,1024]{1,0:T(8,128)(2,1)S(1)} %get-tuple-element.49.own_coarse, ...), custom_call_target="tpu_custom_call" | custom-call | flops 5000000000 | bytes 20000000 | tf_op jit(solution)/shard_map/backward_kernel/pallas_call | solution.py:816
  117.8 18.2 %all_to_all.21.terms = bf16[128,16,128]{2,1,0:T(8,128)(2,1)S(1)} all-to-all(bf16[128,16,128]{2,1,0:T(8,128)(2,1)S(1)} %get-tuple-element.74), channel_id=1, replica_groups=mesh['row'=8,'col'=16] {'row','col'}, dimensions={0} | all-to-all | bytes 1048576 | tf_op jit(solution)/shard_map/all_to_all | solution.py:1084
  136.0 1.0 sum_terms.1
  (15 shorter events, 0.0 us)
Async XLA Ops:
  0.6 18.5 %copy-start = (bf16[1024,1024]{1,0:T(8,128)(2,1)S(1)}, bf16[1024,1024]{1,0:T(8,128)(2,1)}, u32[]{:S(2)}) copy-start(bf16[1024,1024]{1,0:T(8,128)(2,1)} %param.22) | copy-start | bytes 6291460
  0.6 23.4 %copy-start.1 = (bf16[16,24,256]{2,1,0:T(8,128)(2,1)S(1)}, bf16[16,24,256]{2,1,0:T(8,128)(2,1)}, u32[]{:S(2)}) copy-start(bf16[16,24,256]{2,1,0:T(8,128)(2,1)} %param.13) | copy-start | bytes 589828
  0.7 23.4 %copy-start.4 = (bf16[256,256]{1,0:T(8,128)(2,1)S(1)}, bf16[256,256]{1,0:T(8,128)(2,1)}, u32[]{:S(2)}) copy-start(bf16[256,256]{1,0:T(8,128)(2,1)} %w_out.5) | copy-start | bytes 393220
  0.7 23.4 %copy-start.3 = (bf16[256,768]{1,0:T(8,128)(2,1)S(1)}, bf16[256,768]{1,0:T(8,128)(2,1)}, u32[]{:S(2)}) copy-start(bf16[256,768]{1,0:T(8,128)(2,1)} %w_qkv.5) | copy-start | bytes 1179652
  0.7 23.3 %copy-start.14 = (f32[1024]{0:T(1024)S(1)}, f32[1024]{0:T(1024)}, u32[]{:S(2)}) copy-start(f32[1024]{0:T(1024)} %param.20) | copy-start | bytes 12292
  0.7 23.3 %copy-start.15 = (f32[256]{0:T(256)S(1)}, f32[256]{0:T(256)}, u32[]{:S(2)}) copy-start(f32[256]{0:T(256)} %param.16) | copy-start | bytes 3076
  1.9 10.9 %collective-permute-start = (bf16[320,256]{1,0:T(8,128)(2,1)S(1)}, bf16[320,256]{1,0:T(8,128)(2,1)S(1)}, u32[]{:S(2)}, u32[]{:S(2)}) collective-permute-start(bf16[320,256]{1,0:T(8,128)(2,1)S(1)} %get-tuple-element.40), channel_id=1, source_target_pairs={{0,16},{16,32},{32,48},{48,64},{64,80},{80,96},{96,112},{112,0},{1... | collective-permute-start | bytes 491528 | tf_op jit(solution)/shard_map/ppermute | solution.py:863
  6.4 10.4 %collective-permute-start.1 = (bf16[320,256]{1,0:T(8,128)(2,1)S(1)}, bf16[320,256]{1,0:T(8,128)(2,1)S(1)}, u32[]{:S(2)}, u32[]{:S(2)}) collective-permute-start(bf16[320,256]{1,0:T(8,128)(2,1)S(1)} %get-tuple-element.41), channel_id=1, source_target_pairs={{0,112},{16,0},{32,16},{48,32},{64,48},{80,64},{96,80},{112,96},{1... | collective-permute-start | bytes 491528 | tf_op jit(solution)/shard_map/ppermute | solution.py:864
  17.4 3.9 %collective-permute-start.2 = (bf16[256,256]{1,0:T(8,128)(2,1)}, bf16[256,256]{1,0:T(8,128)(2,1)S(1)}, u32[]{:S(2)}, u32[]{:S(2)}) collective-permute-start(bf16[256,256]{1,0:T(8,128)(2,1)} %get-tuple-element.44), channel_id=1, source_target_pairs={{0,1},{1,2},{2,3},{3,4},{4,5},{5,6},{6,7},{7,8},{8,9},{9,10},{10,1... | collective-permute-start | bytes 393224 | tf_op jit(solution)/shard_map/ppermute | solution.py:863
  19.1 4.9 %collective-permute-start.3 = (bf16[256,256]{1,0:T(8,128)(2,1)}, bf16[256,256]{1,0:T(8,128)(2,1)S(1)}, u32[]{:S(2)}, u32[]{:S(2)}) collective-permute-start(bf16[256,256]{1,0:T(8,128)(2,1)} %get-tuple-element.45), channel_id=1, source_target_pairs={{0,15},{1,0},{2,1},{3,2},{4,3},{5,4},{6,5},{7,6},{8,7},{9,8},{10,9... | collective-permute-start | bytes 393224 | tf_op jit(solution)/shard_map/ppermute | solution.py:864
  33.0 0.7 copy-start.6
  33.7 8.9 %copy-start.2 = (bf16[16,24,256]{2,1,0:T(8,128)(2,1)S(1)}, bf16[16,24,256]{2,1,0:T(8,128)(2,1)}, u32[]{:S(2)}) copy-start(bf16[16,24,256]{2,1,0:T(8,128)(2,1)} %param.14) | copy-start | bytes 589828
  33.7 33.3 %all-to-all-start = ((bf16[128,24,256]{2,1,0:T(8,128)(2,1)}), bf16[128,24,256]{2,1,0:T(8,128)(2,1)}, u32[]{:S(2)}, u32[]{:S(2)}) async-start(bf16[128,24,256]{2,1,0:T(8,128)(2,1)} %bitcast.29), calls=%async_computation | async-start | bytes 3145728 | tf_op jit(solution)/shard_map/all_to_all | solution.py:1043
  42.7 12.4 %collective-permute-start.4 = (bf16[128,256]{1,0:T(8,128)(2,1)S(1)}, bf16[128,256]{1,0:T(8,128)(2,1)S(1)}, u32[]{:S(2)}, u32[]{:S(2)}) collective-permute-start(bf16[128,256]{1,0:T(8,128)(2,1)S(1)} %get-tuple-element.52), channel_id=1, source_target_pairs={{0,1},{1,2},{2,3},{3,4},{4,5},{5,6},{6,7},{7,8},{8,9},{9,10},{10,1... | collective-permute-start | bytes 196616 | tf_op jit(solution)/shard_map/ppermute | solution.py:863
  44.4 14.9 %collective-permute-start.5 = (bf16[128,256]{1,0:T(8,128)(2,1)S(1)}, bf16[128,256]{1,0:T(8,128)(2,1)S(1)}, u32[]{:S(2)}, u32[]{:S(2)}) collective-permute-start(bf16[128,256]{1,0:T(8,128)(2,1)S(1)} %get-tuple-element.53), channel_id=1, source_target_pairs={{0,15},{1,0},{2,1},{3,2},{4,3},{5,4},{6,5},{7,6},{8,7},{9,8},{10,9... | collective-permute-start | bytes 196616 | tf_op jit(solution)/shard_map/ppermute | solution.py:864
  44.4 0.9 copy-start.7
  55.1 20.4 %copy-start.5 = (bf16[2,96,384]{2,1,0:T(8,128)(2,1)S(1)}, bf16[2,96,384]{2,1,0:T(8,128)(2,1)}, u32[]{:S(2)}) copy-start(bf16[2,96,384]{2,1,0:T(8,128)(2,1)} %constant.19.clone.strips) | copy-start | bytes 442372
  55.1 0.6 copy-start.9
  59.3 0.6 copy-start.11
  71.9 9.8 %all-to-all-start.1 = ((f32[8,8,128]{2,1,0:T(8,128)}), f32[8,8,128]{2,1,0:T(8,128)S(1)}, u32[]{:S(2)}, u32[]{:S(2)}) async-start(f32[8,8,128]{2,1,0:T(8,128)} %coarse_forward.1.stats), calls=%async_computation.1 | async-start | bytes 65536 | tf_op jit(solution)/shard_map/all_to_all | solution.py:1059
  81.8 24.7 %copy-start.8 = (bf16[48,1024]{1,0:T(8,128)(2,1)S(1)}, bf16[48,1024]{1,0:T(8,128)(2,1)}, u32[]{:S(2)}) copy-start(bf16[48,1024]{1,0:T(8,128)(2,1)} %get-tuple-element.67.coarse) | copy-start | bytes 294916
  81.8 24.7 %copy-start.10 = (bf16[128,256]{1,0:T(8,128)(2,1)S(1)}, bf16[128,256]{1,0:T(8,128)(2,1)}, u32[]{:S(2)}) copy-start(bf16[128,256]{1,0:T(8,128)(2,1)} %copy-done.9) | copy-start | bytes 196612
  81.8 24.7 %copy-start.12 = (bf16[128,256]{1,0:T(8,128)(2,1)S(1)}, bf16[128,256]{1,0:T(8,128)(2,1)}, u32[]{:S(2)}) copy-start(bf16[128,256]{1,0:T(8,128)(2,1)} %copy-done.11) | copy-start | bytes 196612
  81.8 24.7 %copy-start.13 = (f32[8,512]{1,0:T(8,128)S(1)}, f32[8,512]{1,0:T(8,128)}, u32[]{:S(2)}) copy-start(f32[8,512]{1,0:T(8,128)} %get-tuple-element.68.lse) | copy-start | bytes 49156

commit v5 on v4

--- a/solution.py
+++ b/solution.py
@@ -454,8 +454,8 @@
         maxima = jnp.max(scores_ref[b], axis=1, keepdims=True)
         exponent = jnp.exp(scores_ref[b] - maxima)
         totals = jnp.sum(exponent, axis=1, keepdims=True)
-        weights = (exponent * (1.0 / totals)).astype(BF16)
-        attended = dot(weights, keyval, 1, 0).astype(BF16).astype(F32)
+        attended = dot(exponent.astype(BF16), keyval, 1, 0) * (1.0 / totals)
+        attended = attended.astype(BF16).astype(F32)
         product = lane_half(own[rows].astype(F32) * attended, False)
         columns.append((maxima + jnp.log(totals), jnp.sum(product, axis=1, keepdims=True)))
     lane = lax.broadcasted_iota(jnp.int32, (128, 128), 1)

time: 138 us -> 137 us (level)
  no operation moved by 1% of the time
where the time goes in v5:
time: 137 us; the launch traced here: 136 us
  Pallas kernels  52 us (38%)
  blocking collectives  33.6 us (25%)
  waiting for transfers between devices  23.7 us (17%)
  starting transfers between devices  22.6 us (16%)
  local copies, waits for them, and re-layouts  2.86 us (2%)
    all_to_all x1, blocking collectives, on_device(): lax.all_to_all(blocks, ('row', 'col'), split_axis=0, concat_axis=0, tiled...  18.2 us
    all_to_all x1, blocking collectives, on_device(): lax.all_to_all(tiles, 'col', split_axis=0, concat_axis=0, tiled=True)  15.3 us
    pallas_call x1, Pallas kernels, run_backward(): pl.pallas_call(backward_kernel, out_shape=[jax.ShapeDtypeStruct(s, d) for...  11.3 us
    ppermute x3, waiting for transfers between devices, swap_edges(): after = lax.ppermute(first, axis, ring(axis, -1))  10.2 us
    pallas_call x1, Pallas kernels, run_wide(): pl.pallas_call(wide_kernel, out_shape=[pltpu.HBM((STASH, D0), BF16), pltp...  9.77 us
    pallas_call x1, Pallas kernels, run_coarse_backward(): pl.pallas_call(coarse_backward, out_shape=[pltpu.HBM((H1 * EXT, 256), BF1...  9.31 us
    pallas_call x1, Pallas kernels, run_near(): pl.pallas_call(near_kernel, out_shape=pltpu.HBM((8, 8, 2 * own, 256), BF1...  9 us
    all_to_all x1, starting transfers between devices, on_device(): lax.all_to_all(packed.reshape(8 * H1, CROWS * CCOLS, 256), ('row', 'col')...  8.87 us
  transfers between devices with their start and end apart: 8, of which 7 were waited for; matrix products, arithmetic and copies ran while one was open for 1% of the time, Pallas kernels for 11%

profile of v5, /device:TPU:1, one launch (start us, length us, event | category | flops | bytes accessed | tf_op | source)
XLA Modules:
  0.0 136.3 jit_solution(8504208606968692081)
XLA Ops:
  0.6 0.0 copy-start
  0.6 0.0 copy-start.1
  0.7 0.0 copy-start.4
  0.7 0.0 copy-start.3
  0.7 0.0 copy-start.14
  0.7 0.0 copy-start.15
  0.7 1.2 row_strips.1
  1.9 4.5 %collective-permute-start = (bf16[320,256]{1,0:T(8,128)(2,1)S(1)}, bf16[320,256]{1,0:T(8,128)(2,1)S(1)}, u32[]{:S(2)}, u32[]{:S(2)}) collective-permute-start(bf16[320,256]{1,0:T(8,128)(2,1)S(1)} %get-tuple-element.40), channel_id=1, source_target_pairs={{0,16},{16,32},{32,48},{48,64},{64,80},{80,96},{96,112},{112,0},{1... | collective-permute-start | bytes 491528 | tf_op jit(solution)/shard_map/ppermute | solution.py:863
  6.4 2.3 %collective-permute-start.1 = (bf16[320,256]{1,0:T(8,128)(2,1)S(1)}, bf16[320,256]{1,0:T(8,128)(2,1)S(1)}, u32[]{:S(2)}, u32[]{:S(2)}) collective-permute-start(bf16[320,256]{1,0:T(8,128)(2,1)S(1)} %get-tuple-element.41), channel_id=1, source_target_pairs={{0,112},{16,0},{32,16},{48,32},{64,48},{80,64},{96,80},{112,96},{1... | collective-permute-start | bytes 491528 | tf_op jit(solution)/shard_map/ppermute | solution.py:864
  8.6 0.9 own_columns.1
  9.6 3.2 %collective-permute-done.above = bf16[320,256]{1,0:T(8,128)(2,1)S(1)} collective-permute-done((bf16[320,256]{1,0:T(8,128)(2,1)S(1)}, bf16[320,256]{1,0:T(8,128)(2,1)S(1)}, u32[]{:S(2)}, u32[]{:S(2)}) %collective-permute-start) | collective-permute-done | bytes 163872 | tf_op jit(solution)/shard_map/ppermute | solution.py:863
  12.7 4.0 %collective-permute-done.1.below = bf16[320,256]{1,0:T(8,128)(2,1)S(1)} collective-permute-done((bf16[320,256]{1,0:T(8,128)(2,1)S(1)}, bf16[320,256]{1,0:T(8,128)(2,1)S(1)}, u32[]{:S(2)}, u32[]{:S(2)}) %collective-permute-start.1) | collective-permute-done | bytes 163872 | tf_op jit(solution)/shard_map/ppermute | solution.py:864
  16.7 0.7 column_strips.1
  17.4 1.7 %collective-permute-start.2 = (bf16[256,256]{1,0:T(8,128)(2,1)}, bf16[256,256]{1,0:T(8,128)(2,1)S(1)}, u32[]{:S(2)}, u32[]{:S(2)}) collective-permute-start(bf16[256,256]{1,0:T(8,128)(2,1)} %get-tuple-element.44), channel_id=1, source_target_pairs={{0,1},{1,2},{2,3},{3,4},{4,5},{5,6},{6,7},{7,8},{8,9},{9,10},{10,1... | collective-permute-start | bytes 393224 | tf_op jit(solution)/shard_map/ppermute | solution.py:863
  19.1 0.0 collective-permute-start.3
  19.1 0.0 copy-done
  19.1 0.7 convolution_convert_fusion.grads
  19.8 0.1 pad_add_fusion.place
  19.9 1.5 %collective-permute-done.2.left = bf16[256,256]{1,0:T(8,128)(2,1)S(1)} collective-permute-done((bf16[256,256]{1,0:T(8,128)(2,1)}, bf16[256,256]{1,0:T(8,128)(2,1)S(1)}, u32[]{:S(2)}, u32[]{:S(2)}) %collective-permute-start.2) | collective-permute-done | bytes 131104 | tf_op jit(solution)/shard_map/ppermute | solution.py:863
  21.4 2.6 %collective-permute-done.3.right = bf16[256,256]{1,0:T(8,128)(2,1)S(1)} collective-permute-done((bf16[256,256]{1,0:T(8,128)(2,1)}, bf16[256,256]{1,0:T(8,128)(2,1)S(1)}, u32[]{:S(2)}, u32[]{:S(2)}) %collective-permute-start.3) | collective-permute-done | bytes 131104 | tf_op jit(solution)/shard_map/ppermute | solution.py:864
  24.0 0.0 copy-done.1
  24.0 0.0 copy-done.4
  24.0 9.0 %near_kernel.1 = bf16[8,8,48,256]{3,2,1,0:T(8,128)(2,1)} custom-call(s32[3]{0:T(128)S(1)} %pad_add_fusion.place, bf16[384,256]{1,0:T(8,128)(2,1)S(1)} %bitcast.19, bf16[320,256]{1,0:T(8,128)(2,1)S(1)} %collective-permute-done.above, bf16[320,256]{1,0:T(8,128)(2,1)S(1)} %collective-permute-done.1.below, bf16[256,256]{1,0:T(8,128)(2,1)S(1)} %collective-permute-done.2.left, ...), custom_call_target="tpu_custom_call" | custom-call | flops 3000000000 | bytes 20000000 | tf_op jit(solution)/shard_map/near_kernel/pallas_call | solution.py:246
  33.0 0.0 copy-start.6
  33.1 0.6 copy-done.6
  33.7 8.9 %all-to-all-start = ((bf16[128,24,256]{2,1,0:T(8,128)(2,1)}), bf16[128,24,256]{2,1,0:T(8,128)(2,1)}, u32[]{:S(2)}, u32[]{:S(2)}) async-start(bf16[128,24,256]{2,1,0:T(8,128)(2,1)} %bitcast.29), calls=%async_computation | async-start | bytes 3145728 | tf_op jit(solution)/shard_map/all_to_all | solution.py:1043
  42.6 0.1 grad_strips.1
  42.7 1.7 %collective-permute-start.4 = (bf16[128,256]{1,0:T(8,128)(2,1)S(1)}, bf16[128,256]{1,0:T(8,128)(2,1)S(1)}, u32[]{:S(2)}, u32[]{:S(2)}) collective-permute-start(bf16[128,256]{1,0:T(8,128)(2,1)S(1)} %get-tuple-element.52), channel_id=1, source_target_pairs={{0,1},{1,2},{2,3},{3,4},{4,5},{5,6},{6,7},{7,8},{8,9},{9,10},{10,1... | collective-permute-start | bytes 196616 | tf_op jit(solution)/shard_map/ppermute | solution.py:863
  44.4 0.0 collective-permute-start.5
  44.4 0.9 copy-done.7
  45.3 9.8 %wide_kernel.1 = (bf16[3968,256]{1,0:T(8,128)(2,1)}, f32[8,512]{1,0:T(8,128)}, bf16[48,1024]{1,0:T(8,128)(2,1)}) custom-call(s32[3]{0:T(128)S(1)} %pad_add_fusion.place, bf16[384,256]{1,0:T(8,128)(2,1)S(1)} %bitcast.20, bf16[320,256]{1,0:T(8,128)(2,1)S(1)} %collective-permute-done.above, bf16[320,256]{1,0:T(8,128)(2,1)S(1)} %collective-permute-done.1.below, ...), custom_call_target="tpu_custom_call" | custom-call | flops 3000000000 | bytes 10000000 | tf_op jit(solution)/shard_map/wide_kernel/pallas_call | solution.py:383
  55.1 0.0 copy-start.5
  55.1 0.0 collective-permute-done.4.grads_left
  55.1 0.6 copy-done.9
  55.7 3.6 %collective-permute-done.5.grads_right = bf16[128,256]{1,0:T(8,128)(2,1)S(1)} collective-permute-done((bf16[128,256]{1,0:T(8,128)(2,1)S(1)}, bf16[128,256]{1,0:T(8,128)(2,1)S(1)}, u32[]{:S(2)}, u32[]{:S(2)}) %collective-permute-start.5) | collective-permute-done | bytes 65568 | tf_op jit(solution)/shard_map/ppermute | solution.py:864
  59.3 0.6 copy-done.11
  59.9 7.0 %all-to-all-done = bf16[128,24,256]{2,1,0:T(8,128)(2,1)} async-done(((bf16[128,24,256]{2,1,0:T(8,128)(2,1)}), bf16[128,24,256]{2,1,0:T(8,128)(2,1)}, u32[]{:S(2)}, u32[]{:S(2)}) %all-to-all-start) | async-done | bytes 1572896 | tf_op jit(solution)/shard_map/all_to_all | solution.py:1043
  67.0 4.3 %coarse_forward.1.stats = f32[8,8,128]{2,1,0:T(8,128)} custom-call(s32[3]{0:T(128)S(1)} %pad_add_fusion.place, bf16[3072,256]{1,0:T(8,128)(2,1)} %bitcast.11.every), custom_call_target="tpu_custom_call" | custom-call | flops 1000000000 | bytes 2000000 | tf_op jit(solution)/shard_map/coarse_forward/pallas_call | solution.py:473
  71.3 3.5 %all-to-all-start.1 = ((f32[8,8,128]{2,1,0:T(8,128)}), f32[8,8,128]{2,1,0:T(8,128)S(1)}, u32[]{:S(2)}, u32[]{:S(2)}) async-start(f32[8,8,128]{2,1,0:T(8,128)} %coarse_forward.1.stats), calls=%async_computation.1 | async-start | bytes 65536 | tf_op jit(solution)/shard_map/all_to_all | solution.py:1059
  74.8 4.5 %coarse_own.1 = (bf16[576,256]{1,0:T(8,128)(2,1)}, bf16[384,128]{1,0:T(8,128)(2,1)}) custom-call(s32[3]{0:T(128)S(1)} %pad_add_fusion.place, bf16[3072,256]{1,0:T(8,128)(2,1)} %bitcast.11.every, f32[8,8,128]{2,1,0:T(8,128)} %coarse_forward.1.stats, bf16[2,96,384]{2,1,0:T(8,128)(2,1)S(1)} %copy-done.5), custom_call_target="tpu_custom_call" | custom-call | flops 1000000000 | bytes 2000000 | tf_op jit(solution)/shard_map/coarse_own/pallas_call | solution.py:530
  79.3 1.8 %all-to-all-done.1.stats = f32[8,8,128]{2,1,0:T(8,128)S(1)} async-done(((f32[8,8,128]{2,1,0:T(8,128)}), f32[8,8,128]{2,1,0:T(8,128)S(1)}, u32[]{:S(2)}, u32[]{:S(2)}) %all-to-all-start.1) | async-done | bytes 32800 | tf_op jit(solution)/shard_map/all_to_all | solution.py:1059
  81.1 9.3 %coarse_backward.1 = (bf16[768,256]{1,0:T(8,128)(2,1)}, bf16[1024,3072]{1,0:T(8,128)(2,1)S(1)}, bf16[3968,256]{1,0:T(8,128)(2,1)S(1)}, bf16[4096,1024]{1,0:T(8,128)(2,1)S(1)}, bf16[1024,1024]{1,0:T(8,128)(2,1)S(1)}) custom-call(s32[3]{0:T(128)S(1)} %pad_add_fusion.place, bf16[3072,256]{1,0:T(8,128)(2,1)} %bitcast.11.every, ...), custom_call_target="tpu_custom_call" | custom-call | flops 3000000000 | bytes 2000000 | tf_op jit(solution)/shard_map/coarse_backward/pallas_call | solution.py:632
  90.4 15.3 %all_to_all.20.terms_coarse = bf16[16,48,256]{2,1,0:T(8,128)(2,1)S(1)} all-to-all(bf16[16,48,256]{2,1,0:T(8,128)(2,1)} %bitcast.30), channel_id=1, replica_groups=mesh['row'=8,'col'=16] {'col'}, dimensions={0} | all-to-all | bytes 786432 | tf_op jit(solution)/shard_map/all_to_all | solution.py:1066
  105.8 0.0 copy-done.12
  105.8 0.0 copy-done.13
  105.8 11.3 %backward_kernel.1 = (bf16[384,256]{1,0:T(8,128)(2,1)}, bf16[128,16,128]{2,1,0:T(8,128)(2,1)S(1)}) custom-call(s32[3]{0:T(128)S(1)} %pad_add_fusion.place, bf16[16,48,256]{2,1,0:T(8,128)(2,1)S(1)} %all_to_all.20.terms_coarse, bf16[384,256]{1,0:T(8,128)(2,1)S(1)} %bitcast.23, bf16[24,1024]{1,0:T(8,128)(2,1)S(1)} %get-tuple-element.49.own_coarse, ...), custom_call_target="tpu_custom_call" | custom-call | flops 5000000000 | bytes 20000000 | tf_op jit(solution)/shard_map/backward_kernel/pallas_call | solution.py:816
  117.1 18.2 %all_to_all.21.terms = bf16[128,16,128]{2,1,0:T(8,128)(2,1)S(1)} all-to-all(bf16[128,16,128]{2,1,0:T(8,128)(2,1)S(1)} %get-tuple-element.74), channel_id=1, replica_groups=mesh['row'=8,'col'=16] {'row','col'}, dimensions={0} | all-to-all | bytes 1048576 | tf_op jit(solution)/shard_map/all_to_all | solution.py:1084
  135.3 1.0 sum_terms.1
  (15 shorter events, 0.0 us)
Async XLA Ops:
  0.6 18.5 %copy-start = (bf16[1024,1024]{1,0:T(8,128)(2,1)S(1)}, bf16[1024,1024]{1,0:T(8,128)(2,1)}, u32[]{:S(2)}) copy-start(bf16[1024,1024]{1,0:T(8,128)(2,1)} %param.22) | copy-start | bytes 6291460
  0.6 23.4 %copy-start.1 = (bf16[16,24,256]{2,1,0:T(8,128)(2,1)S(1)}, bf16[16,24,256]{2,1,0:T(8,128)(2,1)}, u32[]{:S(2)}) copy-start(bf16[16,24,256]{2,1,0:T(8,128)(2,1)} %param.13) | copy-start | bytes 589828
  0.7 23.4 %copy-start.4 = (bf16[256,256]{1,0:T(8,128)(2,1)S(1)}, bf16[256,256]{1,0:T(8,128)(2,1)}, u32[]{:S(2)}) copy-start(bf16[256,256]{1,0:T(8,128)(2,1)} %w_out.5) | copy-start | bytes 393220
  0.7 23.4 %copy-start.3 = (bf16[256,768]{1,0:T(8,128)(2,1)S(1)}, bf16[256,768]{1,0:T(8,128)(2,1)}, u32[]{:S(2)}) copy-start(bf16[256,768]{1,0:T(8,128)(2,1)} %w_qkv.5) | copy-start | bytes 1179652
  0.7 23.3 %copy-start.14 = (f32[1024]{0:T(1024)S(1)}, f32[1024]{0:T(1024)}, u32[]{:S(2)}) copy-start(f32[1024]{0:T(1024)} %param.20) | copy-start | bytes 12292
  0.7 23.3 %copy-start.15 = (f32[256]{0:T(256)S(1)}, f32[256]{0:T(256)}, u32[]{:S(2)}) copy-start(f32[256]{0:T(256)} %param.16) | copy-start | bytes 3076
  1.9 10.9 %collective-permute-start = (bf16[320,256]{1,0:T(8,128)(2,1)S(1)}, bf16[320,256]{1,0:T(8,128)(2,1)S(1)}, u32[]{:S(2)}, u32[]{:S(2)}) collective-permute-start(bf16[320,256]{1,0:T(8,128)(2,1)S(1)} %get-tuple-element.40), channel_id=1, source_target_pairs={{0,16},{16,32},{32,48},{48,64},{64,80},{80,96},{96,112},{112,0},{1... | collective-permute-start | bytes 491528 | tf_op jit(solution)/shard_map/ppermute | solution.py:863
  6.4 10.4 %collective-permute-start.1 = (bf16[320,256]{1,0:T(8,128)(2,1)S(1)}, bf16[320,256]{1,0:T(8,128)(2,1)S(1)}, u32[]{:S(2)}, u32[]{:S(2)}) collective-permute-start(bf16[320,256]{1,0:T(8,128)(2,1)S(1)} %get-tuple-element.41), channel_id=1, source_target_pairs={{0,112},{16,0},{32,16},{48,32},{64,48},{80,64},{96,80},{112,96},{1... | collective-permute-start | bytes 491528 | tf_op jit(solution)/shard_map/ppermute | solution.py:864
  17.4 3.9 %collective-permute-start.2 = (bf16[256,256]{1,0:T(8,128)(2,1)}, bf16[256,256]{1,0:T(8,128)(2,1)S(1)}, u32[]{:S(2)}, u32[]{:S(2)}) collective-permute-start(bf16[256,256]{1,0:T(8,128)(2,1)} %get-tuple-element.44), channel_id=1, source_target_pairs={{0,1},{1,2},{2,3},{3,4},{4,5},{5,6},{6,7},{7,8},{8,9},{9,10},{10,1... | collective-permute-start | bytes 393224 | tf_op jit(solution)/shard_map/ppermute | solution.py:863
  19.1 4.9 %collective-permute-start.3 = (bf16[256,256]{1,0:T(8,128)(2,1)}, bf16[256,256]{1,0:T(8,128)(2,1)S(1)}, u32[]{:S(2)}, u32[]{:S(2)}) collective-permute-start(bf16[256,256]{1,0:T(8,128)(2,1)} %get-tuple-element.45), channel_id=1, source_target_pairs={{0,15},{1,0},{2,1},{3,2},{4,3},{5,4},{6,5},{7,6},{8,7},{9,8},{10,9... | collective-permute-start | bytes 393224 | tf_op jit(solution)/shard_map/ppermute | solution.py:864
  33.0 0.7 copy-start.6
  33.7 8.9 %copy-start.2 = (bf16[16,24,256]{2,1,0:T(8,128)(2,1)S(1)}, bf16[16,24,256]{2,1,0:T(8,128)(2,1)}, u32[]{:S(2)}) copy-start(bf16[16,24,256]{2,1,0:T(8,128)(2,1)} %param.14) | copy-start | bytes 589828
  33.7 33.3 %all-to-all-start = ((bf16[128,24,256]{2,1,0:T(8,128)(2,1)}), bf16[128,24,256]{2,1,0:T(8,128)(2,1)}, u32[]{:S(2)}, u32[]{:S(2)}) async-start(bf16[128,24,256]{2,1,0:T(8,128)(2,1)} %bitcast.29), calls=%async_computation | async-start | bytes 3145728 | tf_op jit(solution)/shard_map/all_to_all | solution.py:1043
  42.7 12.4 %collective-permute-start.4 = (bf16[128,256]{1,0:T(8,128)(2,1)S(1)}, bf16[128,256]{1,0:T(8,128)(2,1)S(1)}, u32[]{:S(2)}, u32[]{:S(2)}) collective-permute-start(bf16[128,256]{1,0:T(8,128)(2,1)S(1)} %get-tuple-element.52), channel_id=1, source_target_pairs={{0,1},{1,2},{2,3},{3,4},{4,5},{5,6},{6,7},{7,8},{8,9},{9,10},{10,1... | collective-permute-start | bytes 196616 | tf_op jit(solution)/shard_map/ppermute | solution.py:863
  44.4 14.9 %collective-permute-start.5 = (bf16[128,256]{1,0:T(8,128)(2,1)S(1)}, bf16[128,256]{1,0:T(8,128)(2,1)S(1)}, u32[]{:S(2)}, u32[]{:S(2)}) collective-permute-start(bf16[128,256]{1,0:T(8,128)(2,1)S(1)} %get-tuple-element.53), channel_id=1, source_target_pairs={{0,15},{1,0},{2,1},{3,2},{4,3},{5,4},{6,5},{7,6},{8,7},{9,8},{10,9... | collective-permute-start | bytes 196616 | tf_op jit(solution)/shard_map/ppermute | solution.py:864
  44.4 0.9 copy-start.7
  55.1 19.8 %copy-start.5 = (bf16[2,96,384]{2,1,0:T(8,128)(2,1)S(1)}, bf16[2,96,384]{2,1,0:T(8,128)(2,1)}, u32[]{:S(2)}) copy-start(bf16[2,96,384]{2,1,0:T(8,128)(2,1)} %constant.19.clone.strips) | copy-start | bytes 442372
  55.1 0.6 copy-start.9
  59.3 0.6 copy-start.11
  71.3 9.8 %all-to-all-start.1 = ((f32[8,8,128]{2,1,0:T(8,128)}), f32[8,8,128]{2,1,0:T(8,128)S(1)}, u32[]{:S(2)}, u32[]{:S(2)}) async-start(f32[8,8,128]{2,1,0:T(8,128)} %coarse_forward.1.stats), calls=%async_computation.1 | async-start | bytes 65536 | tf_op jit(solution)/shard_map/all_to_all | solution.py:1059
  81.1 24.7 %copy-start.8 = (bf16[48,1024]{1,0:T(8,128)(2,1)S(1)}, bf16[48,1024]{1,0:T(8,128)(2,1)}, u32[]{:S(2)}) copy-start(bf16[48,1024]{1,0:T(8,128)(2,1)} %get-tuple-element.67.coarse) | copy-start | bytes 294916
  81.1 24.7 %copy-start.10 = (bf16[128,256]{1,0:T(8,128)(2,1)S(1)}, bf16[128,256]{1,0:T(8,128)(2,1)}, u32[]{:S(2)}) copy-start(bf16[128,256]{1,0:T(8,128)(2,1)} %copy-done.9) | copy-start | bytes 196612
  81.1 24.7 %copy-start.12 = (bf16[128,256]{1,0:T(8,128)(2,1)S(1)}, bf16[128,256]{1,0:T(8,128)(2,1)}, u32[]{:S(2)}) copy-start(bf16[128,256]{1,0:T(8,128)(2,1)} %copy-done.11) | copy-start | bytes 196612
  81.1 24.7 %copy-start.13 = (f32[8,512]{1,0:T(8,128)S(1)}, f32[8,512]{1,0:T(8,128)}, u32[]{:S(2)}) copy-start(f32[8,512]{1,0:T(8,128)} %get-tuple-element.68.lse) | copy-start | bytes 49156
